TPU v7x, 128 devices: a whole 4x4x4 slice. The times are simulated.
128 devices in a mesh: elem: 32 (over x, y_hi, z), face: 4 (over y_lo, core).
Axes of the slice: x: 4, y: 4 (y_hi: 2, y_lo: 2; y = y_hi * 2 + y_lo), z: 4, core: 2. Of those that a mesh axis runs over, the one named last changes fastest.
Arguments:
- state: bfloat16 [512, 512, 768], P('elem', 'face'), may hold values from -6 to 6
- perturbation: bfloat16 [512, 512, 768], P('elem', 'face'), may hold values from -6 to 6
- adjoint_end: bfloat16 [512, 512, 768], P('elem', 'face'), may hold values from -6 to 6
- kappa: float32 [512, 512], P('elem', 'face'), may hold values from 0.1 to 0.24
- act_list: int32 [32, 4096], P('elem', 'face'), may hold values from 0 to 2047, as said below
- counts: int32 [32, 4], P('elem', 'face'), may hold values from 128 to 1024
- w_in: bfloat16 [768, 512], replicated, may hold values from -0.21875 to 0.21875
- w_mid: bfloat16 [3, 512, 512], replicated, may hold values from -0.25 to 0.25
- w_out: bfloat16 [512, 128], replicated, may hold values from -0.25 to 0.25
- biases: float32 [4, 512], replicated, may hold values from -3 to 3
Outputs:
- tl_out: float32 [512, 512, 768], P('elem', 'face')
- ad_out: float32 [512, 512, 768], P('elem', 'face')
Inputs may be any that keep to these rules, and one draw needn't show every extreme that they name: `act_list`: within each tile's 1024 entries the numbers are distinct columns of that tile, numbered row by row over its 16 x 128 columns.
All inputs are finite; a program needn't handle non-finite values.
Results may differ from a plain program's by a relative error of at most 0.0029.
Values may be sent and summed in bfloat16 or wider, within the bound.
No kernel may reach another device: no remote copies, remote signals or barrier semaphores. Data moves between devices by JAX's collectives and lax.ppermute only.
A program may use at most 192 MiB of HBM per device.

v0:
```python
import jax
import jax.numpy as jnp
from jax import lax
from jax.sharding import PartitionSpec as P

SUBSTEPS = 3
BLK = 128


PHYS_STEP = 4.0


def padded(cells, sides, width):
    for axis, dim in sides:
        count = lax.axis_size(axis)
        ends = count - 1
        head = lax.slice_in_dim(cells, 0, width, axis=dim)
        tail = lax.slice_in_dim(cells, cells.shape[dim] - width, cells.shape[dim], axis=dim)
        cells = jnp.concatenate(
            [
                lax.ppermute(tail, axis, [(i, (i + 1) % count) for i in range(ends)]),
                cells,
                lax.ppermute(head, axis, [((i + 1) % count, i) for i in range(ends)]),
            ],
            axis=dim,
        )
    return cells


def five_point(extended):
    return (
        extended[2:, 1:-1]
        + extended[:-2, 1:-1]
        + extended[1:-1, 2:]
        + extended[1:-1, :-2]
        - 4.0 * extended[1:-1, 1:-1]
    )


def contract_back(left, right):
    return lax.dot_general(
        left, right, (((1,), (1,)), ((), ())), preferred_element_type=jnp.float32
    )


def forward_block(x_rows, d_rows, layer_weights, biases, w_out):
    hidden = x_rows
    tangent = d_rows
    slopes = []
    for layer in range(len(layer_weights)):
        preact = (
            jnp.dot(hidden, layer_weights[layer], preferred_element_type=jnp.float32)
            + biases[layer]
        )
        value = jnp.tanh(preact)
        slope = 1.0 - value * value
        hidden = value.astype(jnp.bfloat16)
        tangent = (
            slope * jnp.dot(tangent, layer_weights[layer], preferred_element_type=jnp.float32)
        ).astype(jnp.bfloat16)
        slopes.append(slope)
    return (jnp.dot(tangent, w_out, preferred_element_type=jnp.float32), jnp.stack(slopes))


def backward_block(upstream_rows, slopes, layer_weights, w_out):
    pulled = contract_back(upstream_rows, w_out)
    for layer in reversed(range(len(layer_weights))):
        scaled = (pulled * slopes[layer]).astype(jnp.bfloat16)
        pulled = contract_back(scaled, layer_weights[layer])
    return pulled


def forward_blocks(flags, x_blocks, d_blocks, layer_weights, biases, w_out):
    rows = x_blocks.shape[1]
    levels = w_out.shape[1]
    units = biases.shape[1]

    def forward_skipped(inputs):
        return (
            jnp.zeros((rows, levels), jnp.float32),
            jnp.zeros((len(layer_weights), rows, units), jnp.float32),
        )

    def forward_evaluate(inputs):
        return forward_block(inputs[0], inputs[1], layer_weights, biases, w_out)

    def forward_run_block(inputs):
        return lax.cond(inputs[0], forward_evaluate, forward_skipped, (inputs[1], inputs[2]))

    return lax.map(forward_run_block, (flags, x_blocks, d_blocks))


def backward_blocks(flags, upstream_blocks, slope_blocks, layer_weights, w_out):
    rows = upstream_blocks.shape[1]
    channels = layer_weights[0].shape[0]

    def backward_skipped(inputs):
        return jnp.zeros((rows, channels), jnp.float32)

    def backward_evaluate(inputs):
        return backward_block(inputs[0], inputs[1], layer_weights, w_out)

    def backward_run_block(inputs):
        return lax.cond(inputs[0], backward_evaluate, backward_skipped, (inputs[1], inputs[2]))

    return lax.map(backward_run_block, (flags, upstream_blocks, slope_blocks))


def per_device(
    state, perturbation, adjoint_end, kappa, act_list, counts, w_in, w_mid, w_out, biases
):
    size_x, size_y, channels = state.shape
    levels = w_out.shape[1]
    columns = size_x * size_y
    capacity = act_list.shape[1]
    blocks = capacity // BLK
    layer_weights = [w_in] + [w_mid[index] for index in range(w_mid.shape[0])]
    count = counts[0, 0]
    kappa_cells = kappa[:, :, None]
    adjoint = adjoint_end.astype(jnp.float32)
    for substep in range(SUBSTEPS):
        extended = padded(kappa_cells * adjoint, (("elem", 0), ("face", 1)), 1)
        adjoint = adjoint + five_point(extended)
    state_flat = state.reshape(columns, channels)
    pert_flat = perturbation.reshape(columns, channels)
    positions = jnp.arange(capacity, dtype=jnp.int32)
    block_ids = jnp.arange(blocks, dtype=jnp.int32)
    index = act_list[0]
    live = (positions < count).astype(jnp.float32)[:, None]
    flags = block_ids * BLK < count
    x_rows = jnp.take(state_flat, index, axis=0).reshape(blocks, BLK, channels)
    d_rows = jnp.take(pert_flat, index, axis=0).reshape(blocks, BLK, channels)
    jac_blocks, slope_blocks = forward_blocks(flags, x_rows, d_rows, layer_weights, biases, w_out)
    jac_rows = jac_blocks.reshape(capacity, levels)
    tendency = jnp.zeros((columns, levels), jnp.float32).at[index].add(PHYS_STEP * live * jac_rows)
    adjoint_levels = adjoint[:, :, :levels].reshape(columns, levels)
    upstream_rows = (PHYS_STEP * live * jnp.take(adjoint_levels, index, axis=0)).astype(
        jnp.bfloat16
    )
    pulled_blocks = backward_blocks(
        flags, upstream_rows.reshape(blocks, BLK, levels), slope_blocks, layer_weights, w_out
    )
    pulled_rows = pulled_blocks.reshape(capacity, channels)
    moved = perturbation.astype(jnp.float32)
    moved = jnp.concatenate(
        [moved[:, :, :levels] + tendency.reshape(size_x, size_y, levels), moved[:, :, levels:]],
        axis=2,
    )
    for substep in range(SUBSTEPS):
        extended = padded(moved, (("elem", 0), ("face", 1)), 1)
        moved = moved + kappa_cells * five_point(extended)
    sensitivity = jnp.zeros((columns, channels), jnp.float32).at[index].add(pulled_rows)
    ad_out = adjoint + sensitivity.reshape(size_x, size_y, channels)
    return (moved, ad_out)


def solution(mesh):
    return jax.shard_map(
        per_device,
        mesh=mesh,
        in_specs=(
            P("elem", "face", None),
            P("elem", "face", None),
            P("elem", "face", None),
            P("elem", "face"),
            P("elem", "face"),
            P("elem", "face"),
            P(),
            P(),
            P(),
            P(),
        ),
        out_specs=(P("elem", "face", None), P("elem", "face", None)),
        check_vma=False,
    )
```

profile of v0, /device:TPU:20, one launch (start us, length us, event | category | flops | bytes accessed | tf_op | source)
XLA Modules:
  0.0 421.7 jit_solution(4685666379210498953)
XLA Ops:
  3.3 4.6 %slice.295 = f32[16,128,640]{2,1,0:T(8,128)} slice(bf16[16,128,768]{2,1,0:T(8,128)(2,1)} %param.21), slice={[0:16], [0:128], [128:768]} | slice | bytes 10485760 | tf_op jit(solution)/shard_map/slice | solution.py:146
  12.0 7.9 %gather_fusion.2 = bf16[1024,768]{1,0:T(8,128)(2,1)} fusion(bf16[2048,768]{1,0:T(8,128)(2,1)} %bitcast.97, s32[1024]{0:T(1024)S(1)} %fusion.80), kind=kCustom, calls=%fused_computation.1.clone | custom fusion | bytes 3149824 | tf_op jit(solution)/shard_map/jit(_take)/gather | solution.py:132
  19.8 5.2 %gather_fusion.1 = bf16[1024,768]{1,0:T(8,128)(2,1)} fusion(bf16[2048,768]{1,0:T(8,128)(2,1)S(1)} %bitcast.96, s32[1024]{0:T(1024)S(1)} %fusion.80), kind=kCustom, calls=%fused_computation.clone | custom fusion | bytes 3149824 | tf_op jit(solution)/shard_map/jit(_take)/gather | solution.py:131
  26.6 3.9 broadcast_select_fusion
  30.5 110.2 %while.22 = (s32[]{:T(128)}, f32[8,128,128]{2,1,0:T(8,128)}, f32[8,4,128,512]{3,2,1,0:T(8,128)}, pred[8]{0:T(512)(128)(4,1)S(1)}, bf16[8,128,768]{2,1,0:T(8,128)...) while((s32[]{:T(128)}, f32[8,128,128]{2,1,0:T(8,128)}, ...), condition=%wide.region_3.5_spmd, body=%wide.region_0.4_spmd.sunk | while | flops 623443968 | bytes 14641384 | solution.py:90
  31.6 8.9 %conditional.4 = (f32[1,128,128]{2,1,0:T(8,128)}, f32[1,4,128,512]{3,2,1,0:T(8,128)}) conditional(s32[]{:T(128)} %bitcast.91, () %tuple.88, (bf16[8,128,768]{2,1,0:T(8,128)(2,1)}, s32[]{:T(128)}, bf16[768,512]{1,0:T(8,128)(2,1)S(1)}, f32[4,512]{1,0:T(4,128)S(1)}, bf16[512,512]{1,0:T(8,128)(2,1)S(1)}, /*index=5*/bf16[512,512]{1,0:T(8,128)(2,1)S(1)}, ...), branch_computations={%region_1.2_spmd, %region_2.3_spmd} | conditional | flops 623443968 | bytes 12411920 | solution.py:88
  45.4 8.9 %conditional.4 = (f32[1,128,128]{2,1,0:T(8,128)}, f32[1,4,128,512]{3,2,1,0:T(8,128)}) conditional(s32[]{:T(128)} %bitcast.91, () %tuple.88, (bf16[8,128,768]{2,1,0:T(8,128)(2,1)}, s32[]{:T(128)}, bf16[768,512]{1,0:T(8,128)(2,1)S(1)}, f32[4,512]{1,0:T(4,128)S(1)}, bf16[512,512]{1,0:T(8,128)(2,1)S(1)}, /*index=5*/bf16[512,512]{1,0:T(8,128)(2,1)S(1)}, ...), branch_computations={%region_1.2_spmd, %region_2.3_spmd} | conditional | flops 623443968 | bytes 12411920 | solution.py:88
  59.2 8.9 %conditional.4 = (f32[1,128,128]{2,1,0:T(8,128)}, f32[1,4,128,512]{3,2,1,0:T(8,128)}) conditional(s32[]{:T(128)} %bitcast.91, () %tuple.88, (bf16[8,128,768]{2,1,0:T(8,128)(2,1)}, s32[]{:T(128)}, bf16[768,512]{1,0:T(8,128)(2,1)S(1)}, f32[4,512]{1,0:T(4,128)S(1)}, bf16[512,512]{1,0:T(8,128)(2,1)S(1)}, /*index=5*/bf16[512,512]{1,0:T(8,128)(2,1)S(1)}, ...), branch_computations={%region_1.2_spmd, %region_2.3_spmd} | conditional | flops 623443968 | bytes 12411920 | solution.py:88
  73.0 8.9 %conditional.4 = (f32[1,128,128]{2,1,0:T(8,128)}, f32[1,4,128,512]{3,2,1,0:T(8,128)}) conditional(s32[]{:T(128)} %bitcast.91, () %tuple.88, (bf16[8,128,768]{2,1,0:T(8,128)(2,1)}, s32[]{:T(128)}, bf16[768,512]{1,0:T(8,128)(2,1)S(1)}, f32[4,512]{1,0:T(4,128)S(1)}, bf16[512,512]{1,0:T(8,128)(2,1)S(1)}, /*index=5*/bf16[512,512]{1,0:T(8,128)(2,1)S(1)}, ...), branch_computations={%region_1.2_spmd, %region_2.3_spmd} | conditional | flops 623443968 | bytes 12411920 | solution.py:88
  86.7 8.9 %conditional.4 = (f32[1,128,128]{2,1,0:T(8,128)}, f32[1,4,128,512]{3,2,1,0:T(8,128)}) conditional(s32[]{:T(128)} %bitcast.91, () %tuple.88, (bf16[8,128,768]{2,1,0:T(8,128)(2,1)}, s32[]{:T(128)}, bf16[768,512]{1,0:T(8,128)(2,1)S(1)}, f32[4,512]{1,0:T(4,128)S(1)}, bf16[512,512]{1,0:T(8,128)(2,1)S(1)}, /*index=5*/bf16[512,512]{1,0:T(8,128)(2,1)S(1)}, ...), branch_computations={%region_1.2_spmd, %region_2.3_spmd} | conditional | flops 623443968 | bytes 12411920 | solution.py:88
  100.5 8.9 %conditional.4 = (f32[1,128,128]{2,1,0:T(8,128)}, f32[1,4,128,512]{3,2,1,0:T(8,128)}) conditional(s32[]{:T(128)} %bitcast.91, () %tuple.88, (bf16[8,128,768]{2,1,0:T(8,128)(2,1)}, s32[]{:T(128)}, bf16[768,512]{1,0:T(8,128)(2,1)S(1)}, f32[4,512]{1,0:T(4,128)S(1)}, bf16[512,512]{1,0:T(8,128)(2,1)S(1)}, /*index=5*/bf16[512,512]{1,0:T(8,128)(2,1)S(1)}, ...), branch_computations={%region_1.2_spmd, %region_2.3_spmd} | conditional | flops 623443968 | bytes 12411920 | solution.py:88
  114.2 8.9 %conditional.4 = (f32[1,128,128]{2,1,0:T(8,128)}, f32[1,4,128,512]{3,2,1,0:T(8,128)}) conditional(s32[]{:T(128)} %bitcast.91, () %tuple.88, (bf16[8,128,768]{2,1,0:T(8,128)(2,1)}, s32[]{:T(128)}, bf16[768,512]{1,0:T(8,128)(2,1)S(1)}, f32[4,512]{1,0:T(4,128)S(1)}, bf16[512,512]{1,0:T(8,128)(2,1)S(1)}, /*index=5*/bf16[512,512]{1,0:T(8,128)(2,1)S(1)}, ...), branch_computations={%region_1.2_spmd, %region_2.3_spmd} | conditional | flops 623443968 | bytes 12411920 | solution.py:88
  128.0 8.9 %conditional.4 = (f32[1,128,128]{2,1,0:T(8,128)}, f32[1,4,128,512]{3,2,1,0:T(8,128)}) conditional(s32[]{:T(128)} %bitcast.91, () %tuple.88, (bf16[8,128,768]{2,1,0:T(8,128)(2,1)}, s32[]{:T(128)}, bf16[768,512]{1,0:T(8,128)(2,1)S(1)}, f32[4,512]{1,0:T(4,128)S(1)}, bf16[512,512]{1,0:T(8,128)(2,1)S(1)}, /*index=5*/bf16[512,512]{1,0:T(8,128)(2,1)S(1)}, ...), branch_computations={%region_1.2_spmd, %region_2.3_spmd} | conditional | flops 623443968 | bytes 12411920 | solution.py:88
  142.0 7.0 %scatter_custom_fusion = f32[2048,128]{1,0:T(8,128)} fusion(s32[1024]{0:T(1024)S(1)} %bitcast.120, f32[1024,128]{1,0:T(8,128)S(1)} %bitcast_multiply_fusion, f32[]{:T(128)} %constant.81.clone.1), kind=kCustom, calls=%fused_computation.166 | custom fusion | flops 131072 | bytes 1048580 | tf_op jit(solution)/shard_map/scatter-add | solution.py:135
  154.0 3.9 collective-permute-start.1
  157.9 3.8 collective-permute-done
  161.7 5.5 %collective-permute-done.1 = f32[1,128,768]{2,1,0:T(8,128)S(1)} collective-permute-done((f32[1,128,768]{2,1,0:T(8,128)S(1)}, f32[1,128,768]{2,1,0:T(8,128)S(1)}, u32[]{:S(2)}, u32[]{:S(2)}) %collective-permute-start.1) | collective-permute-done | bytes 393248 | tf_op jit(solution)/shard_map/ppermute | solution.py:21
  173.1 11.2 %fusion.69 = f32[16,128,768]{2,1,0:T(8,128)S(1)} fusion(f32[18,1,768]{2,1,0:T(1,128)S(1)} %collective-permute-done.3, f32[1,128,768]{2,1,0:T(8,128)S(1)} %collective-permute-done, f32[1,128,768]{2,1,0:T(8,128)S(1)} %collective-permute-done.1, f32[16,128,640]{2,1,0:T(8,128)S(1)} %bitcast.99, f32[16,128,128]{2,1,0:T(8,128)S(1)} %slice_add_fusion, ...), kind=kLoop, calls=%fused_computation.140 | loop fusion | flops 31457280 | bytes 13488128 | tf_op jit(solution)/shard_map/add | solution.py:151
  186.7 4.7 %collective-permute-start.5 = (f32[1,128,768]{2,1,0:T(8,128)S(1)}, f32[1,128,768]{2,1,0:T(8,128)S(1)}, u32[]{:S(2)}, u32[]{:S(2)}) collective-permute-start(f32[1,128,768]{2,1,0:T(8,128)S(1)} %get-tuple-element.342), channel_id=1, source_target_pairs={{0,4},{4,8},{8,12},{12,16},{16,20},{20,24},{24,28},{28,32},{32,36}... | collective-permute-start | bytes 1179656 | tf_op jit(solution)/shard_map/ppermute | solution.py:21
  191.4 5.5 %collective-permute-done.4 = f32[1,128,768]{2,1,0:T(8,128)S(1)} collective-permute-done((f32[1,128,768]{2,1,0:T(8,128)S(1)}, f32[1,128,768]{2,1,0:T(8,128)S(1)}, u32[]{:S(2)}, u32[]{:S(2)}) %collective-permute-start.4) | collective-permute-done | bytes 393248 | tf_op jit(solution)/shard_map/ppermute | solution.py:23
  196.9 5.6 %collective-permute-done.5 = f32[1,128,768]{2,1,0:T(8,128)S(1)} collective-permute-done((f32[1,128,768]{2,1,0:T(8,128)S(1)}, f32[1,128,768]{2,1,0:T(8,128)S(1)}, u32[]{:S(2)}, u32[]{:S(2)}) %collective-permute-start.5) | collective-permute-done | bytes 393248 | tf_op jit(solution)/shard_map/ppermute | solution.py:21
  202.6 3.7 collective-permute-start.7
  209.4 14.7 %convert_multiply_fusion = (f32[16,128,768]{2,1,0:T(8,128)S(1)}, f32[16,128,768]{2,1,0:T(8,128)S(1)}) fusion(bf16[16,128,768]{2,1,0:T(8,128)(2,1)S(1)} %copy-done.7, f32[16,128]{1,0:T(8,128)S(1)} %copy-done.11, f32[16,128,768]{2,1,0:T(8,128)} %copy-done.5, f32[1,128,768]{2,1,0:T(8,128)S(1)} %collective-permute-done.4, ...), kind=kLoop, calls=%fused_computation.67 | loop fusion | flops 26738688 | bytes 22925312 | tf_op jit(solution)/shard_map/mul | solution.py:122
  226.1 3.9 collective-permute-start.13
  230.0 6.6 %collective-permute-done.12 = f32[1,128,768]{2,1,0:T(8,128)S(1)} collective-permute-done((f32[1,128,768]{2,1,0:T(8,128)S(1)}, f32[1,128,768]{2,1,0:T(8,128)S(1)}, u32[]{:S(2)}, u32[]{:S(2)}) %collective-permute-start.12) | collective-permute-done | bytes 393248 | tf_op jit(solution)/shard_map/ppermute | solution.py:23
  236.6 5.5 %collective-permute-done.13 = f32[1,128,768]{2,1,0:T(8,128)S(1)} collective-permute-done((f32[1,128,768]{2,1,0:T(8,128)S(1)}, f32[1,128,768]{2,1,0:T(8,128)S(1)}, u32[]{:S(2)}, u32[]{:S(2)}) %collective-permute-start.13) | collective-permute-done | bytes 393248 | tf_op jit(solution)/shard_map/ppermute | solution.py:21
  248.6 7.4 %broadcast_multiply_fusion.1 = f32[16,128,768]{2,1,0:T(8,128)} fusion(f32[16,128]{1,0:T(8,128)S(1)} %copy-done.11, f32[16,128,768]{2,1,0:T(8,128)S(1)} %get-tuple-element.349, f32[1,128,768]{2,1,0:T(8,128)S(1)} %collective-permute-done.12, f32[1,128,768]{2,1,0:T(8,128)S(1)} %collective-permute-done.13, f32[18,1,768]{2,1,0:T(1,128)S(1)} %collective-permute-done.15, ...), kind=kLoop, calls=%fused_computation.157 | loop fusion | flops 25165824 | bytes 16633856 | tf_op jit(solution)/shard_map/mul | solution.py:122
  259.1 3.9 collective-permute-start.17
  263.0 6.6 %collective-permute-done.16 = f32[1,128,768]{2,1,0:T(8,128)S(1)} collective-permute-done((f32[1,128,768]{2,1,0:T(8,128)S(1)}, f32[1,128,768]{2,1,0:T(8,128)S(1)}, u32[]{:S(2)}, u32[]{:S(2)}) %collective-permute-start.16) | collective-permute-done | bytes 393248 | tf_op jit(solution)/shard_map/ppermute | solution.py:23
  269.6 5.5 %collective-permute-done.17 = f32[1,128,768]{2,1,0:T(8,128)S(1)} collective-permute-done((f32[1,128,768]{2,1,0:T(8,128)S(1)}, f32[1,128,768]{2,1,0:T(8,128)S(1)}, u32[]{:S(2)}, u32[]{:S(2)}) %collective-permute-start.17) | collective-permute-done | bytes 393248 | tf_op jit(solution)/shard_map/ppermute | solution.py:21
  283.8 3.9 collective-permute-start.9
  287.8 19.4 %broadcast_multiply_fusion = (f32[16,128,768]{2,1,0:T(8,128)}, f32[16,128,768]{2,1,0:T(8,128)}) fusion(f32[16,128]{1,0:T(8,128)S(1)} %copy-done.11, f32[16,128,768]{2,1,0:T(8,128)} %broadcast_multiply_fusion.1, f32[1,128,768]{2,1,0:T(8,128)} %copy-done.9, f32[1,128,768]{2,1,0:T(8,128)} %copy-done.10, f32[18,1,768]{2,1,0:T(1,128)S(1)} %collective-permute-done.19, ...), kind=kLoop, calls=%fused_computation.156 | loop fusion | flops 47185920 | bytes 30113792 | tf_op jit(solution)/shard_map/mul | solution.py:122
  309.3 5.5 %collective-permute-start.20 = (f32[1,128,768]{2,1,0:T(8,128)}, f32[1,128,768]{2,1,0:T(8,128)S(1)}, u32[]{:S(2)}, u32[]{:S(2)}) collective-permute-start(f32[1,128,768]{2,1,0:T(8,128)} %get-tuple-element.335), channel_id=1, source_target_pairs={{4,0},{8,4},{12,8},{16,12},{20,16},{24,20},{28,24},{32,28},{36,32}... | collective-permute-start | bytes 1179656 | tf_op jit(solution)/shard_map/ppermute | solution.py:23
  324.6 7.8 %collective-permute-done.21 = f32[1,128,768]{2,1,0:T(8,128)S(1)} collective-permute-done((f32[1,128,768]{2,1,0:T(8,128)}, f32[1,128,768]{2,1,0:T(8,128)S(1)}, u32[]{:S(2)}, u32[]{:S(2)}) %collective-permute-start.21) | collective-permute-done | bytes 393248 | tf_op jit(solution)/shard_map/ppermute | solution.py:21
  336.6 8.6 %fusion.57 = f32[16,128,768]{2,1,0:T(8,128)} fusion(f32[16,128,768]{2,1,0:T(8,128)S(1)} %bitcast.101, f32[18,1,768]{2,1,0:T(1,128)S(1)} %collective-permute-done.11, f32[1,128,768]{2,1,0:T(8,128)} %collective-permute-done.8, f32[1,128,768]{2,1,0:T(8,128)} %collective-permute-done.9, f32[18,1,768]{2,1,0:T(1,128)S(1)} %collective-permute-done.10, ...), kind=kLoop, calls=%fused_computation.112 | loop fusion | flops 23592960 | bytes 13488128 | tf_op jit(solution)/shard_map/add | solution.py:151
  345.3 5.3 %fusion.42 = f32[16,128,768]{2,1,0:T(8,128)S(1)} fusion(f32[16,128,768]{2,1,0:T(8,128)S(1)} %bitcast.107, f32[18,1,768]{2,1,0:T(1,128)S(1)} %collective-permute-done.23, f32[1,128,768]{2,1,0:T(8,128)S(1)} %collective-permute-done.20, f32[16,128,768]{2,1,0:T(8,128)S(1)} %bitcast.103, f32[1,128,768]{2,1,0:T(8,128)S(1)} %collective-permute-done.21, ...), kind=kLoop, calls=%fused_computation.73 | loop fusion | flops 22020096 | bytes 19771392 | tf_op jit(solution)/shard_map/add | solution.py:123
  354.3 4.0 gather_fusion
  358.7 43.6 %while.23 = (s32[]{:T(128)}, f32[8,128,768]{2,1,0:T(8,128)}, pred[8]{0:T(512)(128)(4,1)S(1)}, bf16[8,128,128]{2,1,0:T(8,128)(2,1)S(1)}, bf16[512,128]{1,0:T(8,12...) while((s32[]{:T(128)}, f32[8,128,768]{2,1,0:T(8,128)}, ...), condition=%wide.region_8.10_spmd, body=%wide.region_5.9_spmd.sunk | while | flops 319291392 | bytes 5278968 | solution.py:106
  360.0 3.4 conditional.5
  365.5 3.4 conditional.5
  370.9 3.4 conditional.5
  376.4 3.4 conditional.5
  381.8 3.4 conditional.5
  387.3 3.4 conditional.5
  392.7 3.4 conditional.5
  398.1 3.4 conditional.5
  402.4 11.0 %scatter_custom_fusion.1 = f32[2048,768]{1,0:T(8,128)} fusion(s32[1024]{0:T(1024)S(1)} %bitcast.122, f32[1024,768]{1,0:T(8,128)} %bitcast.123, f32[]{:T(128)} %constant.81.clone.1), kind=kCustom, calls=%fused_computation.154 | custom fusion | flops 786432 | bytes 6291968 | tf_op jit(solution)/shard_map/scatter-add | solution.py:152
  413.3 8.4 %add.206 = f32[16,128,768]{2,1,0:T(8,128)} add(f32[16,128,768]{2,1,0:T(8,128)} %copy-done.6, f32[16,128,768]{2,1,0:T(8,128)} %bitcast.108) | non-fusion elementwise | flops 1572864 | bytes 18874368 | tf_op jit(solution)/shard_map/add | solution.py:153
  (261 shorter events, 208.7 us)
Async XLA Ops:
  0.6 19.2 %copy-start = (bf16[16,128,768]{2,1,0:T(8,128)(2,1)S(1)}, bf16[16,128,768]{2,1,0:T(8,128)(2,1)}, u32[]{:S(2)}) copy-start(bf16[16,128,768]{2,1,0:T(8,128)(2,1)} %param.20) | copy-start | bytes 9437188
  0.7 7.2 %copy-start.3 = (bf16[16,128,768]{2,1,0:T(8,128)(2,1)S(1)}, bf16[16,128,768]{2,1,0:T(8,128)(2,1)}, u32[]{:S(2)}) copy-start(bf16[16,128,768]{2,1,0:T(8,128)(2,1)} %param.21) | copy-start | bytes 9437188
  25.1 5.4 %copy-start.2 = (bf16[768,512]{1,0:T(8,128)(2,1)S(1)}, bf16[768,512]{1,0:T(8,128)(2,1)}, u32[]{:S(2)}) copy-start(bf16[768,512]{1,0:T(8,128)(2,1)} %param.26) | copy-start | bytes 2359300
  25.1 5.4 %copy-start.8 = (bf16[512,128]{1,0:T(8,128)(2,1)S(1)}, bf16[512,128]{1,0:T(8,128)(2,1)}, u32[]{:S(2)}) copy-start(bf16[512,128]{1,0:T(8,128)(2,1)} %param.28) | copy-start | bytes 393220
  25.1 5.4 %copy-start.12 = (f32[4,512]{1,0:T(4,128)S(1)}, f32[4,512]{1,0:T(4,128)}, u32[]{:S(2)}) copy-start(f32[4,512]{1,0:T(4,128)} %param.29) | copy-start | bytes 24580
  149.0 24.1 %slice-start = ((s8[5242880]{0:T(1024)(128)(4,1)}), s8[4194304]{0:T(1024)(128)(4,1)S(1)}, s32[]{:S(2)}) async-start(s8[5242880]{0:T(1024)(128)(4,1)} %bitcast.98), calls=%async_computation | async-start | bytes 8388608
  150.8 22.3 %slice-start.1 = ((s8[5242880]{0:T(1024)(128)(4,1)}), s8[1048576]{0:T(1024)(128)(4,1)S(1)}, s32[]{:S(2)}) async-start(s8[5242880]{0:T(1024)(128)(4,1)} %bitcast.98), calls=%async_computation.1 | async-start | bytes 2097152
  150.8 22.3 %copy-start.11 = (f32[16,128]{1,0:T(8,128)S(1)}, f32[16,128]{1,0:T(8,128)}, u32[]{:S(2)}) copy-start(f32[16,128]{1,0:T(8,128)} %param.23) | copy-start | bytes 24580
  152.1 9.7 %collective-permute-start = (f32[1,128,768]{2,1,0:T(8,128)S(1)}, f32[1,128,768]{2,1,0:T(8,128)S(1)}, u32[]{:S(2)}, u32[]{:S(2)}) collective-permute-start(f32[1,128,768]{2,1,0:T(8,128)S(1)} %get-tuple-element.345), channel_id=1, source_target_pairs={{4,0},{8,4},{12,8},{16,12},{20,16},{24,20},{28,24},{32,28},{36,32}... | collective-permute-start | bytes 1179656 | tf_op jit(solution)/shard_map/ppermute | solution.py:23
  154.0 13.3 %collective-permute-start.1 = (f32[1,128,768]{2,1,0:T(8,128)S(1)}, f32[1,128,768]{2,1,0:T(8,128)S(1)}, u32[]{:S(2)}, u32[]{:S(2)}) collective-permute-start(f32[1,128,768]{2,1,0:T(8,128)S(1)} %get-tuple-element.344), channel_id=1, source_target_pairs={{0,4},{4,8},{8,12},{12,16},{16,20},{20,24},{24,28},{28,32},{32,36}... | collective-permute-start | bytes 1179656 | tf_op jit(solution)/shard_map/ppermute | solution.py:21
  168.4 2.6 collective-permute-start.3
  169.7 3.4 collective-permute-start.2
  184.3 23.3 %copy-start.5 = (f32[16,128,768]{2,1,0:T(8,128)}, f32[16,128,768]{2,1,0:T(8,128)S(1)}, u32[]{:S(2)}) copy-start(f32[16,128,768]{2,1,0:T(8,128)S(1)} %fusion.69) | copy-start | bytes 18874372
  184.3 25.1 %copy-start.7 = (bf16[16,128,768]{2,1,0:T(8,128)(2,1)S(1)}, bf16[16,128,768]{2,1,0:T(8,128)(2,1)}, u32[]{:S(2)}) copy-start(bf16[16,128,768]{2,1,0:T(8,128)(2,1)} %param.22) | copy-start | bytes 9437188
  184.4 12.5 %collective-permute-start.4 = (f32[1,128,768]{2,1,0:T(8,128)S(1)}, f32[1,128,768]{2,1,0:T(8,128)S(1)}, u32[]{:S(2)}, u32[]{:S(2)}) collective-permute-start(f32[1,128,768]{2,1,0:T(8,128)S(1)} %get-tuple-element.343), channel_id=1, source_target_pairs={{4,0},{8,4},{12,8},{16,12},{20,16},{24,20},{28,24},{32,28},{36,32}... | collective-permute-start | bytes 1179656 | tf_op jit(solution)/shard_map/ppermute | solution.py:23
  186.7 15.8 %collective-permute-start.5 = (f32[1,128,768]{2,1,0:T(8,128)S(1)}, f32[1,128,768]{2,1,0:T(8,128)S(1)}, u32[]{:S(2)}, u32[]{:S(2)}) collective-permute-start(f32[1,128,768]{2,1,0:T(8,128)S(1)} %get-tuple-element.342), channel_id=1, source_target_pairs={{0,4},{4,8},{8,12},{12,16},{16,20},{20,24},{24,28},{28,32},{32,36}... | collective-permute-start | bytes 1179656 | tf_op jit(solution)/shard_map/ppermute | solution.py:21
  202.6 5.0 %collective-permute-start.7 = (f32[18,1,768]{2,1,0:T(1,128)S(1)}, f32[18,1,768]{2,1,0:T(1,128)S(1)}, u32[]{:S(2)}, u32[]{:S(2)}) collective-permute-start(f32[18,1,768]{2,1,0:T(1,128)S(1)} %get-tuple-element.331), channel_id=1, source_target_pairs={{0,1},{1,2},{2,3},{4,5},{5,6},{6,7},{8,9},{9,10},{10,11},{12,13},{... | collective-permute-start | bytes 165896 | tf_op jit(solution)/shard_map/ppermute | solution.py:21
  206.3 3.1 collective-permute-start.6
  224.1 56.8 %copy-start.4 = (f32[16,128,768]{2,1,0:T(8,128)}, f32[16,128,768]{2,1,0:T(8,128)S(1)}, u32[]{:S(2)}) copy-start(f32[16,128,768]{2,1,0:T(8,128)S(1)} %get-tuple-element.350) | copy-start | bytes 18874372
  224.2 12.4 %collective-permute-start.12 = (f32[1,128,768]{2,1,0:T(8,128)S(1)}, f32[1,128,768]{2,1,0:T(8,128)S(1)}, u32[]{:S(2)}, u32[]{:S(2)}) collective-permute-start(f32[1,128,768]{2,1,0:T(8,128)S(1)} %get-tuple-element.339), channel_id=1, source_target_pairs={{4,0},{8,4},{12,8},{16,12},{20,16},{24,20},{28,24},{32,28},{36,32}... | collective-permute-start | bytes 1179656 | tf_op jit(solution)/shard_map/ppermute | solution.py:23
  226.1 16.1 %collective-permute-start.13 = (f32[1,128,768]{2,1,0:T(8,128)S(1)}, f32[1,128,768]{2,1,0:T(8,128)S(1)}, u32[]{:S(2)}, u32[]{:S(2)}) collective-permute-start(f32[1,128,768]{2,1,0:T(8,128)S(1)} %get-tuple-element.338), channel_id=1, source_target_pairs={{0,4},{4,8},{8,12},{12,16},{16,20},{20,24},{24,28},{28,32},{32,36}... | collective-permute-start | bytes 1179656 | tf_op jit(solution)/shard_map/ppermute | solution.py:21
  242.2 4.7 %collective-permute-start.15 = (f32[18,1,768]{2,1,0:T(1,128)S(1)}, f32[18,1,768]{2,1,0:T(1,128)S(1)}, u32[]{:S(2)}, u32[]{:S(2)}) collective-permute-start(f32[18,1,768]{2,1,0:T(1,128)S(1)} %get-tuple-element.327), channel_id=1, source_target_pairs={{0,1},{1,2},{2,3},{4,5},{5,6},{6,7},{8,9},{9,10},{10,11},{12,13},{... | collective-permute-start | bytes 165896 | tf_op jit(solution)/shard_map/ppermute | solution.py:21
  245.4 17.6 %copy-start.13 = (s32[1,1024]{1,0:T(1,128)S(1)}, s32[1,1024]{1,0:T(1,128)}, u32[]{:S(2)}) copy-start(s32[1,1024]{1,0:T(1,128)} %param.24) | copy-start | bytes 12292
  245.4 3.1 collective-permute-start.14
  257.1 12.4 %collective-permute-start.16 = (f32[1,128,768]{2,1,0:T(8,128)S(1)}, f32[1,128,768]{2,1,0:T(8,128)S(1)}, u32[]{:S(2)}, u32[]{:S(2)}) collective-permute-start(f32[1,128,768]{2,1,0:T(8,128)S(1)} %get-tuple-element.337), channel_id=1, source_target_pairs={{4,0},{8,4},{12,8},{16,12},{20,16},{24,20},{28,24},{32,28},{36,32}... | collective-permute-start | bytes 1179656 | tf_op jit(solution)/shard_map/ppermute | solution.py:23
  259.1 16.1 %collective-permute-start.17 = (f32[1,128,768]{2,1,0:T(8,128)S(1)}, f32[1,128,768]{2,1,0:T(8,128)S(1)}, u32[]{:S(2)}, u32[]{:S(2)}) collective-permute-start(f32[1,128,768]{2,1,0:T(8,128)S(1)} %get-tuple-element.336), channel_id=1, source_target_pairs={{0,4},{4,8},{8,12},{12,16},{16,20},{20,24},{24,28},{28,32},{32,36}... | collective-permute-start | bytes 1179656 | tf_op jit(solution)/shard_map/ppermute | solution.py:21
  269.6 12.3 %copy-start.9 = (f32[1,128,768]{2,1,0:T(8,128)}, f32[1,128,768]{2,1,0:T(8,128)S(1)}, u32[]{:S(2)}) copy-start(f32[1,128,768]{2,1,0:T(8,128)S(1)} %collective-permute-done.16) | copy-start | bytes 1179652
  275.1 6.8 %copy-start.10 = (f32[1,128,768]{2,1,0:T(8,128)}, f32[1,128,768]{2,1,0:T(8,128)S(1)}, u32[]{:S(2)}) copy-start(f32[1,128,768]{2,1,0:T(8,128)S(1)} %collective-permute-done.17) | copy-start | bytes 1179652
  276.5 11.3 %collective-permute-start.19 = (f32[18,1,768]{2,1,0:T(1,128)S(1)}, f32[18,1,768]{2,1,0:T(1,128)S(1)}, u32[]{:S(2)}, u32[]{:S(2)}) collective-permute-start(f32[18,1,768]{2,1,0:T(1,128)S(1)} %get-tuple-element.325), channel_id=1, source_target_pairs={{0,1},{1,2},{2,3},{4,5},{5,6},{6,7},{8,9},{9,10},{10,11},{12,13},{... | collective-permute-start | bytes 165896 | tf_op jit(solution)/shard_map/ppermute | solution.py:21
  279.6 8.1 %collective-permute-start.18 = (f32[18,1,768]{2,1,0:T(1,128)S(1)}, f32[18,1,768]{2,1,0:T(1,128)}, u32[]{:S(2)}, u32[]{:S(2)}) collective-permute-start(f32[18,1,768]{2,1,0:T(1,128)S(1)} %get-tuple-element.324), channel_id=1, source_target_pairs={{1,0},{2,1},{3,2},{5,4},{6,5},{7,6},{9,8},{10,9},{11,10},{13,12},{... | collective-permute-start | bytes 165896 | tf_op jit(solution)/shard_map/ppermute | solution.py:23
  281.9 34.9 %collective-permute-start.8 = (f32[1,128,768]{2,1,0:T(8,128)}, f32[1,128,768]{2,1,0:T(8,128)}, u32[]{:S(2)}, u32[]{:S(2)}) collective-permute-start(f32[1,128,768]{2,1,0:T(8,128)} %get-tuple-element.341), channel_id=1, source_target_pairs={{4,0},{8,4},{12,8},{16,12},{20,16},{24,20},{28,24},{32,28},{36,32}... | collective-permute-start | bytes 1179656 | tf_op jit(solution)/shard_map/ppermute | solution.py:23
  283.8 33.0 %collective-permute-start.9 = (f32[1,128,768]{2,1,0:T(8,128)}, f32[1,128,768]{2,1,0:T(8,128)}, u32[]{:S(2)}, u32[]{:S(2)}) collective-permute-start(f32[1,128,768]{2,1,0:T(8,128)} %get-tuple-element.340), channel_id=1, source_target_pairs={{0,4},{4,8},{8,12},{12,16},{16,20},{20,24},{24,28},{28,32},{32,36}... | collective-permute-start | bytes 1179656 | tf_op jit(solution)/shard_map/ppermute | solution.py:21
  309.3 15.3 %collective-permute-start.20 = (f32[1,128,768]{2,1,0:T(8,128)}, f32[1,128,768]{2,1,0:T(8,128)S(1)}, u32[]{:S(2)}, u32[]{:S(2)}) collective-permute-start(f32[1,128,768]{2,1,0:T(8,128)} %get-tuple-element.335), channel_id=1, source_target_pairs={{4,0},{8,4},{12,8},{16,12},{20,16},{24,20},{28,24},{32,28},{36,32}... | collective-permute-start | bytes 1179656 | tf_op jit(solution)/shard_map/ppermute | solution.py:23
  314.8 17.6 %collective-permute-start.21 = (f32[1,128,768]{2,1,0:T(8,128)}, f32[1,128,768]{2,1,0:T(8,128)S(1)}, u32[]{:S(2)}, u32[]{:S(2)}) collective-permute-start(f32[1,128,768]{2,1,0:T(8,128)} %get-tuple-element.334), channel_id=1, source_target_pairs={{0,4},{4,8},{8,12},{12,16},{16,20},{20,24},{24,28},{28,32},{32,36}... | collective-permute-start | bytes 1179656 | tf_op jit(solution)/shard_map/ppermute | solution.py:21
  316.7 19.9 %slice-start.2 = ((s8[6291456]{0:T(1024)(128)(4,1)}), s8[4194304]{0:T(1024)(128)(4,1)S(1)}, s32[]{:S(2)}) async-start(s8[6291456]{0:T(1024)(128)(4,1)} %bitcast.100), calls=%async_computation.2 | async-start | bytes 8388608
  316.8 19.9 %slice-start.3 = ((s8[6291456]{0:T(1024)(128)(4,1)}), s8[2097152]{0:T(1024)(128)(4,1)S(1)}, s32[]{:S(2)}) async-start(s8[6291456]{0:T(1024)(128)(4,1)} %bitcast.100), calls=%async_computation.3 | async-start | bytes 4194304
  316.8 28.4 %slice-start.6 = ((s8[6291456]{0:T(1024)(128)(4,1)}), s8[4194304]{0:T(1024)(128)(4,1)S(1)}, s32[]{:S(2)}) async-start(s8[6291456]{0:T(1024)(128)(4,1)} %bitcast.106), calls=%async_computation.6 | async-start | bytes 8388608
  318.2 18.4 %collective-permute-start.11 = (f32[18,1,768]{2,1,0:T(1,128)S(1)}, f32[18,1,768]{2,1,0:T(1,128)S(1)}, u32[]{:S(2)}, u32[]{:S(2)}) collective-permute-start(f32[18,1,768]{2,1,0:T(1,128)S(1)} %get-tuple-element.329), channel_id=1, source_target_pairs={{0,1},{1,2},{2,3},{4,5},{5,6},{6,7},{8,9},{9,10},{10,11},{12,13},{... | collective-permute-start | bytes 165896 | tf_op jit(solution)/shard_map/ppermute | solution.py:21
  320.9 24.3 %slice-start.7 = ((s8[6291456]{0:T(1024)(128)(4,1)}), s8[2097152]{0:T(1024)(128)(4,1)S(1)}, s32[]{:S(2)}) async-start(s8[6291456]{0:T(1024)(128)(4,1)} %bitcast.106), calls=%async_computation.7 | async-start | bytes 4194304
  320.9 15.7 %collective-permute-start.10 = (f32[18,1,768]{2,1,0:T(1,128)S(1)}, f32[18,1,768]{2,1,0:T(1,128)S(1)}, u32[]{:S(2)}, u32[]{:S(2)}) collective-permute-start(f32[18,1,768]{2,1,0:T(1,128)S(1)} %get-tuple-element.328), channel_id=1, source_target_pairs={{1,0},{2,1},{3,2},{5,4},{6,5},{7,6},{9,8},{10,9},{11,10},{13,12},{... | collective-permute-start | bytes 165896 | tf_op jit(solution)/shard_map/ppermute | solution.py:23
  333.6 11.6 %collective-permute-start.23 = (f32[18,1,768]{2,1,0:T(1,128)S(1)}, f32[18,1,768]{2,1,0:T(1,128)S(1)}, u32[]{:S(2)}, u32[]{:S(2)}) collective-permute-start(f32[18,1,768]{2,1,0:T(1,128)S(1)} %get-tuple-element.323), channel_id=1, source_target_pairs={{0,1},{1,2},{2,3},{4,5},{5,6},{6,7},{8,9},{9,10},{10,11},{12,13},{... | collective-permute-start | bytes 165896 | tf_op jit(solution)/shard_map/ppermute | solution.py:21
  335.0 10.2 %slice-start.4 = ((s8[6291456]{0:T(1024)(128)(4,1)}), s8[4194304]{0:T(1024)(128)(4,1)S(1)}, s32[]{:S(2)}) async-start(s8[6291456]{0:T(1024)(128)(4,1)} %bitcast.102), calls=%async_computation.4 | async-start | bytes 8388608
  335.0 10.2 %slice-start.5 = ((s8[6291456]{0:T(1024)(128)(4,1)}), s8[2097152]{0:T(1024)(128)(4,1)S(1)}, s32[]{:S(2)}) async-start(s8[6291456]{0:T(1024)(128)(4,1)} %bitcast.102), calls=%async_computation.5 | async-start | bytes 4194304
  335.0 10.2 %collective-permute-start.22 = (f32[18,1,768]{2,1,0:T(1,128)S(1)}, f32[18,1,768]{2,1,0:T(1,128)S(1)}, u32[]{:S(2)}, u32[]{:S(2)}) collective-permute-start(f32[18,1,768]{2,1,0:T(1,128)S(1)} %get-tuple-element.322), channel_id=1, source_target_pairs={{1,0},{2,1},{3,2},{5,4},{6,5},{7,6},{9,8},{10,9},{11,10},{13,12},{... | collective-permute-start | bytes 165896 | tf_op jit(solution)/shard_map/ppermute | solution.py:23
  350.6 2.7 copy-start.6
  413.3 8.4 %copy-start.1 = (bf16[16,128,768]{2,1,0:T(8,128)(2,1)S(1)}, bf16[16,128,768]{2,1,0:T(8,128)(2,1)}, u32[]{:S(2)}) copy-start(bf16[16,128,768]{2,1,0:T(8,128)(2,1)} %param.20) | copy-start | bytes 9437188
where the time goes:
time: 425 us; the launch traced here: 422 us
  other arithmetic  122 us (29%)
  matrix products  88 us (21%)
  local copies, waits for them, and re-layouts  77.5 us (18%)
  starting transfers between devices  61.5 us (14%)
  waiting for transfers between devices  60.3 us (14%)
  loops' own time  10.4 us (2%)
    mul x3, other arithmetic, per_device(): extended = padded(kappa_cells * adjoint, (('elem', 0), ('face', 1)), 1)  41.5 us
    ppermute x12, starting transfers between devices, padded(): lax.ppermute(tail, axis, [(i, (i + 1) % count) for i in range(ends)])  37.7 us
    dot_general x16, matrix products, forward_block(): jnp.dot(tangent, layer_weights[layer], preferred_element_type=jnp.float32)  30.6 us
    ppermute x12, waiting for transfers between devices, padded(): lax.ppermute(head, axis, [((i + 1) % count, i) for i in range(ends)])  30.2 us
    dynamic_update_slice x16, local copies, waits for them, and re-layouts, forward_blocks(): return lax.map(forward_run_block, (flags, x_blocks, d_blocks))  30.1 us
    ppermute x12, waiting for transfers between devices, padded(): lax.ppermute(tail, axis, [(i, (i + 1) % count) for i in range(ends)])  30.1 us
    dot_general x24, matrix products, contract_back(): lax.dot_general(left, right, (((1,), (1,)), ((), ())), preferred_element_...  26.8 us
    ppermute x12, starting transfers between devices, padded(): lax.ppermute(head, axis, [((i + 1) % count, i) for i in range(ends)])  23.8 us
  transfers between devices with their start and end apart: 24, of which 13 were waited for; matrix products, arithmetic and copies ran while one was open for 8% of the time, Pallas kernels for 0%

commit v1 on v0

v1 whole, which is shorter than its diff:
```python
import jax
import jax.numpy as jnp
import numpy as np
from jax import lax
from jax.experimental import pallas as pl
from jax.experimental.pallas import tpu as pltpu
from jax.sharding import PartitionSpec as P

PHYS_STEP = 4.0
REACH = 3
LANES = 128
SIDE = 8
CORNERS = 16
F32 = jnp.float32
BF16 = jnp.bfloat16
VMEM = 60 * 1024 * 1024


def _params(count=1):
    return pltpu.CompilerParams(
        dimension_semantics=("arbitrary",) * count, vmem_limit_bytes=VMEM
    )


def _dot(a, b):
    return jnp.dot(a, b, preferred_element_type=F32)


def _dot_t(a, b):
    return lax.dot_general(a, b, (((1,), (1,)), ((), ())), preferred_element_type=F32)


def _pick(shape, targets):
    row = lax.broadcasted_iota(jnp.int32, shape, 0)
    col = lax.broadcasted_iota(jnp.int32, shape, 1)
    hit = jnp.zeros(shape, jnp.bool_)
    for k, c in targets:
        hit = hit | ((row == k) & (col == c))
    return hit.astype(F32).astype(BF16)


def _split(value):
    hi = value.astype(BF16)
    return hi, (value - hi.astype(F32)).astype(BF16)


def edge_kernel(
    counts, listed, kappa, s_lo, s_hi, p_lo, p_hi, a_lo, a_hi, left, right, mask_out
):
    size_x, size_y = kappa.shape
    width = s_lo.shape[1]
    channels = s_lo.shape[2]
    count = counts[0, 0]
    index = listed[...]
    cap = index.shape[1]
    shift = size_y.bit_length() - 1
    pos = lax.broadcasted_iota(jnp.int32, (size_x, cap), 1)
    sub = lax.broadcasted_iota(jnp.int32, (size_x, cap), 0)
    rows = ((sub == (index >> shift)) & (pos < count)).astype(F32).astype(BF16)
    sub_y = lax.broadcasted_iota(jnp.int32, (size_y, cap), 0)
    cols = (sub_y == (index & (size_y - 1))).astype(F32).astype(BF16)
    mask = _dot_t(rows, cols)
    mask_t = _dot_t(cols, rows)
    for x in range(size_x):
        mask_out[x * size_y : (x + 1) * size_y, :] = jnp.broadcast_to(
            mask_t[:, x : x + 1], (size_y, LANES)
        ).astype(BF16)
    k_all = kappa[...]
    shape = (REACH * size_x, size_x * width)
    row = lax.broadcasted_iota(jnp.int32, shape, 0)
    col = lax.broadcasted_iota(jnp.int32, shape, 1)
    want = (row % size_x) * width + row // size_x
    for msg, blocks, first in (
        (left, (s_lo, p_lo, a_lo), 0),
        (right, (s_hi, p_hi, a_hi), size_y - REACH),
    ):
        pick = (col == want + first % width).astype(F32).astype(BF16)
        for n, block in enumerate(blocks):
            msg[:, n * channels : (n + 1) * channels] = _dot(
                pick, block[...].reshape(size_x * width, channels)
            ).astype(BF16)
        at = len(blocks) * channels
        for j in range(REACH):
            here = slice(j * size_x, (j + 1) * size_x)
            y = first + j
            hi, lo = _split(jnp.broadcast_to(k_all[:, y : y + 1], (size_x, LANES)))
            msg[here, at : at + LANES] = jnp.broadcast_to(
                mask[:, y : y + 1], (size_x, LANES)
            ).astype(BF16)
            msg[here, at + LANES : at + 2 * LANES] = hi
            msg[here, at + 2 * LANES : at + 3 * LANES] = lo


def make_edges(counts, listed, kappa, state, pert, adj):
    size_x, size_y, channels = state.shape
    width = 16
    last = size_y // width - 1
    low = pl.BlockSpec((size_x, width, channels), lambda i: (0, 0, 0))
    high = pl.BlockSpec((size_x, width, channels), lambda i: (0, last, 0))
    strip = jax.ShapeDtypeStruct((REACH * size_x, 3 * channels + 3 * LANES), BF16)
    return pl.pallas_call(
        edge_kernel,
        grid=(1,),
        in_specs=[
            pl.BlockSpec(memory_space=pltpu.SMEM),
            pl.BlockSpec(listed.shape, lambda i: (0, 0)),
            pl.BlockSpec(kappa.shape, lambda i: (0, 0)),
            low, high, low, high, low, high,
        ],
        out_specs=[
            pl.BlockSpec(strip.shape, lambda i: (0, 0)),
            pl.BlockSpec(strip.shape, lambda i: (0, 0)),
            pl.BlockSpec((size_x * size_y, LANES), lambda i: (0, 0)),
        ],
        out_shape=[strip, strip, jax.ShapeDtypeStruct((size_x * size_y, LANES), BF16)],
        compiler_params=_params(),
        name="edges",
    )(counts, listed, kappa, state, state, pert, pert, adj, adj)


def _corner_picks(size_x, top):
    near, next_ = (0, 1) if top else (size_x - 1, size_x - 2)
    left = [(0, 2 * size_x + near), (1, size_x + near), (2, 2 * size_x + next_)]
    right = [(3, near), (4, size_x + near), (5, next_)]
    shape = (CORNERS, REACH * size_x)
    return _pick(shape, left), _pick(shape, right)


def _kappa_wide(kappa, aux_l, aux_r):
    size_x, size_y = kappa.shape
    wide = jnp.concatenate([kappa[...], jnp.zeros((size_x, LANES), F32)], axis=1)
    lane = lax.broadcasted_iota(jnp.int32, wide.shape, 1)
    for aux, first in ((aux_l, wide.shape[1] - REACH), (aux_r, size_y)):
        for j in range(REACH):
            here = slice(j * size_x, (j + 1) * size_x)
            value = aux[here, LANES : 2 * LANES].astype(F32) + aux[
                here, 2 * LANES : 3 * LANES
            ].astype(F32)
            wide = jnp.where(lane == first + j, jnp.concatenate([value, value], axis=1), wide)
    return wide


def adjoint_border_kernel(kappa, aux_l, aux_r, strip_l, strip_r, rows_t, rows_b, top, bot):
    size_x, size_y = kappa.shape
    channels = strip_l.shape[1]
    body = REACH * size_y
    hi, lo = _split(_kappa_wide(kappa, aux_l, aux_r))
    extra = jnp.zeros((size_x, channels - 2 * hi.shape[1]), BF16)
    for msg, rows, is_top in ((top, rows_t, True), (bot, rows_b, False)):
        first = 0 if is_top else rows.shape[0] - REACH
        msg[0:body, :] = rows[first : first + REACH].reshape(body, channels)
        pick_l, pick_r = _corner_picks(size_x, is_top)
        msg[body : body + CORNERS, :] = (
            _dot(pick_l, strip_l[...]) + _dot(pick_r, strip_r[...])
        ).astype(BF16)
        msg[body + CORNERS :, :] = jnp.concatenate([hi, lo, extra], axis=1)


def adjoint_border(kappa, from_l, from_r, adj):
    size_x, size_y, channels = adj.shape
    block = 4
    last = size_x // block - 1
    out = jax.ShapeDtypeStruct((REACH * size_y + CORNERS + size_x, channels), BF16)
    strip = pl.BlockSpec((REACH * size_x, channels), lambda i: (0, 2))
    aux = pl.BlockSpec((REACH * size_x, 3 * LANES), lambda i: (0, channels // LANES))
    return pl.pallas_call(
        adjoint_border_kernel,
        grid=(1,),
        in_specs=[
            pl.BlockSpec(kappa.shape, lambda i: (0, 0)),
            aux, aux, strip, strip,
            pl.BlockSpec((block, size_y, channels), lambda i: (0, 0, 0)),
            pl.BlockSpec((block, size_y, channels), lambda i: (last, 0, 0)),
        ],
        out_specs=[pl.BlockSpec(out.shape, lambda i: (0, 0))] * 2,
        out_shape=[out, out],
        compiler_params=_params(),
        name="adjoint_border",
    )(kappa, from_l, from_r, from_l, from_r, adj, adj)


def tangent_border_kernel(strip_l, strip_r, moved_s, rows_t, rows_b, moved_t, moved_b, top, bot):
    channels = strip_l.shape[1]
    size_y = rows_t.shape[1]
    size_x = strip_l.shape[0] // REACH
    body = REACH * size_y
    for msg, rows, moved, is_top in (
        (top, rows_t, moved_t, True),
        (bot, rows_b, moved_b, False),
    ):
        first = 0 if is_top else rows.shape[0] - REACH
        msg[0:body, :LANES] = moved[first * size_y : (first + REACH) * size_y]
        msg[0:body, LANES:] = rows[first : first + REACH, :, LANES:].reshape(
            body, channels - LANES
        )
        pick_l, pick_r = _corner_picks(size_x, is_top)
        cut = REACH * size_x
        msg[body:, :LANES] = (
            _dot(pick_l, moved_s[:cut]) + _dot(pick_r, moved_s[cut:])
        ).astype(BF16)
        msg[body:, LANES:] = (
            _dot(pick_l, strip_l[:, LANES:]) + _dot(pick_r, strip_r[:, LANES:])
        ).astype(BF16)


def tangent_border(from_l, from_r, moved_strips, pert, moved):
    size_x, size_y, channels = pert.shape
    block = 4
    last = size_x // block - 1
    out = jax.ShapeDtypeStruct((REACH * size_y + CORNERS, channels), BF16)
    strip = pl.BlockSpec((REACH * size_x, channels), lambda i: (0, 1))
    return pl.pallas_call(
        tangent_border_kernel,
        grid=(1,),
        in_specs=[
            strip, strip,
            pl.BlockSpec(moved_strips.shape, lambda i: (0, 0)),
            pl.BlockSpec((block, size_y, channels), lambda i: (0, 0, 0)),
            pl.BlockSpec((block, size_y, channels), lambda i: (last, 0, 0)),
            pl.BlockSpec((block * size_y, LANES), lambda i: (0, 0)),
            pl.BlockSpec((block * size_y, LANES), lambda i: (last, 0)),
        ],
        out_specs=[pl.BlockSpec(out.shape, lambda i: (0, 0))] * 2,
        out_shape=[out, out],
        compiler_params=_params(),
        name="tangent_border",
    )(from_l, from_r, moved_strips, pert, pert, moved, moved)


def _forward(h, t, w_in, w_mid, w_out, biases, slopes):
    rows = h.shape[0]
    units = w_in.shape[1]
    for layer in range(1 + w_mid.shape[0]):
        weights = w_in[...] if layer == 0 else w_mid[layer - 1]
        a = _dot(h, weights) + biases[layer : layer + 1, :]
        v = jnp.tanh(a)
        slope = 1.0 - v * v
        h = v.astype(BF16)
        t = (slope * _dot(t, weights)).astype(BF16)
        if slopes is not None:
            slopes[0:rows, layer * units : (layer + 1) * units] = slope.astype(BF16)
    return _dot(t, w_out[...])


def forward_kernel(
    state, pert, mask, s_l, s_r, p_l, p_r, aux_l, aux_r, w_in, w_mid, w_out, biases,
    slopes, moved, moved_s,
):
    step = pl.program_id(0)
    blocks = pl.num_programs(0) - 1

    @pl.when(step < blocks)
    def _():
        channels = state.shape[2]
        x = state[...].reshape(-1, channels)
        d = pert[...].reshape(-1, channels)
        jac = _forward(x, d, w_in, w_mid, w_out, biases, slopes)
        moved[...] = (
            d[:, :LANES].astype(F32) + PHYS_STEP * mask[...].astype(F32) * jac
        ).astype(BF16)

    @pl.when(step == blocks)
    def _():
        x = jnp.concatenate([s_l[...], s_r[...]], axis=0)
        d = jnp.concatenate([p_l[...], p_r[...]], axis=0)
        live = jnp.concatenate([aux_l[:, :LANES], aux_r[:, :LANES]], axis=0)
        jac = _forward(x, d, w_in, w_mid, w_out, biases, None)
        moved_s[...] = (
            d[:, :LANES].astype(F32) + PHYS_STEP * live.astype(F32) * jac
        ).astype(BF16)


def forward(state, pert, mask, from_l, from_r, w_in, w_mid, w_out, biases):
    size_x, size_y, channels = state.shape
    columns = size_x * size_y
    xs = 2
    rows = xs * size_y
    blocks = size_x // xs
    layers, units = biases.shape
    cut = REACH * size_x
    whole = lambda a: pl.BlockSpec(a.shape, lambda i: (0,) * a.ndim)
    own = lambda i: (jnp.minimum(i, blocks - 1), 0, 0)
    own2 = lambda i: (jnp.minimum(i, blocks - 1), 0)
    strip = lambda n: pl.BlockSpec((cut, channels), lambda i: (0, n))
    aux = pl.BlockSpec((cut, 3 * LANES), lambda i: (0, channels // LANES))
    return pl.pallas_call(
        forward_kernel,
        grid=(blocks + 1,),
        in_specs=[
            pl.BlockSpec((xs, size_y, channels), own),
            pl.BlockSpec((xs, size_y, channels), own),
            pl.BlockSpec((rows, LANES), own2),
            strip(0), strip(0), strip(1), strip(1), aux, aux,
            whole(w_in), whole(w_mid), whole(w_out), whole(biases),
        ],
        out_specs=[
            pl.BlockSpec((rows, layers * units), own2),
            pl.BlockSpec((rows, LANES), own2),
            pl.BlockSpec((2 * cut, LANES), lambda i: (0, 0)),
        ],
        out_shape=[
            jax.ShapeDtypeStruct((columns, layers * units), BF16),
            jax.ShapeDtypeStruct((columns, LANES), BF16),
            jax.ShapeDtypeStruct((2 * cut, LANES), BF16),
        ],
        compiler_params=_params(),
        name="forward",
    )(state, pert, mask, from_l, from_r, from_l, from_r, from_l, from_r, w_in, w_mid, w_out, biases)


def _side_picks(size_x):
    frame = size_x + 2 * REACH
    strips = REACH * size_x
    picks = np.zeros((2, frame * SIDE, LANES), np.float32)
    for x in range(size_x):
        for j in range(REACH):
            picks[0, (x + REACH) * SIDE + SIDE - REACH + j, j * size_x + x] = 1
            picks[1, (x + REACH) * SIDE + j, j * size_x + x] = 1
    for base, step, near in ((strips, -1, REACH - 1), (strips + CORNERS, 1, REACH + size_x)):
        for k, (dx, dy) in enumerate(((0, 0), (0, 1), (1, 0))):
            picks[0, (near + step * dx) * SIDE + SIDE - 1 - dy, base + k] = 1
            picks[1, (near + step * dx) * SIDE + dy, base + 3 + k] = 1
    return jnp.asarray(picks.reshape(2 * frame * SIDE, LANES), BF16)


def _fill(frame, own, above, below, strip_l, strip_r, picks, size_x, size_y):
    row = size_y + 2 * SIDE
    count = size_x + 2 * REACH
    body = REACH * size_y
    half = count * SIDE
    spare = jnp.zeros((LANES - strip_l.shape[0] - 2 * CORNERS, LANES), BF16)
    ends = [above[body : body + CORNERS, :], below[body : body + CORNERS, :], spare]
    side_l = _dot(picks[:half], jnp.concatenate([strip_l] + ends, axis=0))
    side_r = _dot(picks[half:], jnp.concatenate([strip_r] + ends, axis=0))
    for r in range(count):
        at = r * row
        frame[at : at + SIDE, :] = side_l[r * SIDE : (r + 1) * SIDE]
        frame[at + SIDE + size_y : at + row, :] = side_r[r * SIDE : (r + 1) * SIDE]
        if r < REACH:
            value = above[r * size_y : (r + 1) * size_y, :]
        elif r < REACH + size_x:
            value = own[r - REACH]
        else:
            k = r - REACH - size_x
            value = below[k * size_y : (k + 1) * size_y, :]
        frame[at + SIDE : at + SIDE + size_y, :] = value.astype(F32)


def _substep(src, kap, row, r, lo, size):
    at = r * row + lo
    mid = src[at : at + size, :]
    near = (src[at - row : at - row + size, :] + src[at + row : at + row + size, :]) + (
        src[at - 1 : at - 1 + size, :] + src[at + 1 : at + 1 + size, :]
    )
    return mid + kap[at : at + size, :] * (near - 4.0 * mid)


def _transport(ping, pong, kap, size_x, size_y, emit):
    row = size_y + 2 * SIDE
    count = size_x + 2 * REACH
    src, dst = ping, pong
    for step in range(1, REACH):
        for r in range(step, count - step):
            dst[r * row : (r + 1) * row, :] = _substep(src, kap, row, r, 0, row)
        src, dst = dst, src
    for x in range(size_x):
        emit(x, _substep(src, kap, row, x + REACH, SIDE, size_y))


def _kappa_frame(kappa, aux_l, aux_r, above, below, natural, out):
    size_x, size_y = kappa.shape
    row = size_y + 2 * SIDE
    natural[...] = jnp.zeros(natural.shape, F32)
    wide = 2 * LANES
    natural[REACH : REACH + size_x, :] = _kappa_wide(kappa, aux_l, aux_r)
    up = above[:, :wide].astype(F32) + above[:, wide : 2 * wide].astype(F32)
    down = below[:, :wide].astype(F32) + below[:, wide : 2 * wide].astype(F32)
    natural[0:REACH, :] = up[size_x - REACH :]
    natural[REACH + size_x : 2 * REACH + size_x, :] = down[:REACH]
    own = natural[:, :LANES].T
    rest = natural[:, LANES:].T
    for r in range(size_x + 2 * REACH):
        at = r * row
        put = lambda a: jnp.broadcast_to(a[:, r : r + 1], (a.shape[0], LANES))
        out[at : at + SIDE, :] = put(rest[LANES - SIDE :])
        out[at + SIDE : at + SIDE + size_y, :] = put(own)
        out[at + SIDE + size_y : at + row, :] = put(rest[:SIDE])


def adjoint_kernel(
    adj, above, below, strip_l, strip_r, picks, kappa, aux_l, aux_r, k_above, k_below,
    mask, slopes, w_in, w_mid, w_out, kap, out, ping, pong, natural, inverse, moved,
):
    step = pl.program_id(0)
    groups = moved.shape[0]
    size_x, size_y = kappa.shape
    row = size_y + 2 * SIDE

    @pl.when(step == 0)
    def _():
        _kappa_frame(kappa, aux_l, aux_r, k_above, k_below, natural, kap)
        for x in range(size_x):
            at = (x + REACH) * row + SIDE
            inverse[x * size_y : (x + 1) * size_y, :] = 1.0 / kap[at : at + size_y, :]

    @pl.when(step < groups)
    def _():
        _fill(ping, adj, above, below, strip_l[...], strip_r[...], picks, size_x, size_y)
        ping[...] = ping[...] * kap[...]

        def emit(x, value):
            here = slice(x * size_y, (x + 1) * size_y)
            moved[step, here, :] = value * inverse[here, :]

        _transport(ping, pong, kap, size_x, size_y, emit)

    @pl.when(step >= groups)
    def _():
        rows = out.shape[0]
        units = w_in.shape[1]
        here = pl.ds(pl.multiple_of((step - groups) * rows, rows), rows)
        upstream = (PHYS_STEP * mask[...].astype(F32) * moved[0, here, :]).astype(BF16)
        pulled = _dot_t(upstream, w_out[...])
        for layer in reversed(range(1 + w_mid.shape[0])):
            weights = w_in[...] if layer == 0 else w_mid[layer - 1]
            slope = slopes[:, layer * units : (layer + 1) * units].astype(F32)
            pulled = _dot_t((pulled * slope).astype(BF16), weights)
        for g in range(groups):
            lanes = slice(g * LANES, (g + 1) * LANES)
            out[:, lanes] = moved[g, here, :] + pulled[:, lanes]


def adjoint_all(adj, above, below, from_l, from_r, kappa, mask, slopes, w_in, w_mid, w_out):
    size_x, size_y, channels = adj.shape
    columns = size_x * size_y
    groups = channels // LANES
    blocks = 8
    rows = columns // blocks
    row = size_y + 2 * SIDE
    frame = (size_x + 2 * REACH) * row
    cut = REACH * size_x
    picks = _side_picks(size_x)
    ends = REACH * size_y + CORNERS
    whole = lambda a: pl.BlockSpec(a.shape, lambda i: (0,) * a.ndim)
    lane = lambda i: jnp.minimum(i, groups - 1)
    later = lambda i: (jnp.maximum(i - groups, 0), 0)
    border = pl.BlockSpec((ends, LANES), lambda i: (0, lane(i)))
    strip = pl.BlockSpec((cut, LANES), lambda i: (0, 2 * groups + lane(i)))
    aux = pl.BlockSpec((cut, 3 * LANES), lambda i: (0, groups))
    k_rows = pl.BlockSpec((size_x, channels), lambda i: (ends // size_x, 0))
    return pl.pallas_call(
        adjoint_kernel,
        grid=(groups + blocks,),
        in_specs=[
            pl.BlockSpec((size_x, size_y, LANES), lambda i: (0, 0, lane(i))),
            border, border, strip, strip, whole(picks), whole(kappa), aux, aux, k_rows, k_rows,
            pl.BlockSpec((rows, LANES), later),
            pl.BlockSpec((rows, slopes.shape[1]), later),
            whole(w_in), whole(w_mid), whole(w_out),
        ],
        out_specs=[
            pl.BlockSpec((frame, LANES), lambda i: (0, 0)),
            pl.BlockSpec((rows, channels), later),
        ],
        out_shape=[
            jax.ShapeDtypeStruct((frame, LANES), F32),
            jax.ShapeDtypeStruct((columns, channels), F32),
        ],
        scratch_shapes=[
            pltpu.VMEM((frame, LANES), F32),
            pltpu.VMEM((frame, LANES), F32),
            pltpu.VMEM((LANES, 2 * LANES), F32),
            pltpu.VMEM((columns, LANES), F32),
            pltpu.VMEM((groups, columns, LANES), F32),
        ],
        compiler_params=_params(),
        name="adjoint",
    )(adj, above, below, from_l, from_r, picks, kappa, from_l, from_r, above, below,
      mask, slopes, w_in, w_mid, w_out)


def tangent_kernel(
    pert, moved, above, below, strip_l, strip_r, moved_s, picks, kap, out, ping, pong
):
    step = pl.program_id(0)
    size_x, size_y, _ = out.shape
    cut = moved_s.shape[0] // 2

    @pl.when(step == 0)
    def _():
        own = [moved[x * size_y : (x + 1) * size_y, :] for x in range(size_x)]
        _fill(ping, own, above, below, moved_s[:cut], moved_s[cut:], picks, size_x, size_y)

    @pl.when(step > 0)
    def _():
        _fill(ping, pert, above, below, strip_l[...], strip_r[...], picks, size_x, size_y)

    def emit(x, value):
        out[x] = value

    _transport(ping, pong, kap, size_x, size_y, emit)


def tangent_all(pert, moved, moved_strips, above, below, from_l, from_r, kap):
    size_x, size_y, channels = pert.shape
    groups = channels // LANES
    cut = REACH * size_x
    picks = _side_picks(size_x)
    whole = lambda a: pl.BlockSpec(a.shape, lambda i: (0,) * a.ndim)
    border = pl.BlockSpec((above.shape[0], LANES), lambda i: (0, i))
    strip = pl.BlockSpec((cut, LANES), lambda i: (0, groups + i))
    tile = pl.BlockSpec((size_x, size_y, LANES), lambda i: (0, 0, i))
    return pl.pallas_call(
        tangent_kernel,
        grid=(groups,),
        in_specs=[
            tile, whole(moved), border, border, strip, strip, whole(moved_strips),
            whole(picks), whole(kap),
        ],
        out_specs=tile,
        out_shape=jax.ShapeDtypeStruct((size_x, size_y, channels), F32),
        scratch_shapes=[pltpu.VMEM(kap.shape, F32), pltpu.VMEM(kap.shape, F32)],
        compiler_params=_params(),
        name="tangent",
    )(pert, moved, above, below, from_l, from_r, moved_strips, picks, kap)


def _shift(value, axis, way):
    ends = lax.axis_size(axis) - 1
    pairs = [(i, i + 1) if way > 0 else (i + 1, i) for i in range(ends)]
    return lax.ppermute(value, axis, pairs)


def per_device(
    state, perturbation, adjoint_end, kappa, act_list, counts, w_in, w_mid, w_out, biases
):
    size_x, size_y, channels = state.shape
    left, right, mask = make_edges(counts, act_list, kappa, state, perturbation, adjoint_end)
    from_l = _shift(right, "face", 1)
    from_r = _shift(left, "face", -1)
    top, bot = adjoint_border(kappa, from_l, from_r, adjoint_end)
    above = _shift(bot, "elem", 1)
    below = _shift(top, "elem", -1)
    slopes, moved, moved_s = forward(
        state, perturbation, mask, from_l, from_r, w_in, w_mid, w_out, biases
    )
    t_top, t_bot = tangent_border(from_l, from_r, moved_s, perturbation, moved)
    t_above = _shift(t_bot, "elem", 1)
    t_below = _shift(t_top, "elem", -1)
    kap, ad_out = adjoint_all(
        adjoint_end, above, below, from_l, from_r, kappa, mask, slopes, w_in, w_mid, w_out
    )
    tl_out = tangent_all(perturbation, moved, moved_s, t_above, t_below, from_l, from_r, kap)
    return tl_out, ad_out.reshape(size_x, size_y, channels)


def solution(mesh):
    tile = P("elem", "face", None)
    plane = P("elem", "face")
    return jax.shard_map(
        per_device,
        mesh=mesh,
        in_specs=(tile, tile, tile, plane, plane, plane, P(), P(), P(), P()),
        out_specs=(tile, tile),
        check_vma=False,
    )
```

time: 425 us -> 99.9 us (0.24)
  the two profiles are of different devices: /device:TPU:20 before, /device:TPU:7 now
where the time goes in v1:
time: 99.9 us; the launch traced here: 99.2 us
  Pallas kernels  63.5 us (64%)
  starting transfers between devices  25.6 us (26%)
  waiting for transfers between devices  5.94 us (6%)
  local copies, waits for them, and re-layouts  2.75 us (3%)
  between operations  1.39 us (1%)
    ppermute x6, starting transfers between devices, _shift(): return lax.ppermute(value, axis, pairs)  25.6 us
    pallas_call x1, Pallas kernels, adjoint_all(): pl.pallas_call(adjoint_kernel, grid=(groups + blocks,), in_specs=[pl.Bloc...  25.5 us
    pallas_call x1, Pallas kernels, forward(): pl.pallas_call(forward_kernel, grid=(blocks + 1,), in_specs=[pl.BlockSpec...  17.4 us
    pallas_call x1, Pallas kernels, tangent_all(): pl.pallas_call(tangent_kernel, grid=(groups,), in_specs=[tile, whole(move...  12 us
    ppermute x6, waiting for transfers between devices, _shift(): return lax.ppermute(value, axis, pairs)  5.94 us
    pallas_call x1, Pallas kernels, make_edges(): pl.pallas_call(edge_kernel, grid=(1,), in_specs=[pl.BlockSpec(memory_spac...  3.2 us
    unnamed x12, local copies, waits for them, and re-layouts  2.75 us
    pallas_call x1, Pallas kernels, tangent_border(): pl.pallas_call(tangent_border_kernel, grid=(1,), in_specs=[strip, strip,...  2.7 us
  transfers between devices with their start and end apart: 6, of which 2 were waited for; matrix products, arithmetic and copies ran while one was open for 0% of the time, Pallas kernels for 46%

profile of v1, /device:TPU:7, one launch (start us, length us, event | category | flops | bytes accessed | tf_op | source)
XLA Modules:
  0.0 99.2 jit_solution(9031357951654701925)
XLA Ops:
  1.3 3.2 %edges.1 = (bf16[48,2688]{1,0:T(8,128)(2,1)}, bf16[48,2688]{1,0:T(8,128)(2,1)}, bf16[2048,128]{1,0:T(8,128)(2,1)}) custom-call(s32[1,1]{1,0:T(1,128)S(6)} %copy.14.counts, s32[1,1024]{1,0:T(1,128)} %listed.1, f32[16,128]{1,0:T(8,128)} %kappa.5, bf16[16,128,768]{2,1,0:T(8,128)(2,1)} %state.1, bf16[16,128,768]{2,1,0:T(8,128)(2,1)} %state.1, ...), custom_call_target="tpu_custom_call" | custom-call | tf_op jit(solution)/shard_map/edges/pallas_call | solution.py:101
  4.5 3.8 %collective-permute-start = (bf16[48,2688]{1,0:T(8,128)(2,1)}, bf16[48,2688]{1,0:T(8,128)(2,1)S(1)}, u32[]{:S(2)}, u32[]{:S(2)}) collective-permute-start(bf16[48,2688]{1,0:T(8,128)(2,1)} %get-tuple-element.15), channel_id=1, source_target_pairs={{0,1},{1,2},{2,3},{4,5},{5,6},{6,7},{8,9},{9,10},{10,11},{12,13},{... | collective-permute-start | bytes 774152 | tf_op jit(solution)/shard_map/ppermute | solution.py:531
  8.2 1.9 %collective-permute-start.1 = (bf16[48,2688]{1,0:T(8,128)(2,1)}, bf16[48,2688]{1,0:T(8,128)(2,1)S(1)}, u32[]{:S(2)}, u32[]{:S(2)}) collective-permute-start(bf16[48,2688]{1,0:T(8,128)(2,1)} %get-tuple-element.16), channel_id=1, source_target_pairs={{1,0},{2,1},{3,2},{5,4},{6,5},{7,6},{9,8},{10,9},{11,10},{13,12},{... | collective-permute-start | bytes 774152 | tf_op jit(solution)/shard_map/ppermute | solution.py:531
  10.2 1.6 %collective-permute-done.s_l.p_l.aux_l.strip_l = bf16[48,2688]{1,0:T(8,128)(2,1)S(1)} collective-permute-done((bf16[48,2688]{1,0:T(8,128)(2,1)}, bf16[48,2688]{1,0:T(8,128)(2,1)S(1)}, u32[]{:S(2)}, u32[]{:S(2)}) %collective-permute-start) | collective-permute-done | bytes 258080 | tf_op jit(solution)/shard_map/ppermute | solution.py:531
  11.8 0.0 copy-start
  11.8 4.3 %collective-permute-done.1.s_r.p_r.aux_r.strip_r = bf16[48,2688]{1,0:T(8,128)(2,1)S(1)} collective-permute-done((bf16[48,2688]{1,0:T(8,128)(2,1)}, bf16[48,2688]{1,0:T(8,128)(2,1)S(1)}, u32[]{:S(2)}, u32[]{:S(2)}) %collective-permute-start.1) | collective-permute-done | bytes 258080 | tf_op jit(solution)/shard_map/ppermute | solution.py:531
  16.1 0.0 copy-done
  16.1 0.0 copy-start.1
  16.1 0.7 copy-done.1
  16.8 2.7 %adjoint_border.1 = (bf16[416,768]{1,0:T(8,128)(2,1)}, bf16[416,768]{1,0:T(8,128)(2,1)}) custom-call(f32[16,128]{1,0:T(8,128)} %kappa.5, bf16[48,2688]{1,0:T(8,128)(2,1)} %copy-done, bf16[48,2688]{1,0:T(8,128)(2,1)} %copy-done.1, bf16[48,2688]{1,0:T(8,128)(2,1)} %copy-done, bf16[48,2688]{1,0:T(8,128)(2,1)} %copy-done.1, bf16[16,128,768]{2,1,0:T(8,128)(2,1)} %adj.1, ...), custom_call_target="tpu_custom_call" | custom-call | tf_op jit(solution)/shard_map/adjoint_border/pallas_call | solution.py:166
  19.5 3.5 %collective-permute-start.4 = (bf16[416,768]{1,0:T(8,128)(2,1)}, bf16[416,768]{1,0:T(8,128)(2,1)S(1)}, u32[]{:S(2)}, u32[]{:S(2)}) collective-permute-start(bf16[416,768]{1,0:T(8,128)(2,1)} %get-tuple-element.21), channel_id=1, source_target_pairs={{0,4},{4,8},{8,12},{12,16},{16,20},{20,24},{24,28},{28,32},{32,36}... | collective-permute-start | bytes 1916936 | tf_op jit(solution)/shard_map/ppermute | solution.py:531
  23.0 6.6 %collective-permute-start.5 = (bf16[416,768]{1,0:T(8,128)(2,1)}, bf16[416,768]{1,0:T(8,128)(2,1)S(1)}, u32[]{:S(2)}, u32[]{:S(2)}) collective-permute-start(bf16[416,768]{1,0:T(8,128)(2,1)} %get-tuple-element.22), channel_id=1, source_target_pairs={{4,0},{8,4},{12,8},{16,12},{20,16},{24,20},{28,24},{32,28},{36,32}... | collective-permute-start | bytes 1916936 | tf_op jit(solution)/shard_map/ppermute | solution.py:531
  29.7 17.4 %forward.1 = (bf16[2048,2048]{1,0:T(8,128)(2,1)}, bf16[2048,128]{1,0:T(8,128)(2,1)}, bf16[96,128]{1,0:T(8,128)(2,1)}) custom-call(bf16[16,128,768]{2,1,0:T(8,128)(2,1)} %state.1, bf16[16,128,768]{2,1,0:T(8,128)(2,1)} %pert.3, bf16[2048,128]{1,0:T(8,128)(2,1)} %get-tuple-element.14.mask, bf16[48,2688]{1,0:T(8,128)(2,1)} %copy-done, ...), custom_call_target="tpu_custom_call" | custom-call | tf_op jit(solution)/shard_map/forward/pallas_call | solution.py:286
  47.1 2.7 %tangent_border.1 = (bf16[400,768]{1,0:T(8,128)(2,1)}, bf16[400,768]{1,0:T(8,128)(2,1)}) custom-call(bf16[48,2688]{1,0:T(8,128)(2,1)} %copy-done, bf16[48,2688]{1,0:T(8,128)(2,1)} %copy-done.1, bf16[96,128]{1,0:T(8,128)(2,1)} %get-tuple-element.18.moved_s, bf16[16,128,768]{2,1,0:T(8,128)(2,1)} %pert.3, bf16[16,128,768]{2,1,0:T(8,128)(2,1)} %pert.3, ...), custom_call_target="tpu_custom_call" | custom-call | tf_op jit(solution)/shard_map/tangent_border/pallas_call | solution.py:212
  49.8 1.9 %collective-permute-start.2 = (bf16[400,768]{1,0:T(8,128)(2,1)}, bf16[400,768]{1,0:T(8,128)(2,1)S(1)}, u32[]{:S(2)}, u32[]{:S(2)}) collective-permute-start(bf16[400,768]{1,0:T(8,128)(2,1)} %get-tuple-element.19), channel_id=1, source_target_pairs={{0,4},{4,8},{8,12},{12,16},{16,20},{20,24},{24,28},{28,32},{32,36}... | collective-permute-start | bytes 1843208 | tf_op jit(solution)/shard_map/ppermute | solution.py:531
  51.8 7.9 %collective-permute-start.3 = (bf16[400,768]{1,0:T(8,128)(2,1)}, bf16[400,768]{1,0:T(8,128)(2,1)S(1)}, u32[]{:S(2)}, u32[]{:S(2)}) collective-permute-start(bf16[400,768]{1,0:T(8,128)(2,1)} %get-tuple-element.20), channel_id=1, source_target_pairs={{4,0},{8,4},{12,8},{16,12},{20,16},{24,20},{28,24},{32,28},{36,32}... | collective-permute-start | bytes 1843208 | tf_op jit(solution)/shard_map/ppermute | solution.py:531
  59.6 0.0 collective-permute-done.4.above.k_above
  59.6 0.0 copy-start.2
  59.7 0.0 collective-permute-done.5.below.k_below
  59.7 0.0 copy-start.3
  59.7 0.8 copy-done.2
  60.5 0.2 copy-done.3
  60.7 25.5 %adjoint.1 = (f32[3168,128]{1,0:T(8,128)}, f32[2048,768]{1,0:T(8,128)}) custom-call(bf16[16,128,768]{2,1,0:T(8,128)(2,1)} %adj.1, bf16[416,768]{1,0:T(8,128)(2,1)} %copy-done.2, bf16[416,768]{1,0:T(8,128)(2,1)} %copy-done.3, bf16[48,2688]{1,0:T(8,128)(2,1)} %copy-done, bf16[48,2688]{1,0:T(8,128)(2,1)} %copy-done.1, bf16[352,128]{1,0:T(8,128)(2,1)} %constant.2.clone.picks, ...), custom_call_target="tpu_custom_call" | custom-call | tf_op jit(solution)/shard_map/adjoint/pallas_call | solution.py:451
  86.2 0.0 collective-permute-done.2.above
  86.2 0.0 copy-start.4
  86.2 0.0 collective-permute-done.3.below
  86.2 0.0 copy-start.5
  86.2 0.8 copy-done.4
  87.0 0.2 copy-done.5
  87.2 12.0 %tangent.1 = f32[16,128,768]{2,1,0:T(8,128)} custom-call(bf16[16,128,768]{2,1,0:T(8,128)(2,1)} %pert.3, bf16[2048,128]{1,0:T(8,128)(2,1)} %get-tuple-element.17.moved_t.moved_b.moved, bf16[400,768]{1,0:T(8,128)(2,1)} %copy-done.4, bf16[400,768]{1,0:T(8,128)(2,1)} %copy-done.5, bf16[48,2688]{1,0:T(8,128)(2,1)} %copy-done, bf16[48,2688]{1,0:T(8,128)(2,1)} %copy-done.1, ...), custom_call_target="tpu_custom_call" | custom-call | tf_op jit(solution)/shard_map/tangent/pallas_call | solution.py:513
Async XLA Ops:
  4.5 7.3 %collective-permute-start = (bf16[48,2688]{1,0:T(8,128)(2,1)}, bf16[48,2688]{1,0:T(8,128)(2,1)S(1)}, u32[]{:S(2)}, u32[]{:S(2)}) collective-permute-start(bf16[48,2688]{1,0:T(8,128)(2,1)} %get-tuple-element.15), channel_id=1, source_target_pairs={{0,1},{1,2},{2,3},{4,5},{5,6},{6,7},{8,9},{9,10},{10,11},{12,13},{... | collective-permute-start | bytes 774152 | tf_op jit(solution)/shard_map/ppermute | solution.py:531
  8.2 7.9 %collective-permute-start.1 = (bf16[48,2688]{1,0:T(8,128)(2,1)}, bf16[48,2688]{1,0:T(8,128)(2,1)S(1)}, u32[]{:S(2)}, u32[]{:S(2)}) collective-permute-start(bf16[48,2688]{1,0:T(8,128)(2,1)} %get-tuple-element.16), channel_id=1, source_target_pairs={{1,0},{2,1},{3,2},{5,4},{6,5},{7,6},{9,8},{10,9},{11,10},{13,12},{... | collective-permute-start | bytes 774152 | tf_op jit(solution)/shard_map/ppermute | solution.py:531
  11.8 4.3 %copy-start = (bf16[48,2688]{1,0:T(8,128)(2,1)}, bf16[48,2688]{1,0:T(8,128)(2,1)S(1)}, u32[]{:S(2)}) copy-start(bf16[48,2688]{1,0:T(8,128)(2,1)S(1)} %collective-permute-done.s_l.p_l.aux_l.strip_l) | copy-start | bytes 774148
  16.1 0.7 copy-start.1
  19.5 40.1 %collective-permute-start.4 = (bf16[416,768]{1,0:T(8,128)(2,1)}, bf16[416,768]{1,0:T(8,128)(2,1)S(1)}, u32[]{:S(2)}, u32[]{:S(2)}) collective-permute-start(bf16[416,768]{1,0:T(8,128)(2,1)} %get-tuple-element.21), channel_id=1, source_target_pairs={{0,4},{4,8},{8,12},{12,16},{16,20},{20,24},{24,28},{28,32},{32,36}... | collective-permute-start | bytes 1916936 | tf_op jit(solution)/shard_map/ppermute | solution.py:531
  23.0 36.6 %collective-permute-start.5 = (bf16[416,768]{1,0:T(8,128)(2,1)}, bf16[416,768]{1,0:T(8,128)(2,1)S(1)}, u32[]{:S(2)}, u32[]{:S(2)}) collective-permute-start(bf16[416,768]{1,0:T(8,128)(2,1)} %get-tuple-element.22), channel_id=1, source_target_pairs={{4,0},{8,4},{12,8},{16,12},{20,16},{24,20},{28,24},{32,28},{36,32}... | collective-permute-start | bytes 1916936 | tf_op jit(solution)/shard_map/ppermute | solution.py:531
  49.8 36.3 %collective-permute-start.2 = (bf16[400,768]{1,0:T(8,128)(2,1)}, bf16[400,768]{1,0:T(8,128)(2,1)S(1)}, u32[]{:S(2)}, u32[]{:S(2)}) collective-permute-start(bf16[400,768]{1,0:T(8,128)(2,1)} %get-tuple-element.19), channel_id=1, source_target_pairs={{0,4},{4,8},{8,12},{12,16},{16,20},{20,24},{24,28},{28,32},{32,36}... | collective-permute-start | bytes 1843208 | tf_op jit(solution)/shard_map/ppermute | solution.py:531
  51.8 34.4 %collective-permute-start.3 = (bf16[400,768]{1,0:T(8,128)(2,1)}, bf16[400,768]{1,0:T(8,128)(2,1)S(1)}, u32[]{:S(2)}, u32[]{:S(2)}) collective-permute-start(bf16[400,768]{1,0:T(8,128)(2,1)} %get-tuple-element.20), channel_id=1, source_target_pairs={{4,0},{8,4},{12,8},{16,12},{20,16},{24,20},{28,24},{32,28},{36,32}... | collective-permute-start | bytes 1843208 | tf_op jit(solution)/shard_map/ppermute | solution.py:531
  59.6 0.9 copy-start.2
  59.7 1.0 %copy-start.3 = (bf16[416,768]{1,0:T(8,128)(2,1)}, bf16[416,768]{1,0:T(8,128)(2,1)S(1)}, u32[]{:S(2)}) copy-start(bf16[416,768]{1,0:T(8,128)(2,1)S(1)} %collective-permute-done.5.below.k_below) | copy-start | bytes 1916932
  86.2 0.8 copy-start.4
  86.2 1.0 %copy-start.5 = (bf16[400,768]{1,0:T(8,128)(2,1)}, bf16[400,768]{1,0:T(8,128)(2,1)S(1)}, u32[]{:S(2)}) copy-start(bf16[400,768]{1,0:T(8,128)(2,1)S(1)} %collective-permute-done.3.below) | copy-start | bytes 1843204

commit v2 on v1

v2 whole, which is shorter than its diff:
```python
import functools

import jax
import jax.numpy as jnp
import numpy as np
from jax import lax
from jax.experimental import pallas as pl
from jax.experimental.pallas import tpu as pltpu
from jax.sharding import PartitionSpec as P

PHYS_STEP = 4.0
REACH = 3
LANES = 128
SIDE = 8
CORNERS = 16
F32 = jnp.float32
BF16 = jnp.bfloat16
EARLY = 1


def _params(mib):
    return pltpu.CompilerParams(
        dimension_semantics=("arbitrary",), vmem_limit_bytes=mib * 1024 * 1024
    )


def _held():
    return pl.BlockSpec(memory_space=pltpu.VMEM)


def _dot(a, b):
    return jnp.dot(a, b, preferred_element_type=F32)


def _dot_t(a, b):
    return lax.dot_general(a, b, (((1,), (1,)), ((), ())), preferred_element_type=F32)


def _pick(shape, targets):
    row = lax.broadcasted_iota(jnp.int32, shape, 0)
    col = lax.broadcasted_iota(jnp.int32, shape, 1)
    hit = jnp.zeros(shape, jnp.bool_)
    for k, c in targets:
        hit = hit | ((row == k) & (col == c))
    return hit.astype(F32).astype(BF16)


def _split(value):
    hi = value.astype(BF16)
    return hi, (value - hi.astype(F32)).astype(BF16)


def edge_kernel(
    counts, listed_hbm, kappa_hbm, state, pert, adj, left, right, mask_out,
    listed, kappa, near, far, sems,
):
    size_x, size_y = kappa.shape
    width = near.shape[2]
    channels = near.shape[3]
    copies = [
        pltpu.make_async_copy(listed_hbm, listed, sems.at[0]),
        pltpu.make_async_copy(kappa_hbm, kappa, sems.at[1]),
    ]
    for n, field in enumerate((state, pert, adj)):
        low, high = pl.ds(0, width), pl.ds(size_y - width, width)
        copies.append(pltpu.make_async_copy(field.at[:, low], near.at[n], sems.at[2 + 2 * n]))
        copies.append(pltpu.make_async_copy(field.at[:, high], far.at[n], sems.at[3 + 2 * n]))
    for copy in copies:
        copy.start()
    copies[0].wait()
    copies[1].wait()
    count = counts[0, 0]
    index = listed[...]
    cap = index.shape[1]
    shift = size_y.bit_length() - 1
    pos = lax.broadcasted_iota(jnp.int32, (size_x, cap), 1)
    sub = lax.broadcasted_iota(jnp.int32, (size_x, cap), 0)
    rows = ((sub == (index >> shift)) & (pos < count)).astype(F32).astype(BF16)
    sub_y = lax.broadcasted_iota(jnp.int32, (size_y, cap), 0)
    cols = (sub_y == (index & (size_y - 1))).astype(F32).astype(BF16)
    mask = _dot_t(rows, cols)
    mask_t = _dot_t(cols, rows)
    for x in range(size_x):
        mask_out[x * size_y : (x + 1) * size_y, :] = jnp.broadcast_to(
            mask_t[:, x : x + 1], (size_y, LANES)
        ).astype(BF16)
    k_all = kappa[...]
    shape = (REACH * size_x, size_x * width)
    row = lax.broadcasted_iota(jnp.int32, shape, 0)
    col = lax.broadcasted_iota(jnp.int32, shape, 1)
    want = (row % size_x) * width + row // size_x
    for copy in copies[2:]:
        copy.wait()
    for msg, blocks, first in ((left, near, 0), (right, far, size_y - REACH)):
        pick = (col == want + first % width).astype(F32).astype(BF16)
        for n in range(3):
            msg[:, n * channels : (n + 1) * channels] = _dot(
                pick, blocks[n].reshape(size_x * width, channels)
            ).astype(BF16)
        at = 3 * channels
        for j in range(REACH):
            here = slice(j * size_x, (j + 1) * size_x)
            y = first + j
            hi, lo = _split(jnp.broadcast_to(k_all[:, y : y + 1], (size_x, LANES)))
            msg[here, at : at + LANES] = jnp.broadcast_to(
                mask[:, y : y + 1], (size_x, LANES)
            ).astype(BF16)
            msg[here, at + LANES : at + 2 * LANES] = hi
            msg[here, at + 2 * LANES : at + 3 * LANES] = lo


def make_edges(counts, listed, kappa, state, pert, adj):
    size_x, size_y, channels = state.shape
    width = 16
    strip = jax.ShapeDtypeStruct((REACH * size_x, 3 * channels + 3 * LANES), BF16)
    far = pl.BlockSpec(memory_space=pltpu.HBM)
    return pl.pallas_call(
        edge_kernel,
        in_specs=[pl.BlockSpec(memory_space=pltpu.SMEM)] + [far] * 5,
        out_specs=[_held()] * 3,
        out_shape=[strip, strip, jax.ShapeDtypeStruct((size_x * size_y, LANES), BF16)],
        scratch_shapes=[
            pltpu.VMEM(listed.shape, jnp.int32),
            pltpu.VMEM(kappa.shape, F32),
            pltpu.VMEM((3, size_x, width, channels), BF16),
            pltpu.VMEM((3, size_x, width, channels), BF16),
            pltpu.SemaphoreType.DMA((8,)),
        ],
        compiler_params=pltpu.CompilerParams(vmem_limit_bytes=12 * 1024 * 1024),
        name="edges",
    )(counts, *[pltpu.with_memory_space_constraint(a, pltpu.HBM) for a in (listed, kappa, state, pert, adj)])


def _corner_picks(size_x, top):
    near, next_ = (0, 1) if top else (size_x - 1, size_x - 2)
    left = [(0, 2 * size_x + near), (1, size_x + near), (2, 2 * size_x + next_)]
    right = [(3, near), (4, size_x + near), (5, next_)]
    shape = (CORNERS, REACH * size_x)
    return _pick(shape, left), _pick(shape, right)


def _kappa_wide(kappa, aux_l, aux_r):
    size_x, size_y = kappa.shape
    wide = jnp.concatenate([kappa[...], jnp.zeros((size_x, LANES), F32)], axis=1)
    lane = lax.broadcasted_iota(jnp.int32, wide.shape, 1)
    for aux, first in ((aux_l, wide.shape[1] - REACH), (aux_r, size_y)):
        for j in range(REACH):
            here = slice(j * size_x, (j + 1) * size_x)
            value = aux[here, LANES : 2 * LANES].astype(F32) + aux[
                here, 2 * LANES : 3 * LANES
            ].astype(F32)
            wide = jnp.where(lane == first + j, jnp.concatenate([value, value], axis=1), wide)
    return wide


def border_kernel(kappa, from_l, from_r, adj_t, adj_b, pert_t, pert_b, top, bot):
    size_x, size_y = kappa.shape
    channels = adj_t.shape[2]
    body = REACH * size_y
    early = EARLY * LANES
    aux = 3 * channels
    hi, lo = _split(_kappa_wide(kappa, from_l[:, aux:], from_r[:, aux:]))
    extra = jnp.zeros((size_x, channels + early - 2 * hi.shape[1]), BF16)
    for msg, adj, pert, is_top in ((top, adj_t, pert_t, True), (bot, adj_b, pert_b, False)):
        first = 0 if is_top else adj.shape[0] - REACH
        msg[0:body, :channels] = adj[first : first + REACH].reshape(body, channels)
        msg[0:body, channels:] = pert[
            first : first + REACH, :, LANES : LANES + early
        ].reshape(body, early)
        pick_l, pick_r = _corner_picks(size_x, is_top)
        here = slice(body, body + CORNERS)
        msg[here, :channels] = (
            _dot(pick_l, from_l[:, 2 * channels : aux])
            + _dot(pick_r, from_r[:, 2 * channels : aux])
        ).astype(BF16)
        lanes = slice(channels + LANES, channels + LANES + early)
        msg[here, channels:] = (
            _dot(pick_l, from_l[:, lanes]) + _dot(pick_r, from_r[:, lanes])
        ).astype(BF16)
        msg[body + CORNERS :, :] = jnp.concatenate([hi, lo, extra], axis=1)


def first_border(kappa, from_l, from_r, adj, pert):
    size_x, size_y, channels = adj.shape
    block = 4
    last = size_x // block - 1
    whole = lambda a: pl.BlockSpec(a.shape, lambda i: (0,) * a.ndim)
    low = pl.BlockSpec((block, size_y, channels), lambda i: (0, 0, 0))
    high = pl.BlockSpec((block, size_y, channels), lambda i: (last, 0, 0))
    shape = (REACH * size_y + CORNERS + size_x, channels + EARLY * LANES)
    out = jax.ShapeDtypeStruct(shape, BF16)
    return pl.pallas_call(
        border_kernel,
        grid=(1,),
        in_specs=[whole(kappa), whole(from_l), whole(from_r), low, high, low, high],
        out_specs=[whole(out)] * 2,
        out_shape=[out, out],
        compiler_params=_params(12),
        name="first_border",
    )(kappa, from_l, from_r, adj, adj, pert, pert)


def late_border_kernel(from_l, from_r, moved_s, pert_t, pert_b, moved_t, moved_b, top, bot):
    size_y, channels = pert_t.shape[1:]
    size_x = moved_s.shape[0] // (2 * REACH)
    body = REACH * size_y
    cut = REACH * size_x
    lanes = slice((1 + EARLY) * LANES, channels)
    side = slice(channels + lanes.start, 2 * channels)
    for msg, pert, moved, is_top in (
        (top, pert_t, moved_t, True),
        (bot, pert_b, moved_b, False),
    ):
        first = 0 if is_top else pert.shape[0] - REACH
        msg[0:body, :LANES] = moved[first * size_y : (first + REACH) * size_y]
        msg[0:body, LANES:] = pert[first : first + REACH, :, lanes].reshape(
            body, channels - lanes.start
        )
        pick_l, pick_r = _corner_picks(size_x, is_top)
        msg[body:, :LANES] = (
            _dot(pick_l, moved_s[:cut]) + _dot(pick_r, moved_s[cut:])
        ).astype(BF16)
        msg[body:, LANES:] = (_dot(pick_l, from_l[:, side]) + _dot(pick_r, from_r[:, side])).astype(
            BF16
        )


def late_border(from_l, from_r, moved_s, pert, moved_a, moved_b):
    size_x, size_y, channels = pert.shape
    block = 4
    last = size_x // block - 1
    end = moved_b.shape[0] // (block * size_y) - 1
    whole = lambda a: pl.BlockSpec(a.shape, lambda i: (0,) * a.ndim)
    out = jax.ShapeDtypeStruct(
        (REACH * size_y + CORNERS, channels - EARLY * LANES), BF16
    )
    return pl.pallas_call(
        late_border_kernel,
        grid=(1,),
        in_specs=[
            whole(from_l), whole(from_r), whole(moved_s),
            pl.BlockSpec((block, size_y, channels), lambda i: (0, 0, 0)),
            pl.BlockSpec((block, size_y, channels), lambda i: (last, 0, 0)),
            pl.BlockSpec((block * size_y, LANES), lambda i: (0, 0)),
            pl.BlockSpec((block * size_y, LANES), lambda i: (end, 0)),
        ],
        out_specs=[whole(out)] * 2,
        out_shape=[out, out],
        compiler_params=_params(12),
        name="late_border",
    )(from_l, from_r, moved_s, pert, pert, moved_a, moved_b)


def _forward(pairs, w_in, w_mid, w_out, biases, keep):
    pairs = list(pairs)
    for layer in range(1 + w_mid.shape[0]):
        weights = w_in[...] if layer == 0 else w_mid[layer - 1]
        bias = biases[layer : layer + 1, :]
        for n, (h, t) in enumerate(pairs):
            rows = h.shape[0]
            both = _dot(jnp.concatenate([h, t], axis=0), weights)
            v = jnp.tanh(both[:rows] + bias)
            slope = 1.0 - v * v
            pairs[n] = (v.astype(BF16), (slope * both[rows:]).astype(BF16))
            keep(n, layer, slope)
    return [_dot(t, w_out[...]) for _, t in pairs]


def forward_kernel(first, strips, rows, chunks, *refs):
    if strips:
        (state, pert, mask, from_l, from_r, w_in, w_mid, w_out, biases,
         slopes, moved, moved_s, side_x, side_d, side_m) = refs
    else:
        state, pert, mask, w_in, w_mid, w_out, biases, slopes, moved = refs
    step = pl.program_id(0)
    _, size_y, channels = state.shape
    units = biases.shape[1]
    xs = rows // size_y
    if strips:
        cut = from_l.shape[0]
        each = 2 * cut // pl.num_programs(0)

        @pl.when(step == 0)
        def _():
            for n, msg in enumerate((from_l, from_r)):
                here = slice(n * cut, (n + 1) * cut)
                side_x[here, :] = msg[:, :channels]
                side_d[here, :] = msg[:, channels : 2 * channels]
                side_m[here, :] = msg[:, 3 * channels : 3 * channels + LANES]

        beside = pl.ds(pl.multiple_of(step * each, each), each)
    x_here = pl.ds(first + step * xs, xs)
    x = state[x_here].reshape(rows, channels)
    d = pert[x_here].reshape(rows, channels)
    part = rows // chunks
    pairs = [(x[n * part : (n + 1) * part], d[n * part : (n + 1) * part]) for n in range(chunks)]
    if strips:
        h, t = pairs[-1]
        pairs[-1] = (
            jnp.concatenate([h, side_x[beside, :]], axis=0),
            jnp.concatenate([t, side_d[beside, :]], axis=0),
        )

    def at(n):
        return pl.ds(pl.multiple_of(step * rows + n * part, part), part)

    def keep(n, layer, slope):
        slopes[at(n), layer * units : (layer + 1) * units] = slope[:part].astype(BF16)

    jac = _forward(pairs, w_in, w_mid, w_out, biases, keep)

    def shift(live, value, base):
        return (base.astype(F32) + PHYS_STEP * live.astype(F32) * value).astype(BF16)

    for n in range(chunks):
        here = pl.ds(pl.multiple_of((first + step * xs) * size_y + n * part, part), part)
        base = d[n * part : (n + 1) * part, :LANES]
        moved[at(n), :] = shift(mask[here, :], jac[n][:part], base)
    if strips:
        moved_s[beside, :] = shift(side_m[beside, :], jac[-1][part:], side_d[beside, :LANES])


def forward(first, count, state, pert, mask, sides, weights):
    _, size_y, channels = state.shape
    xs = 4
    rows = xs * size_y
    layers, units = weights[3].shape
    columns = count * size_y
    args = (state, pert, mask) + sides + weights
    out = [
        jax.ShapeDtypeStruct((columns, layers * units), BF16),
        jax.ShapeDtypeStruct((columns, LANES), BF16),
    ]
    scratch = []
    if sides:
        beside = 2 * sides[0].shape[0]
        out.append(jax.ShapeDtypeStruct((beside, LANES), BF16))
        scratch = [
            pltpu.VMEM((beside, channels), BF16),
            pltpu.VMEM((beside, channels), BF16),
            pltpu.VMEM((beside, LANES), BF16),
        ]
    return pl.pallas_call(
        functools.partial(forward_kernel, first, bool(sides), rows, 2),
        grid=(count // xs,),
        in_specs=[_held()] * len(args),
        out_specs=[_held()] * len(out),
        out_shape=out,
        scratch_shapes=scratch,
        compiler_params=_params(14),
        name="forward_rest" if sides else "forward_part",
    )(*args)


def _side_picks(size_x):
    frame = size_x + 2 * REACH
    strips = REACH * size_x
    picks = np.zeros((2, frame * SIDE, LANES), np.float32)
    for x in range(size_x):
        for j in range(REACH):
            picks[0, (x + REACH) * SIDE + SIDE - REACH + j, j * size_x + x] = 1
            picks[1, (x + REACH) * SIDE + j, j * size_x + x] = 1
    for base, step, near in ((strips, -1, REACH - 1), (strips + CORNERS, 1, REACH + size_x)):
        for k, (dx, dy) in enumerate(((0, 0), (0, 1), (1, 0))):
            picks[0, (near + step * dx) * SIDE + SIDE - 1 - dy, base + k] = 1
            picks[1, (near + step * dx) * SIDE + dy, base + 3 + k] = 1
    return jnp.asarray(picks.reshape(2 * frame * SIDE, LANES), BF16)


def _place_sides(out, picks, strip_l, strip_r, ends):
    half = out.shape[0] // 2
    spare = LANES - strip_l.shape[0] - sum(e.shape[0] for e in ends)
    ends = list(ends) + [jnp.zeros((spare, out.shape[1]), BF16)]
    out[:half, :] = _dot(picks[:half, :], jnp.concatenate([strip_l] + ends, axis=0))
    out[half:, :] = _dot(picks[half:, :], jnp.concatenate([strip_r] + ends, axis=0))


def _fill(frame, own, above, below, sides, lanes, size_x, size_y, scale=None):
    row = size_y + 2 * SIDE
    count = size_x + 2 * REACH
    half = count * SIDE

    def put(at, value):
        here = slice(at, at + value.shape[0])
        frame[here, :] = value if scale is None else value * scale[here, :]

    for r in range(count):
        at = r * row
        put(at, sides[r * SIDE : (r + 1) * SIDE, lanes])
        put(at + SIDE + size_y, sides[half + r * SIDE : half + (r + 1) * SIDE, lanes])
        if r < REACH:
            value = above(slice(r * size_y, (r + 1) * size_y))
        elif r < REACH + size_x:
            value = own(r - REACH)
        else:
            k = r - REACH - size_x
            value = below(slice(k * size_y, (k + 1) * size_y))
        put(at + SIDE, value.astype(F32))


def _transport(ping, pong, kap, size_x, size_y, emit):
    row = size_y + 2 * SIDE
    count = size_x + 2 * REACH
    src, dst = ping, pong
    for step in range(1, REACH + 1):
        last = step == REACH
        start, stop = (SIDE, SIDE + size_y) if last else (0, row)
        size = (stop - start) // 2
        for lo in range(start, stop, size):
            at = step * row + lo
            prev = src[at - row : at - row + size, :]
            mid = src[at : at + size, :]
            for r in range(step, count - step):
                at = r * row + lo
                following = src[at + row : at + row + size, :]
                near = (prev + following) + (
                    src[at - 1 : at - 1 + size, :] + src[at + 1 : at + 1 + size, :]
                )
                value = mid + kap[at : at + size, :] * (near - 4.0 * mid)
                if last:
                    emit(r - REACH, lo - SIDE, size, value)
                else:
                    dst[at : at + size, :] = value
                prev, mid = mid, following
        src, dst = dst, src


def _kappa_frame(kappa, aux_l, aux_r, above, below, natural, out):
    size_x, size_y = kappa.shape
    row = size_y + 2 * SIDE
    natural[...] = jnp.zeros(natural.shape, F32)
    wide = 2 * LANES
    natural[REACH : REACH + size_x, :] = _kappa_wide(kappa, aux_l, aux_r)
    up = above[:, :wide].astype(F32) + above[:, wide : 2 * wide].astype(F32)
    down = below[:, :wide].astype(F32) + below[:, wide : 2 * wide].astype(F32)
    natural[0:REACH, :] = up[size_x - REACH :]
    natural[REACH + size_x : 2 * REACH + size_x, :] = down[:REACH]
    own = natural[:, :LANES].T
    rest = natural[:, LANES:].T
    for r in range(size_x + 2 * REACH):
        at = r * row
        put = lambda a: jnp.broadcast_to(a[:, r : r + 1], (a.shape[0], LANES))
        out[at : at + SIDE, :] = put(rest[LANES - SIDE :])
        out[at + SIDE : at + SIDE + size_y, :] = put(own)
        out[at + SIDE + size_y : at + row, :] = put(rest[:SIDE])


def _lanes(group):
    return pl.ds(pl.multiple_of(group * LANES, LANES), LANES)


def adjoint_kernel(
    adj, above, below, from_l, from_r, picks, kappa, mask, slopes_a, slopes_b, w_in, w_mid, w_out,
    kap, out, ping, pong, natural, inverse, moved, sides,
):
    step = pl.program_id(0)
    groups = moved.shape[0]
    size_x, size_y = kappa.shape
    channels = adj.shape[2]
    row = size_y + 2 * SIDE
    body = REACH * size_y
    aux = 3 * channels

    @pl.when(step == 0)
    def _():
        k_rows = slice(body + CORNERS, body + CORNERS + size_x)
        _kappa_frame(
            kappa, from_l[:, aux:], from_r[:, aux:], above[k_rows, :], below[k_rows, :], natural, kap
        )
        for x in range(size_x):
            at = (x + REACH) * row + SIDE
            inverse[x * size_y : (x + 1) * size_y, :] = 1.0 / kap[at : at + size_y, :]
        ends = [m[body : body + CORNERS, :channels] for m in (above, below)]
        strip = slice(2 * channels, aux)
        _place_sides(sides, picks, from_l[:, strip], from_r[:, strip], ends)

    @pl.when(step < groups)
    def _():
        lanes = _lanes(step)
        _fill(
            ping, lambda x: adj[x, :, lanes], lambda r: above[r, lanes], lambda r: below[r, lanes],
            sides, lanes, size_x, size_y, kap,
        )

        def emit(x, lo, size, value):
            here = slice(x * size_y + lo, x * size_y + lo + size)
            moved[step, here, :] = value * inverse[here, :]

        _transport(ping, pong, kap, size_x, size_y, emit)

    rows = out.shape[0]
    units = w_in.shape[1]

    def back(slopes, block, base):
        here = pl.ds(pl.multiple_of(block * rows, rows), rows)
        kept = pl.ds(pl.multiple_of((block - base) * rows, rows), rows)
        upstream = (PHYS_STEP * mask[here, :].astype(F32) * moved[0, here, :]).astype(BF16)
        half = rows // 2
        parts = [_dot_t(upstream[n * half : (n + 1) * half], w_out[...]) for n in range(2)]
        for layer in reversed(range(1 + w_mid.shape[0])):
            weights = w_in[...] if layer == 0 else w_mid[layer - 1]
            slope = slopes[kept, layer * units : (layer + 1) * units]
            for n in range(2):
                part = slope[n * half : (n + 1) * half].astype(F32)
                parts[n] = _dot_t((parts[n] * part).astype(BF16), weights)
        for n in range(2):
            at = pl.ds(pl.multiple_of(block * rows + n * half, half), half)
            for g in range(groups):
                lanes = slice(g * LANES, (g + 1) * LANES)
                out[n * half : (n + 1) * half, lanes] = moved[g, at, :] + parts[n][:, lanes]

    split = slopes_a.shape[0] // rows

    @pl.when((step >= groups) & (step < groups + split))
    def _():
        back(slopes_a, step - groups, 0)

    @pl.when(step >= groups + split)
    def _():
        back(slopes_b, step - groups, split)


def adjoint_all(adj, above, below, from_l, from_r, kappa, mask, slopes_a, slopes_b, weights):
    size_x, size_y, channels = adj.shape
    columns = size_x * size_y
    groups = channels // LANES
    blocks = 4
    rows = columns // blocks
    frame = (size_x + 2 * REACH) * (size_y + 2 * SIDE)
    picks = _side_picks(size_x)
    args = (adj, above, below, from_l, from_r, picks, kappa, mask, slopes_a, slopes_b) + weights
    return pl.pallas_call(
        adjoint_kernel,
        grid=(groups + blocks,),
        in_specs=[_held()] * len(args),
        out_specs=[
            _held(),
            pl.BlockSpec((rows, channels), lambda i: (jnp.maximum(i - groups, 0), 0)),
        ],
        out_shape=[
            jax.ShapeDtypeStruct((frame, LANES), F32),
            jax.ShapeDtypeStruct((columns, channels), F32),
        ],
        scratch_shapes=[
            pltpu.VMEM((frame, LANES), F32),
            pltpu.VMEM((frame, LANES), F32),
            pltpu.VMEM((LANES, 2 * LANES), F32),
            pltpu.VMEM((columns, LANES), F32),
            pltpu.VMEM((groups, columns, LANES), F32),
            pltpu.VMEM((picks.shape[0], channels), F32),
        ],
        compiler_params=_params(26),
        name="adjoint",
    )(*args)


def tangent_kernel(
    pert, moved_a, moved_b, first_t, first_b, late_t, late_b, from_l, from_r, moved_s, picks, kap,
    out, ping, pong, sides,
):
    step = pl.program_id(0)
    size_x, size_y, _ = out.shape
    channels = pert.shape[2]
    cut = moved_s.shape[0] // 2
    body = REACH * size_y
    early = EARLY * LANES

    @pl.when(step == 0)
    def _():
        ends = [
            jnp.concatenate(
                [
                    late[body : body + CORNERS, :LANES],
                    first[body : body + CORNERS, channels : channels + early],
                    late[body : body + CORNERS, LANES:],
                ],
                axis=1,
            )
            for first, late in ((first_t, late_t), (first_b, late_b))
        ]
        strips = [
            jnp.concatenate(
                [moved_s[n * cut : (n + 1) * cut, :], msg[:, channels + LANES : 2 * channels]], axis=1
            )
            for n, msg in enumerate((from_l, from_r))
        ]
        _place_sides(sides, picks, strips[0], strips[1], ends)
        split = moved_a.shape[0] // size_y

        def own(x):
            source, k = (moved_a, x) if x < split else (moved_b, x - split)
            return source[k * size_y : (k + 1) * size_y, :]

        _fill(
            ping, own, lambda r: late_t[r, :LANES], lambda r: late_b[r, :LANES],
            sides, slice(0, LANES), size_x, size_y,
        )

    def fill(top, bot, lanes):
        here = _lanes(step)
        _fill(
            ping, lambda x: pert[x, :, here], lambda r: top[r, lanes], lambda r: bot[r, lanes],
            sides, here, size_x, size_y,
        )

    @pl.when((step > 0) & (step <= EARLY))
    def _():
        fill(first_t, first_b, _lanes(channels // LANES + step - 1))

    @pl.when(step > EARLY)
    def _():
        fill(late_t, late_b, _lanes(step - EARLY))

    def emit(x, lo, size, value):
        out[x, lo : lo + size, :] = value

    _transport(ping, pong, kap, size_x, size_y, emit)


def tangent_all(pert, moved_a, moved_b, first, late, from_l, from_r, moved_s, kap):
    size_x, size_y, channels = pert.shape
    picks = _side_picks(size_x)
    args = (pert, moved_a, moved_b) + first + late + (from_l, from_r, moved_s, picks, kap)
    return pl.pallas_call(
        tangent_kernel,
        grid=(channels // LANES,),
        in_specs=[_held()] * len(args),
        out_specs=pl.BlockSpec((size_x, size_y, LANES), lambda i: (0, 0, i)),
        out_shape=jax.ShapeDtypeStruct((size_x, size_y, channels), F32),
        scratch_shapes=[
            pltpu.VMEM(kap.shape, F32),
            pltpu.VMEM(kap.shape, F32),
            pltpu.VMEM((picks.shape[0], channels), F32),
        ],
        compiler_params=_params(12),
        name="tangent",
    )(*args)


def _shift(value, axis, way):
    ends = lax.axis_size(axis) - 1
    pairs = [(i, i + 1) if way > 0 else (i + 1, i) for i in range(ends)]
    return lax.ppermute(value, axis, pairs)


def per_device(
    state, perturbation, adjoint_end, kappa, act_list, counts, w_in, w_mid, w_out, biases
):
    size_x, size_y, channels = state.shape
    weights = (w_in, w_mid, w_out)
    nets = weights + (biases,)
    part = 4
    left, right, mask = make_edges(counts, act_list, kappa, state, perturbation, adjoint_end)
    from_l = _shift(right, "face", 1)
    from_r = _shift(left, "face", -1)
    slopes_a, moved_a = forward(0, part, state, perturbation, mask, (), nets)
    from_l, from_r, slopes_a = lax.optimization_barrier((from_l, from_r, slopes_a))
    top, bot = first_border(kappa, from_l, from_r, adjoint_end, perturbation)
    first = (_shift(bot, "elem", 1), _shift(top, "elem", -1))
    slopes_b, moved_b, moved_s = forward(
        part, size_x - part, state, perturbation, mask, (from_l, from_r), nets
    )
    top, bot = late_border(from_l, from_r, moved_s, perturbation, moved_a, moved_b)
    late = (_shift(bot, "elem", 1), _shift(top, "elem", -1))
    kap, ad_out = adjoint_all(
        adjoint_end, first[0], first[1], from_l, from_r, kappa, mask, slopes_a, slopes_b, weights
    )
    tl_out = tangent_all(perturbation, moved_a, moved_b, first, late, from_l, from_r, moved_s, kap)
    return tl_out, ad_out.reshape(size_x, size_y, channels)


def solution(mesh):
    tile = P("elem", "face", None)
    plane = P("elem", "face")
    return jax.shard_map(
        per_device,
        mesh=mesh,
        in_specs=(tile, tile, tile, plane, plane, plane, P(), P(), P(), P()),
        out_specs=(tile, tile),
        check_vma=False,
    )
```

time: 99.9 us -> 68.6 us (0.69)
  Pallas kernels: 63.5 us -> 38 us
  waiting for transfers between devices: 5.94 us -> 2.78 us
  local copies, waits for them, and re-layouts: 2.75 us -> 0.04 us
    pallas_call x6 -> x7, Pallas kernels: 63.5 us -> 38 us  [the longest x1 15.4 us: adjoint_all(): pl.pallas_call(adjoint_kernel, grid=(groups + blocks,), in_specs=[_held()...]
    ppermute x6, waiting for transfers between devices: 5.94 us -> 2.78 us  [_shift(): return lax.ppermute(value, axis, pairs)]
    unnamed x12 -> x18, local copies, waits for them, and re-layouts: 2.75 us -> 0.04 us
  transfers between devices with their start and end apart: 6 -> 6, of which waited for: 2 -> 1; matrix products, arithmetic and copies ran while one was open for 0% -> 0% of each run, Pallas kernels for 46% -> 40%
where the time goes in v2:
time: 68.6 us; the launch traced here: 68.4 us
  Pallas kernels  38 us (55%)
  starting transfers between devices  26.1 us (38%)
  waiting for transfers between devices  2.78 us (4%)
  between operations  1.51 us (2%)
    ppermute x6, starting transfers between devices, _shift(): return lax.ppermute(value, axis, pairs)  26.1 us
    pallas_call x1, Pallas kernels, adjoint_all(): pl.pallas_call(adjoint_kernel, grid=(groups + blocks,), in_specs=[_held()...  15.4 us
    pallas_call x2, Pallas kernels, forward(): pl.pallas_call(functools.partial(forward_kernel, first, bool(sides), rows...  11.9 us
    pallas_call x1, Pallas kernels, tangent_all(): pl.pallas_call(tangent_kernel, grid=(channels // LANES,), in_specs=[_held...  7.79 us
    ppermute x6, waiting for transfers between devices, _shift(): return lax.ppermute(value, axis, pairs)  2.78 us
    pallas_call x1, Pallas kernels, make_edges(): pl.pallas_call(edge_kernel, in_specs=[pl.BlockSpec(memory_space=pltpu.SME...  2.4 us
  transfers between devices with their start and end apart: 6, of which 1 were waited for; matrix products, arithmetic and copies ran while one was open for 0% of the time, Pallas kernels for 40%

profile of v2, /device:TPU:7, one launch (start us, length us, event | category | flops | bytes accessed | tf_op | source)
XLA Modules:
  0.0 68.4 jit_solution(5510245516029768098)
XLA Ops:
  1.3 0.0 copy-start
  1.3 0.0 copy-start.2
  1.3 0.0 copy-start.3
  1.3 0.0 copy-start.4
  1.3 0.0 copy-start.5
  1.3 0.0 copy-start.8
  1.3 2.4 %edges.1 = (bf16[48,2688]{1,0:T(8,128)(2,1)S(1)}, bf16[48,2688]{1,0:T(8,128)(2,1)S(1)}, bf16[2048,128]{1,0:T(8,128)(2,1)S(1)}) custom-call(s32[1,1]{1,0:T(1,128)S(6)} %copy.14.counts, s32[1,1024]{1,0:T(1,128)} %listed_hbm.1, f32[16,128]{1,0:T(8,128)} %kappa.3, bf16[16,128,768]{2,1,0:T(8,128)(2,1)} %refs_0_.3, bf16[16,128,768]{2,1,0:T(8,128)(2,1)} %pert.3, ...), custom_call_target="tpu_custom_call" | custom-call | tf_op jit(solution)/shard_map/edges/pallas_call | solution.py:117
  3.7 4.0 %collective-permute-start = (bf16[48,2688]{1,0:T(8,128)(2,1)S(1)}, bf16[48,2688]{1,0:T(8,128)(2,1)S(1)}, u32[]{:S(2)}, u32[]{:S(2)}) collective-permute-start(bf16[48,2688]{1,0:T(8,128)(2,1)S(1)} %get-tuple-element.21), channel_id=1, source_target_pairs={{0,1},{1,2},{2,3},{4,5},{5,6},{6,7},{8,9},{9,10},{10,11},{12,13},{... | collective-permute-start | bytes 774152 | tf_op jit(solution)/shard_map/ppermute | solution.py:643
  7.8 1.9 %collective-permute-start.1 = (bf16[48,2688]{1,0:T(8,128)(2,1)S(1)}, bf16[48,2688]{1,0:T(8,128)(2,1)S(1)}, u32[]{:S(2)}, u32[]{:S(2)}) collective-permute-start(bf16[48,2688]{1,0:T(8,128)(2,1)S(1)} %get-tuple-element.22), channel_id=1, source_target_pairs={{1,0},{2,1},{3,2},{5,4},{6,5},{7,6},{9,8},{10,9},{11,10},{13,12},{... | collective-permute-start | bytes 774152 | tf_op jit(solution)/shard_map/ppermute | solution.py:643
  9.7 0.0 copy-done
  9.7 0.0 copy-done.2
  9.7 0.0 copy-done.3
  9.7 0.0 copy-done.4
  9.7 0.0 copy-done.5
  9.8 0.0 copy-done.8
  9.8 0.0 copy-start.1
  9.8 0.0 copy-start.7
  9.8 2.9 %forward_part.1 = (bf16[512,2048]{1,0:T(8,128)(2,1)S(1)}, bf16[512,128]{1,0:T(8,128)(2,1)S(1)}) custom-call(bf16[16,128,768]{2,1,0:T(8,128)(2,1)S(1)} %copy-done.2, bf16[16,128,768]{2,1,0:T(8,128)(2,1)S(1)} %copy-done, bf16[2048,128]{1,0:T(8,128)(2,1)S(1)} %get-tuple-element.19.refs_2_.mask, bf16[768,512]{1,0:T(8,128)(2,1)S(1)} %copy-done.4, ...), custom_call_target="tpu_custom_call" | custom-call | tf_op jit(solution)/shard_map/forward_part/pallas_call | solution.py:343
  12.7 0.0 collective-permute-done.refs_3_.from_l
  12.7 2.8 %collective-permute-done.1.refs_4_.from_r = bf16[48,2688]{1,0:T(8,128)(2,1)S(1)} collective-permute-done((bf16[48,2688]{1,0:T(8,128)(2,1)S(1)}, bf16[48,2688]{1,0:T(8,128)(2,1)S(1)}, u32[]{:S(2)}, u32[]{:S(2)}) %collective-permute-start.1) | collective-permute-done | bytes 258080 | tf_op jit(solution)/shard_map/ppermute | solution.py:643
  15.4 0.0 copy-done.1
  15.4 0.0 copy-done.7
  15.4 0.3 first_border.1
  15.7 3.5 %collective-permute-start.2 = (bf16[416,896]{1,0:T(8,128)(2,1)S(1)}, bf16[416,896]{1,0:T(8,128)(2,1)S(1)}, u32[]{:S(2)}, u32[]{:S(2)}) collective-permute-start(bf16[416,896]{1,0:T(8,128)(2,1)S(1)} %get-tuple-element.27), channel_id=1, source_target_pairs={{0,4},{4,8},{8,12},{12,16},{16,20},{20,24},{24,28},{28,32},{32,36}... | collective-permute-start | bytes 2236424 | tf_op jit(solution)/shard_map/ppermute | solution.py:643
  19.3 6.6 %collective-permute-start.3 = (bf16[416,896]{1,0:T(8,128)(2,1)S(1)}, bf16[416,896]{1,0:T(8,128)(2,1)S(1)}, u32[]{:S(2)}, u32[]{:S(2)}) collective-permute-start(bf16[416,896]{1,0:T(8,128)(2,1)S(1)} %get-tuple-element.28), channel_id=1, source_target_pairs={{4,0},{8,4},{12,8},{16,12},{20,16},{24,20},{28,24},{32,28},{36,32}... | collective-permute-start | bytes 2236424 | tf_op jit(solution)/shard_map/ppermute | solution.py:643
  25.9 9.1 %forward_rest.1 = (bf16[1536,2048]{1,0:T(8,128)(2,1)S(1)}, bf16[1536,128]{1,0:T(8,128)(2,1)S(1)}, bf16[96,128]{1,0:T(8,128)(2,1)S(1)}) custom-call(bf16[16,128,768]{2,1,0:T(8,128)(2,1)S(1)} %copy-done.2, bf16[16,128,768]{2,1,0:T(8,128)(2,1)S(1)} %copy-done, bf16[2048,128]{1,0:T(8,128)(2,1)S(1)} %get-tuple-element.19.refs_2_.mask, ...), custom_call_target="tpu_custom_call" | custom-call | tf_op jit(solution)/shard_map/forward_rest/pallas_call | solution.py:343
  35.0 0.0 copy-start.6
  35.0 0.2 late_border.1
  35.2 1.9 %collective-permute-start.4 = (bf16[400,640]{1,0:T(8,128)(2,1)S(1)}, bf16[400,640]{1,0:T(8,128)(2,1)S(1)}, u32[]{:S(2)}, u32[]{:S(2)}) collective-permute-start(bf16[400,640]{1,0:T(8,128)(2,1)S(1)} %get-tuple-element.30), channel_id=1, source_target_pairs={{0,4},{4,8},{8,12},{12,16},{16,20},{20,24},{24,28},{28,32},{32,36}... | collective-permute-start | bytes 1536008 | tf_op jit(solution)/shard_map/ppermute | solution.py:643
  37.1 8.1 %collective-permute-start.5 = (bf16[400,640]{1,0:T(8,128)(2,1)S(1)}, bf16[400,640]{1,0:T(8,128)(2,1)S(1)}, u32[]{:S(2)}, u32[]{:S(2)}) collective-permute-start(bf16[400,640]{1,0:T(8,128)(2,1)S(1)} %get-tuple-element.31), channel_id=1, source_target_pairs={{4,0},{8,4},{12,8},{16,12},{20,16},{24,20},{28,24},{32,28},{36,32}... | collective-permute-start | bytes 1536008 | tf_op jit(solution)/shard_map/ppermute | solution.py:643
  45.2 0.0 collective-permute-done.2.above.first_t
  45.2 0.0 collective-permute-done.3.below.first_b
  45.2 0.0 copy-done.6
  45.2 15.4 %adjoint.1 = (f32[3168,128]{1,0:T(8,128)S(1)}, f32[2048,768]{1,0:T(8,128)}) custom-call(bf16[16,128,768]{2,1,0:T(8,128)(2,1)S(1)} %copy-done.1, bf16[416,896]{1,0:T(8,128)(2,1)S(1)} %collective-permute-done.2.above.first_t, bf16[416,896]{1,0:T(8,128)(2,1)S(1)} %collective-permute-done.3.below.first_b, ...), custom_call_target="tpu_custom_call" | custom-call | tf_op jit(solution)/shard_map/adjoint/pallas_call | solution.py:532
  60.6 0.0 collective-permute-done.4.late_t
  60.6 0.0 collective-permute-done.5.late_b
  60.6 7.8 %tangent.1 = f32[16,128,768]{2,1,0:T(8,128)} custom-call(bf16[16,128,768]{2,1,0:T(8,128)(2,1)S(1)} %copy-done, bf16[512,128]{1,0:T(8,128)(2,1)S(1)} %get-tuple-element.20.moved_t.moved_a, bf16[1536,128]{1,0:T(8,128)(2,1)S(1)} %get-tuple-element.26.moved_b, bf16[416,896]{1,0:T(8,128)(2,1)S(1)} %collective-permute-done.2.above.first_t, ...), custom_call_target="tpu_custom_call" | custom-call | tf_op jit(solution)/shard_map/tangent/pallas_call | solution.py:624
Async XLA Ops:
  1.3 8.4 %copy-start = (bf16[16,128,768]{2,1,0:T(8,128)(2,1)S(1)}, bf16[16,128,768]{2,1,0:T(8,128)(2,1)}, u32[]{:S(2)}) copy-start(bf16[16,128,768]{2,1,0:T(8,128)(2,1)} %pert.3) | copy-start | bytes 9437188
  1.3 8.4 %copy-start.2 = (bf16[16,128,768]{2,1,0:T(8,128)(2,1)S(1)}, bf16[16,128,768]{2,1,0:T(8,128)(2,1)}, u32[]{:S(2)}) copy-start(bf16[16,128,768]{2,1,0:T(8,128)(2,1)} %refs_0_.3) | copy-start | bytes 9437188
  1.3 8.4 %copy-start.3 = (bf16[3,512,512]{2,1,0:T(8,128)(2,1)S(1)}, bf16[3,512,512]{2,1,0:T(8,128)(2,1)}, u32[]{:S(2)}) copy-start(bf16[3,512,512]{2,1,0:T(8,128)(2,1)} %w_mid.1) | copy-start | bytes 4718596
  1.3 8.4 %copy-start.4 = (bf16[768,512]{1,0:T(8,128)(2,1)S(1)}, bf16[768,512]{1,0:T(8,128)(2,1)}, u32[]{:S(2)}) copy-start(bf16[768,512]{1,0:T(8,128)(2,1)} %w_in.1) | copy-start | bytes 2359300
  1.3 8.4 %copy-start.5 = (bf16[512,128]{1,0:T(8,128)(2,1)S(1)}, bf16[512,128]{1,0:T(8,128)(2,1)}, u32[]{:S(2)}) copy-start(bf16[512,128]{1,0:T(8,128)(2,1)} %w_out.1) | copy-start | bytes 393220
  1.3 8.4 %copy-start.8 = (f32[4,512]{1,0:T(4,128)S(1)}, f32[4,512]{1,0:T(4,128)}, u32[]{:S(2)}) copy-start(f32[4,512]{1,0:T(4,128)} %refs_8_.1) | copy-start | bytes 24580
  3.7 8.9 %collective-permute-start = (bf16[48,2688]{1,0:T(8,128)(2,1)S(1)}, bf16[48,2688]{1,0:T(8,128)(2,1)S(1)}, u32[]{:S(2)}, u32[]{:S(2)}) collective-permute-start(bf16[48,2688]{1,0:T(8,128)(2,1)S(1)} %get-tuple-element.21), channel_id=1, source_target_pairs={{0,1},{1,2},{2,3},{4,5},{5,6},{6,7},{8,9},{9,10},{10,11},{12,13},{... | collective-permute-start | bytes 774152 | tf_op jit(solution)/shard_map/ppermute | solution.py:643
  7.8 7.6 %collective-permute-start.1 = (bf16[48,2688]{1,0:T(8,128)(2,1)S(1)}, bf16[48,2688]{1,0:T(8,128)(2,1)S(1)}, u32[]{:S(2)}, u32[]{:S(2)}) collective-permute-start(bf16[48,2688]{1,0:T(8,128)(2,1)S(1)} %get-tuple-element.22), channel_id=1, source_target_pairs={{1,0},{2,1},{3,2},{5,4},{6,5},{7,6},{9,8},{10,9},{11,10},{13,12},{... | collective-permute-start | bytes 774152 | tf_op jit(solution)/shard_map/ppermute | solution.py:643
  9.8 5.7 %copy-start.1 = (bf16[16,128,768]{2,1,0:T(8,128)(2,1)S(1)}, bf16[16,128,768]{2,1,0:T(8,128)(2,1)}, u32[]{:S(2)}) copy-start(bf16[16,128,768]{2,1,0:T(8,128)(2,1)} %adj.3) | copy-start | bytes 9437188
  9.8 5.7 %copy-start.7 = (f32[16,128]{1,0:T(8,128)S(1)}, f32[16,128]{1,0:T(8,128)}, u32[]{:S(2)}) copy-start(f32[16,128]{1,0:T(8,128)} %kappa.3) | copy-start | bytes 24580
  15.7 29.5 %collective-permute-start.2 = (bf16[416,896]{1,0:T(8,128)(2,1)S(1)}, bf16[416,896]{1,0:T(8,128)(2,1)S(1)}, u32[]{:S(2)}, u32[]{:S(2)}) collective-permute-start(bf16[416,896]{1,0:T(8,128)(2,1)S(1)} %get-tuple-element.27), channel_id=1, source_target_pairs={{0,4},{4,8},{8,12},{12,16},{16,20},{20,24},{24,28},{28,32},{32,36}... | collective-permute-start | bytes 2236424 | tf_op jit(solution)/shard_map/ppermute | solution.py:643
  19.3 25.9 %collective-permute-start.3 = (bf16[416,896]{1,0:T(8,128)(2,1)S(1)}, bf16[416,896]{1,0:T(8,128)(2,1)S(1)}, u32[]{:S(2)}, u32[]{:S(2)}) collective-permute-start(bf16[416,896]{1,0:T(8,128)(2,1)S(1)} %get-tuple-element.28), channel_id=1, source_target_pairs={{4,0},{8,4},{12,8},{16,12},{20,16},{24,20},{28,24},{32,28},{36,32}... | collective-permute-start | bytes 2236424 | tf_op jit(solution)/shard_map/ppermute | solution.py:643
  35.0 10.2 %copy-start.6 = (bf16[352,128]{1,0:T(8,128)(2,1)S(1)}, bf16[352,128]{1,0:T(8,128)(2,1)}, u32[]{:S(2)}) copy-start(bf16[352,128]{1,0:T(8,128)(2,1)} %constant.2.clone.picks) | copy-start | bytes 270340
  35.2 25.4 %collective-permute-start.4 = (bf16[400,640]{1,0:T(8,128)(2,1)S(1)}, bf16[400,640]{1,0:T(8,128)(2,1)S(1)}, u32[]{:S(2)}, u32[]{:S(2)}) collective-permute-start(bf16[400,640]{1,0:T(8,128)(2,1)S(1)} %get-tuple-element.30), channel_id=1, source_target_pairs={{0,4},{4,8},{8,12},{12,16},{16,20},{20,24},{24,28},{28,32},{32,36}... | collective-permute-start | bytes 1536008 | tf_op jit(solution)/shard_map/ppermute | solution.py:643
  37.1 23.5 %collective-permute-start.5 = (bf16[400,640]{1,0:T(8,128)(2,1)S(1)}, bf16[400,640]{1,0:T(8,128)(2,1)S(1)}, u32[]{:S(2)}, u32[]{:S(2)}) collective-permute-start(bf16[400,640]{1,0:T(8,128)(2,1)S(1)} %get-tuple-element.31), channel_id=1, source_target_pairs={{4,0},{8,4},{12,8},{16,12},{20,16},{24,20},{28,24},{32,28},{36,32}... | collective-permute-start | bytes 1536008 | tf_op jit(solution)/shard_map/ppermute | solution.py:643

commit v3 on v2

--- a/solution.py
+++ b/solution.py
@@ -15,7 +15,6 @@
 CORNERS = 16
 F32 = jnp.float32
 BF16 = jnp.bfloat16
-EARLY = 1
 
 
 def _params(mib):
@@ -26,6 +25,22 @@
 
 def _held():
     return pl.BlockSpec(memory_space=pltpu.VMEM)
+
+
+def _even(axis):
+    return lax.axis_index(axis) % 2 == 0
+
+
+def _both_ways(axis, act):
+    even = _even(axis)
+
+    @pl.when(even)
+    def _():
+        act(False)
+
+    @pl.when(jnp.logical_not(even))
+    def _():
+        act(True)
 
 
 def _dot(a, b):
@@ -51,7 +66,7 @@
 
 
 def edge_kernel(
-    counts, listed_hbm, kappa_hbm, state, pert, adj, left, right, mask_out,
+    counts, listed_hbm, kappa_hbm, state, pert, adj, msg_1, msg_2, mask_out,
     listed, kappa, near, far, sems,
 ):
     size_x, size_y = kappa.shape
@@ -91,22 +106,25 @@
     want = (row % size_x) * width + row // size_x
     for copy in copies[2:]:
         copy.wait()
-    for msg, blocks, first in ((left, near, 0), (right, far, size_y - REACH)):
-        pick = (col == want + first % width).astype(F32).astype(BF16)
-        for n in range(3):
-            msg[:, n * channels : (n + 1) * channels] = _dot(
-                pick, blocks[n].reshape(size_x * width, channels)
-            ).astype(BF16)
-        at = 3 * channels
-        for j in range(REACH):
-            here = slice(j * size_x, (j + 1) * size_x)
-            y = first + j
-            hi, lo = _split(jnp.broadcast_to(k_all[:, y : y + 1], (size_x, LANES)))
-            msg[here, at : at + LANES] = jnp.broadcast_to(
-                mask[:, y : y + 1], (size_x, LANES)
-            ).astype(BF16)
-            msg[here, at + LANES : at + 2 * LANES] = hi
-            msg[here, at + 2 * LANES : at + 3 * LANES] = lo
+    def write(left, right):
+        for msg, blocks, first in ((left, near, 0), (right, far, size_y - REACH)):
+            pick = (col == want + first % width).astype(F32).astype(BF16)
+            for n in range(3):
+                msg[:, n * channels : (n + 1) * channels] = _dot(
+                    pick, blocks[n].reshape(size_x * width, channels)
+                ).astype(BF16)
+            at = 3 * channels
+            for j in range(REACH):
+                here = slice(j * size_x, (j + 1) * size_x)
+                y = first + j
+                hi, lo = _split(jnp.broadcast_to(k_all[:, y : y + 1], (size_x, LANES)))
+                msg[here, at : at + LANES] = jnp.broadcast_to(
+                    mask[:, y : y + 1], (size_x, LANES)
+                ).astype(BF16)
+                msg[here, at + LANES : at + 2 * LANES] = hi
+                msg[here, at + 2 * LANES : at + 3 * LANES] = lo
+
+    _both_ways("face", lambda odd: write(msg_1, msg_2) if odd else write(msg_2, msg_1))
 
 
 def make_edges(counts, listed, kappa, state, pert, adj):
@@ -153,59 +171,75 @@
     return wide
 
 
-def border_kernel(kappa, from_l, from_r, adj_t, adj_b, pert_t, pert_b, top, bot):
+def border_kernel(kappa, got_1, got_2, adj_t, adj_b, msg_1, msg_2, strips):
+    def order(odd):
+        strips[0], strips[1] = (got_1[...], got_2[...]) if odd else (got_2[...], got_1[...])
+
+    _both_ways("face", order)
+
+    def write(odd):
+        top, bot = (msg_1, msg_2) if odd else (msg_2, msg_1)
+        _write_border(kappa, strips.at[0], strips.at[1], adj_t, adj_b, top, bot)
+
+    _both_ways("elem", write)
+
+
+def _write_border(kappa, from_l, from_r, adj_t, adj_b, top, bot):
     size_x, size_y = kappa.shape
     channels = adj_t.shape[2]
     body = REACH * size_y
-    early = EARLY * LANES
     aux = 3 * channels
     hi, lo = _split(_kappa_wide(kappa, from_l[:, aux:], from_r[:, aux:]))
-    extra = jnp.zeros((size_x, channels + early - 2 * hi.shape[1]), BF16)
-    for msg, adj, pert, is_top in ((top, adj_t, pert_t, True), (bot, adj_b, pert_b, False)):
+    extra = jnp.zeros((size_x, channels - 2 * hi.shape[1]), BF16)
+    for msg, adj, is_top in ((top, adj_t, True), (bot, adj_b, False)):
         first = 0 if is_top else adj.shape[0] - REACH
-        msg[0:body, :channels] = adj[first : first + REACH].reshape(body, channels)
-        msg[0:body, channels:] = pert[
-            first : first + REACH, :, LANES : LANES + early
-        ].reshape(body, early)
+        msg[0:body, :] = adj[first : first + REACH].reshape(body, channels)
         pick_l, pick_r = _corner_picks(size_x, is_top)
         here = slice(body, body + CORNERS)
-        msg[here, :channels] = (
+        msg[here, :] = (
             _dot(pick_l, from_l[:, 2 * channels : aux])
             + _dot(pick_r, from_r[:, 2 * channels : aux])
         ).astype(BF16)
-        lanes = slice(channels + LANES, channels + LANES + early)
-        msg[here, channels:] = (
-            _dot(pick_l, from_l[:, lanes]) + _dot(pick_r, from_r[:, lanes])
-        ).astype(BF16)
         msg[body + CORNERS :, :] = jnp.concatenate([hi, lo, extra], axis=1)
 
 
-def first_border(kappa, from_l, from_r, adj, pert):
+def first_border(kappa, got, adj):
     size_x, size_y, channels = adj.shape
     block = 4
     last = size_x // block - 1
     whole = lambda a: pl.BlockSpec(a.shape, lambda i: (0,) * a.ndim)
     low = pl.BlockSpec((block, size_y, channels), lambda i: (0, 0, 0))
     high = pl.BlockSpec((block, size_y, channels), lambda i: (last, 0, 0))
-    shape = (REACH * size_y + CORNERS + size_x, channels + EARLY * LANES)
+    shape = (REACH * size_y + CORNERS + size_x, channels)
     out = jax.ShapeDtypeStruct(shape, BF16)
+    strips = jax.ShapeDtypeStruct((2,) + got[0].shape, BF16)
     return pl.pallas_call(
         border_kernel,
         grid=(1,),
-        in_specs=[whole(kappa), whole(from_l), whole(from_r), low, high, low, high],
-        out_specs=[whole(out)] * 2,
-        out_shape=[out, out],
+        in_specs=[whole(kappa), whole(got[0]), whole(got[1]), low, high],
+        out_specs=[whole(out), whole(out), whole(strips)],
+        out_shape=[out, out, strips],
         compiler_params=_params(12),
         name="first_border",
-    )(kappa, from_l, from_r, adj, adj, pert, pert)
-
-
-def late_border_kernel(from_l, from_r, moved_s, pert_t, pert_b, moved_t, moved_b, top, bot):
+    )(kappa, got[0], got[1], adj, adj)
+
+
+def late_border_kernel(strips, moved_s, pert_t, pert_b, moved_t, moved_b, msg_1, msg_2):
+    def write(odd):
+        top, bot = (msg_1, msg_2) if odd else (msg_2, msg_1)
+        _write_late(
+            strips.at[0], strips.at[1], moved_s, pert_t, pert_b, moved_t, moved_b, top, bot
+        )
+
+    _both_ways("elem", write)
+
+
+def _write_late(from_l, from_r, moved_s, pert_t, pert_b, moved_t, moved_b, top, bot):
     size_y, channels = pert_t.shape[1:]
     size_x = moved_s.shape[0] // (2 * REACH)
     body = REACH * size_y
     cut = REACH * size_x
-    lanes = slice((1 + EARLY) * LANES, channels)
+    lanes = slice(LANES, channels)
     side = slice(channels + lanes.start, 2 * channels)
     for msg, pert, moved, is_top in (
         (top, pert_t, moved_t, True),
@@ -225,20 +259,20 @@
         )
 
 
-def late_border(from_l, from_r, moved_s, pert, moved_a, moved_b):
+def late_border(strips, moved_s, pert, moved_a, moved_b):
     size_x, size_y, channels = pert.shape
     block = 4
     last = size_x // block - 1
     end = moved_b.shape[0] // (block * size_y) - 1
     whole = lambda a: pl.BlockSpec(a.shape, lambda i: (0,) * a.ndim)
     out = jax.ShapeDtypeStruct(
-        (REACH * size_y + CORNERS, channels - EARLY * LANES), BF16
+        (REACH * size_y + CORNERS, channels), BF16
     )
     return pl.pallas_call(
         late_border_kernel,
         grid=(1,),
         in_specs=[
-            whole(from_l), whole(from_r), whole(moved_s),
+            whole(strips), whole(moved_s),
             pl.BlockSpec((block, size_y, channels), lambda i: (0, 0, 0)),
             pl.BlockSpec((block, size_y, channels), lambda i: (last, 0, 0)),
             pl.BlockSpec((block * size_y, LANES), lambda i: (0, 0)),
@@ -248,7 +282,7 @@
         out_shape=[out, out],
         compiler_params=_params(12),
         name="late_border",
-    )(from_l, from_r, moved_s, pert, pert, moved_a, moved_b)
+    )(strips, moved_s, pert, pert, moved_a, moved_b)
 
 
 def _forward(pairs, w_in, w_mid, w_out, biases, keep):
@@ -268,7 +302,7 @@
 
 def forward_kernel(first, strips, rows, chunks, *refs):
     if strips:
-        (state, pert, mask, from_l, from_r, w_in, w_mid, w_out, biases,
+        (state, pert, mask, beside_all, w_in, w_mid, w_out, biases,
          slopes, moved, moved_s, side_x, side_d, side_m) = refs
     else:
         state, pert, mask, w_in, w_mid, w_out, biases, slopes, moved = refs
@@ -277,16 +311,16 @@
     units = biases.shape[1]
     xs = rows // size_y
     if strips:
-        cut = from_l.shape[0]
+        cut = beside_all.shape[1]
         each = 2 * cut // pl.num_programs(0)
 
         @pl.when(step == 0)
         def _():
-            for n, msg in enumerate((from_l, from_r)):
+            for n in range(2):
                 here = slice(n * cut, (n + 1) * cut)
-                side_x[here, :] = msg[:, :channels]
-                side_d[here, :] = msg[:, channels : 2 * channels]
-                side_m[here, :] = msg[:, 3 * channels : 3 * channels + LANES]
+                side_x[here, :] = beside_all[n, :, :channels]
+                side_d[here, :] = beside_all[n, :, channels : 2 * channels]
+                side_m[here, :] = beside_all[n, :, 3 * channels : 3 * channels + LANES]
 
         beside = pl.ds(pl.multiple_of(step * each, each), each)
     x_here = pl.ds(first + step * xs, xs)
@@ -333,7 +367,7 @@
     ]
     scratch = []
     if sides:
-        beside = 2 * sides[0].shape[0]
+        beside = 2 * sides[0].shape[1]
         out.append(jax.ShapeDtypeStruct((beside, LANES), BF16))
         scratch = [
             pltpu.VMEM((beside, channels), BF16),
@@ -450,9 +484,11 @@
 
 
 def adjoint_kernel(
-    adj, above, below, from_l, from_r, picks, kappa, mask, slopes_a, slopes_b, w_in, w_mid, w_out,
-    kap, out, ping, pong, natural, inverse, moved, sides,
+    adj, got_1, got_2, strips, picks, kappa, mask, slopes_a, slopes_b, w_in, w_mid, w_out,
+    kap, out, ping, pong, natural, inverse, moved, sides, border,
 ):
+    above, below = border.at[0], border.at[1]
+    from_l, from_r = strips.at[0], strips.at[1]
     step = pl.program_id(0)
     groups = moved.shape[0]
     size_x, size_y = kappa.shape
@@ -463,6 +499,10 @@
 
     @pl.when(step == 0)
     def _():
+        def order(odd):
+            border[0], border[1] = (got_1[...], got_2[...]) if odd else (got_2[...], got_1[...])
+
+        _both_ways("elem", order)
         k_rows = slice(body + CORNERS, body + CORNERS + size_x)
         _kappa_frame(
             kappa, from_l[:, aux:], from_r[:, aux:], above[k_rows, :], below[k_rows, :], natural, kap
@@ -520,7 +560,7 @@
         back(slopes_b, step - groups, split)
 
 
-def adjoint_all(adj, above, below, from_l, from_r, kappa, mask, slopes_a, slopes_b, weights):
+def adjoint_all(adj, got, strips, kappa, mask, slopes_a, slopes_b, weights):
     size_x, size_y, channels = adj.shape
     columns = size_x * size_y
     groups = channels // LANES
@@ -528,7 +568,7 @@
     rows = columns // blocks
     frame = (size_x + 2 * REACH) * (size_y + 2 * SIDE)
     picks = _side_picks(size_x)
-    args = (adj, above, below, from_l, from_r, picks, kappa, mask, slopes_a, slopes_b) + weights
+    args = (adj,) + got + (strips, picks, kappa, mask, slopes_a, slopes_b) + weights
     return pl.pallas_call(
         adjoint_kernel,
         grid=(groups + blocks,),
@@ -548,68 +588,60 @@
             pltpu.VMEM((columns, LANES), F32),
             pltpu.VMEM((groups, columns, LANES), F32),
             pltpu.VMEM((picks.shape[0], channels), F32),
+            pltpu.VMEM((2,) + got[0].shape, BF16),
         ],
-        compiler_params=_params(26),
+        compiler_params=_params(28),
         name="adjoint",
     )(*args)
 
 
 def tangent_kernel(
-    pert, moved_a, moved_b, first_t, first_b, late_t, late_b, from_l, from_r, moved_s, picks, kap,
-    out, ping, pong, sides,
+    pert, moved_a, moved_b, late_1, late_2, strips, moved_s, picks, kap,
+    out, ping, pong, sides, border,
 ):
     step = pl.program_id(0)
     size_x, size_y, _ = out.shape
     channels = pert.shape[2]
     cut = moved_s.shape[0] // 2
     body = REACH * size_y
-    early = EARLY * LANES
 
     @pl.when(step == 0)
     def _():
-        ends = [
+        def order(odd):
+            border[0], border[1] = (late_1[...], late_2[...]) if odd else (late_2[...], late_1[...])
+
+        _both_ways("elem", order)
+        ends = [border[n, body : body + CORNERS, :] for n in range(2)]
+        beside = [
             jnp.concatenate(
-                [
-                    late[body : body + CORNERS, :LANES],
-                    first[body : body + CORNERS, channels : channels + early],
-                    late[body : body + CORNERS, LANES:],
-                ],
+                [moved_s[n * cut : (n + 1) * cut, :], strips[n, :, channels + LANES : 2 * channels]],
                 axis=1,
             )
-            for first, late in ((first_t, late_t), (first_b, late_b))
+            for n in range(2)
         ]
-        strips = [
-            jnp.concatenate(
-                [moved_s[n * cut : (n + 1) * cut, :], msg[:, channels + LANES : 2 * channels]], axis=1
-            )
-            for n, msg in enumerate((from_l, from_r))
-        ]
-        _place_sides(sides, picks, strips[0], strips[1], ends)
+        _place_sides(sides, picks, beside[0], beside[1], ends)
+
+    here = _lanes(step)
+
+    def fill(own):
+        _fill(
+            ping, own, lambda r: border[0, r, here], lambda r: border[1, r, here],
+            sides, here, size_x, size_y,
+        )
+
+    @pl.when(step == 0)
+    def _():
         split = moved_a.shape[0] // size_y
 
         def own(x):
             source, k = (moved_a, x) if x < split else (moved_b, x - split)
             return source[k * size_y : (k + 1) * size_y, :]
 
-        _fill(
-            ping, own, lambda r: late_t[r, :LANES], lambda r: late_b[r, :LANES],
-            sides, slice(0, LANES), size_x, size_y,
-        )
-
-    def fill(top, bot, lanes):
-        here = _lanes(step)
-        _fill(
-            ping, lambda x: pert[x, :, here], lambda r: top[r, lanes], lambda r: bot[r, lanes],
-            sides, here, size_x, size_y,
-        )
-
-    @pl.when((step > 0) & (step <= EARLY))
-    def _():
-        fill(first_t, first_b, _lanes(channels // LANES + step - 1))
-
-    @pl.when(step > EARLY)
-    def _():
-        fill(late_t, late_b, _lanes(step - EARLY))
+        fill(own)
+
+    @pl.when(step > 0)
+    def _():
+        fill(lambda x: pert[x, :, here])
 
     def emit(x, lo, size, value):
         out[x, lo : lo + size, :] = value
@@ -617,10 +649,10 @@
     _transport(ping, pong, kap, size_x, size_y, emit)
 
 
-def tangent_all(pert, moved_a, moved_b, first, late, from_l, from_r, moved_s, kap):
+def tangent_all(pert, moved_a, moved_b, late, strips, moved_s, kap):
     size_x, size_y, channels = pert.shape
     picks = _side_picks(size_x)
-    args = (pert, moved_a, moved_b) + first + late + (from_l, from_r, moved_s, picks, kap)
+    args = (pert, moved_a, moved_b) + late + (strips, moved_s, picks, kap)
     return pl.pallas_call(
         tangent_kernel,
         grid=(channels // LANES,),
@@ -631,16 +663,18 @@
             pltpu.VMEM(kap.shape, F32),
             pltpu.VMEM(kap.shape, F32),
             pltpu.VMEM((picks.shape[0], channels), F32),
+            pltpu.VMEM((2, REACH * size_y + CORNERS, channels), BF16),
         ],
-        compiler_params=_params(12),
+        compiler_params=_params(14),
         name="tangent",
     )(*args)
 
 
-def _shift(value, axis, way):
-    ends = lax.axis_size(axis) - 1
-    pairs = [(i, i + 1) if way > 0 else (i + 1, i) for i in range(ends)]
-    return lax.ppermute(value, axis, pairs)
+def _swap(first, second, axis):
+    count = lax.axis_size(axis)
+    pairs = [(i, i ^ 1) for i in range(count)]
+    others = [(i, ((i + 1) ^ 1) - 1) for i in range(1, count - 1)]
+    return lax.ppermute(first, axis, pairs), lax.ppermute(second, axis, others)
 
 
 def per_device(
@@ -650,22 +684,20 @@
     weights = (w_in, w_mid, w_out)
     nets = weights + (biases,)
     part = 4
-    left, right, mask = make_edges(counts, act_list, kappa, state, perturbation, adjoint_end)
-    from_l = _shift(right, "face", 1)
-    from_r = _shift(left, "face", -1)
+    msg_1, msg_2, mask = make_edges(counts, act_list, kappa, state, perturbation, adjoint_end)
+    got = _swap(msg_1, msg_2, "face")
     slopes_a, moved_a = forward(0, part, state, perturbation, mask, (), nets)
-    from_l, from_r, slopes_a = lax.optimization_barrier((from_l, from_r, slopes_a))
-    top, bot = first_border(kappa, from_l, from_r, adjoint_end, perturbation)
-    first = (_shift(bot, "elem", 1), _shift(top, "elem", -1))
+    got, slopes_a = lax.optimization_barrier((got, slopes_a))
+    msg_1, msg_2, strips = first_border(kappa, got, adjoint_end)
+    first = _swap(msg_1, msg_2, "elem")
     slopes_b, moved_b, moved_s = forward(
-        part, size_x - part, state, perturbation, mask, (from_l, from_r), nets
+        part, size_x - part, state, perturbation, mask, (strips,), nets
     )
-    top, bot = late_border(from_l, from_r, moved_s, perturbation, moved_a, moved_b)
-    late = (_shift(bot, "elem", 1), _shift(top, "elem", -1))
+    late = _swap(*late_border(strips, moved_s, perturbation, moved_a, moved_b), "elem")
     kap, ad_out = adjoint_all(
-        adjoint_end, first[0], first[1], from_l, from_r, kappa, mask, slopes_a, slopes_b, weights
+        adjoint_end, first, strips, kappa, mask, slopes_a, slopes_b, weights
     )
-    tl_out = tangent_all(perturbation, moved_a, moved_b, first, late, from_l, from_r, moved_s, kap)
+    tl_out = tangent_all(perturbation, moved_a, moved_b, late, strips, moved_s, kap)
     return tl_out, ad_out.reshape(size_x, size_y, channels)
 
 

time: 68.6 us -> 58.7 us (0.86)
  starting transfers between devices: 26.1 us -> 16.4 us
    ppermute x6, starting transfers between devices: 26.1 us -> 16.4 us  [the longest x3 13.8 us: _swap(): lax.ppermute(second, axis, others)]
  transfers between devices with their start and end apart: 6 -> 6, of which waited for: 1 -> 3; matrix products, arithmetic and copies ran while one was open for 0% -> 0% of each run, Pallas kernels for 40% -> 47%
where the time goes in v3:
time: 58.7 us; the launch traced here: 58.5 us
  Pallas kernels  38.1 us (65%)
  starting transfers between devices  16.4 us (28%)
  waiting for transfers between devices  2.47 us (4%)
  between operations  1.48 us (3%)
    pallas_call x1, Pallas kernels, adjoint_all(): pl.pallas_call(adjoint_kernel, grid=(groups + blocks,), in_specs=[_held()...  15.4 us
    ppermute x3, starting transfers between devices, _swap(): lax.ppermute(second, axis, others)  13.8 us
    pallas_call x2, Pallas kernels, forward(): pl.pallas_call(functools.partial(forward_kernel, first, bool(sides), rows...  11.9 us
    pallas_call x1, Pallas kernels, tangent_all(): pl.pallas_call(tangent_kernel, grid=(channels // LANES,), in_specs=[_held...  7.92 us
    ppermute x3, starting transfers between devices, _swap(): lax.ppermute(first, axis, pairs)  2.56 us
    ppermute x3, waiting for transfers between devices, _swap(): lax.ppermute(second, axis, others)  2.47 us
    pallas_call x1, Pallas kernels, make_edges(): pl.pallas_call(edge_kernel, in_specs=[pl.BlockSpec(memory_space=pltpu.SME...  2.37 us
  transfers between devices with their start and end apart: 6, of which 3 were waited for; matrix products, arithmetic and copies ran while one was open for 0% of the time, Pallas kernels for 47%

profile of v3, /device:TPU:7, one launch (start us, length us, event | category | flops | bytes accessed | tf_op | source)
XLA Modules:
  0.0 58.5 jit_solution(10423827489407596942)
XLA Ops:
  1.3 0.0 copy-start
  1.3 0.0 copy-start.2
  1.3 0.0 copy-start.3
  1.3 0.0 copy-start.4
  1.3 0.0 copy-start.5
  1.3 0.0 copy-start.8
  1.3 2.4 %edges.1 = (bf16[48,2688]{1,0:T(8,128)(2,1)S(1)}, bf16[48,2688]{1,0:T(8,128)(2,1)S(1)}, bf16[2048,128]{1,0:T(8,128)(2,1)S(1)}) custom-call(s32[1,1]{1,0:T(1,128)S(6)} %copy.14.counts, s32[1,1024]{1,0:T(1,128)} %listed_hbm.1, f32[16,128]{1,0:T(8,128)} %kappa.3, bf16[16,128,768]{2,1,0:T(8,128)(2,1)} %refs_0_.3, bf16[16,128,768]{2,1,0:T(8,128)(2,1)} %pert.3, ...), custom_call_target="tpu_custom_call" | custom-call | tf_op jit(solution)/shard_map/edges/pallas_call | solution.py:135
  3.7 0.8 %collective-permute-start = (bf16[48,2688]{1,0:T(8,128)(2,1)S(1)}, bf16[48,2688]{1,0:T(8,128)(2,1)S(1)}, u32[]{:S(2)}, u32[]{:S(2)}) collective-permute-start(bf16[48,2688]{1,0:T(8,128)(2,1)S(1)} %get-tuple-element.22), channel_id=1, source_target_pairs={{0,1},{1,0},{2,3},{3,2},{4,5},{5,4},{6,7},{7,6},{8,9},{9,8},{10,11... | collective-permute-start | bytes 774152 | tf_op jit(solution)/shard_map/ppermute | solution.py:677
  4.5 3.4 %collective-permute-start.1 = (bf16[48,2688]{1,0:T(8,128)(2,1)S(1)}, bf16[48,2688]{1,0:T(8,128)(2,1)S(1)}, u32[]{:S(2)}, u32[]{:S(2)}) collective-permute-start(bf16[48,2688]{1,0:T(8,128)(2,1)S(1)} %get-tuple-element.23), channel_id=1, source_target_pairs={{1,2},{2,1},{5,6},{6,5},{9,10},{10,9},{13,14},{14,13},{17,18},{18,... | collective-permute-start | bytes 774152 | tf_op jit(solution)/shard_map/ppermute | solution.py:677
  7.8 0.0 copy-done
  7.9 0.0 copy-done.2
  7.9 0.0 copy-done.3
  7.9 0.0 copy-done.4
  7.9 0.0 copy-done.5
  7.9 0.0 copy-done.8
  7.9 0.0 copy-start.1
  7.9 0.0 copy-start.7
  7.9 2.9 %forward_part.1 = (bf16[512,2048]{1,0:T(8,128)(2,1)S(1)}, bf16[512,128]{1,0:T(8,128)(2,1)S(1)}) custom-call(bf16[16,128,768]{2,1,0:T(8,128)(2,1)S(1)} %copy-done.2, bf16[16,128,768]{2,1,0:T(8,128)(2,1)S(1)} %copy-done, bf16[2048,128]{1,0:T(8,128)(2,1)S(1)} %get-tuple-element.20.refs_2_.mask, bf16[768,512]{1,0:T(8,128)(2,1)S(1)} %copy-done.4, ...), custom_call_target="tpu_custom_call" | custom-call | tf_op jit(solution)/shard_map/forward_part/pallas_call | solution.py:377
  10.8 0.0 collective-permute-done.got_1
  10.8 1.4 %collective-permute-done.1.got_2 = bf16[48,2688]{1,0:T(8,128)(2,1)S(1)} collective-permute-done((bf16[48,2688]{1,0:T(8,128)(2,1)S(1)}, bf16[48,2688]{1,0:T(8,128)(2,1)S(1)}, u32[]{:S(2)}, u32[]{:S(2)}) %collective-permute-start.1) | collective-permute-done | bytes 258080 | tf_op jit(solution)/shard_map/ppermute | solution.py:677
  12.2 0.0 copy-done.1
  12.2 0.0 copy-done.7
  12.2 0.3 first_border.1
  12.5 1.7 %collective-permute-start.4 = (bf16[416,768]{1,0:T(8,128)(2,1)S(1)}, bf16[416,768]{1,0:T(8,128)(2,1)S(1)}, u32[]{:S(2)}, u32[]{:S(2)}) collective-permute-start(bf16[416,768]{1,0:T(8,128)(2,1)S(1)} %get-tuple-element.32), channel_id=1, source_target_pairs={{0,4},{4,0},{8,12},{12,8},{16,20},{20,16},{24,28},{28,24},{32,36},... | collective-permute-start | bytes 1916936 | tf_op jit(solution)/shard_map/ppermute | solution.py:677
  14.2 7.0 %collective-permute-start.5 = (bf16[416,768]{1,0:T(8,128)(2,1)S(1)}, bf16[416,768]{1,0:T(8,128)(2,1)S(1)}, u32[]{:S(2)}, u32[]{:S(2)}) collective-permute-start(bf16[416,768]{1,0:T(8,128)(2,1)S(1)} %get-tuple-element.33), channel_id=1, source_target_pairs={{4,8},{8,4},{12,16},{16,12},{20,24},{24,20},{28,32},{32,28},{36,40... | collective-permute-start | bytes 1916936 | tf_op jit(solution)/shard_map/ppermute | solution.py:677
  21.3 9.1 %forward_rest.1 = (bf16[1536,2048]{1,0:T(8,128)(2,1)S(1)}, bf16[1536,128]{1,0:T(8,128)(2,1)S(1)}, bf16[96,128]{1,0:T(8,128)(2,1)S(1)}) custom-call(bf16[16,128,768]{2,1,0:T(8,128)(2,1)S(1)} %copy-done.2, bf16[16,128,768]{2,1,0:T(8,128)(2,1)S(1)} %copy-done, bf16[2048,128]{1,0:T(8,128)(2,1)S(1)} %get-tuple-element.20.refs_2_.mask, ...), custom_call_target="tpu_custom_call" | custom-call | tf_op jit(solution)/shard_map/forward_rest/pallas_call | solution.py:377
  30.4 0.0 copy-start.6
  30.4 0.3 late_border.1
  30.7 0.1 collective-permute-start.2
  30.7 3.4 %collective-permute-start.3 = (bf16[400,768]{1,0:T(8,128)(2,1)S(1)}, bf16[400,768]{1,0:T(8,128)(2,1)S(1)}, u32[]{:S(2)}, u32[]{:S(2)}) collective-permute-start(bf16[400,768]{1,0:T(8,128)(2,1)S(1)} %get-tuple-element.31), channel_id=1, source_target_pairs={{4,8},{8,4},{12,16},{16,12},{20,24},{24,20},{28,32},{32,28},{36,40... | collective-permute-start | bytes 1843208 | tf_op jit(solution)/shard_map/ppermute | solution.py:677
  34.2 0.0 collective-permute-done.4.got_1
  34.2 0.1 collective-permute-done.5.got_2
  34.3 0.0 copy-done.6
  34.3 15.4 %adjoint.1 = (f32[3168,128]{1,0:T(8,128)S(1)}, f32[2048,768]{1,0:T(8,128)}) custom-call(bf16[16,128,768]{2,1,0:T(8,128)(2,1)S(1)} %copy-done.1, bf16[416,768]{1,0:T(8,128)(2,1)S(1)} %collective-permute-done.4.got_1, bf16[416,768]{1,0:T(8,128)(2,1)S(1)} %collective-permute-done.5.got_2, bf16[2,48,2688]{2,1,0:T(8,128)(2,1)S(1)} %get-tuple-element.27.refs_3_.strips, ...), custom_call_target="tpu_custom_call" | custom-call | tf_op jit(solution)/shard_map/adjoint/pallas_call | solution.py:572
  49.7 0.0 collective-permute-done.2.late_1
  49.7 0.9 %collective-permute-done.3.late_2 = bf16[400,768]{1,0:T(8,128)(2,1)S(1)} collective-permute-done((bf16[400,768]{1,0:T(8,128)(2,1)S(1)}, bf16[400,768]{1,0:T(8,128)(2,1)S(1)}, u32[]{:S(2)}, u32[]{:S(2)}) %collective-permute-start.3) | collective-permute-done | bytes 614432 | tf_op jit(solution)/shard_map/ppermute | solution.py:677
  50.6 7.9 %tangent.1 = f32[16,128,768]{2,1,0:T(8,128)} custom-call(bf16[16,128,768]{2,1,0:T(8,128)(2,1)S(1)} %copy-done, bf16[512,128]{1,0:T(8,128)(2,1)S(1)} %get-tuple-element.21.moved_t.moved_a, bf16[1536,128]{1,0:T(8,128)(2,1)S(1)} %get-tuple-element.28.moved_b, bf16[400,768]{1,0:T(8,128)(2,1)S(1)} %collective-permute-done.2.late_1, ...), custom_call_target="tpu_custom_call" | custom-call | tf_op jit(solution)/shard_map/tangent/pallas_call | solution.py:656
Async XLA Ops:
  1.3 6.6 %copy-start = (bf16[16,128,768]{2,1,0:T(8,128)(2,1)S(1)}, bf16[16,128,768]{2,1,0:T(8,128)(2,1)}, u32[]{:S(2)}) copy-start(bf16[16,128,768]{2,1,0:T(8,128)(2,1)} %pert.3) | copy-start | bytes 9437188
  1.3 6.6 %copy-start.2 = (bf16[16,128,768]{2,1,0:T(8,128)(2,1)S(1)}, bf16[16,128,768]{2,1,0:T(8,128)(2,1)}, u32[]{:S(2)}) copy-start(bf16[16,128,768]{2,1,0:T(8,128)(2,1)} %refs_0_.3) | copy-start | bytes 9437188
  1.3 6.6 %copy-start.3 = (bf16[3,512,512]{2,1,0:T(8,128)(2,1)S(1)}, bf16[3,512,512]{2,1,0:T(8,128)(2,1)}, u32[]{:S(2)}) copy-start(bf16[3,512,512]{2,1,0:T(8,128)(2,1)} %w_mid.1) | copy-start | bytes 4718596
  1.3 6.6 %copy-start.4 = (bf16[768,512]{1,0:T(8,128)(2,1)S(1)}, bf16[768,512]{1,0:T(8,128)(2,1)}, u32[]{:S(2)}) copy-start(bf16[768,512]{1,0:T(8,128)(2,1)} %w_in.1) | copy-start | bytes 2359300
  1.3 6.6 %copy-start.5 = (bf16[512,128]{1,0:T(8,128)(2,1)S(1)}, bf16[512,128]{1,0:T(8,128)(2,1)}, u32[]{:S(2)}) copy-start(bf16[512,128]{1,0:T(8,128)(2,1)} %w_out.1) | copy-start | bytes 393220
  1.3 6.6 %copy-start.8 = (f32[4,512]{1,0:T(4,128)S(1)}, f32[4,512]{1,0:T(4,128)}, u32[]{:S(2)}) copy-start(f32[4,512]{1,0:T(4,128)} %refs_7_.1) | copy-start | bytes 24580
  3.7 7.1 %collective-permute-start = (bf16[48,2688]{1,0:T(8,128)(2,1)S(1)}, bf16[48,2688]{1,0:T(8,128)(2,1)S(1)}, u32[]{:S(2)}, u32[]{:S(2)}) collective-permute-start(bf16[48,2688]{1,0:T(8,128)(2,1)S(1)} %get-tuple-element.22), channel_id=1, source_target_pairs={{0,1},{1,0},{2,3},{3,2},{4,5},{5,4},{6,7},{7,6},{8,9},{9,8},{10,11... | collective-permute-start | bytes 774152 | tf_op jit(solution)/shard_map/ppermute | solution.py:677
  4.5 7.8 %collective-permute-start.1 = (bf16[48,2688]{1,0:T(8,128)(2,1)S(1)}, bf16[48,2688]{1,0:T(8,128)(2,1)S(1)}, u32[]{:S(2)}, u32[]{:S(2)}) collective-permute-start(bf16[48,2688]{1,0:T(8,128)(2,1)S(1)} %get-tuple-element.23), channel_id=1, source_target_pairs={{1,2},{2,1},{5,6},{6,5},{9,10},{10,9},{13,14},{14,13},{17,18},{18,... | collective-permute-start | bytes 774152 | tf_op jit(solution)/shard_map/ppermute | solution.py:677
  7.9 4.3 %copy-start.1 = (bf16[16,128,768]{2,1,0:T(8,128)(2,1)S(1)}, bf16[16,128,768]{2,1,0:T(8,128)(2,1)}, u32[]{:S(2)}) copy-start(bf16[16,128,768]{2,1,0:T(8,128)(2,1)} %adj.3) | copy-start | bytes 9437188
  7.9 4.3 %copy-start.7 = (f32[16,128]{1,0:T(8,128)S(1)}, f32[16,128]{1,0:T(8,128)}, u32[]{:S(2)}) copy-start(f32[16,128]{1,0:T(8,128)} %kappa.3) | copy-start | bytes 24580
  12.5 21.7 %collective-permute-start.4 = (bf16[416,768]{1,0:T(8,128)(2,1)S(1)}, bf16[416,768]{1,0:T(8,128)(2,1)S(1)}, u32[]{:S(2)}, u32[]{:S(2)}) collective-permute-start(bf16[416,768]{1,0:T(8,128)(2,1)S(1)} %get-tuple-element.32), channel_id=1, source_target_pairs={{0,4},{4,0},{8,12},{12,8},{16,20},{20,16},{24,28},{28,24},{32,36},... | collective-permute-start | bytes 1916936 | tf_op jit(solution)/shard_map/ppermute | solution.py:677
  14.2 20.1 %collective-permute-start.5 = (bf16[416,768]{1,0:T(8,128)(2,1)S(1)}, bf16[416,768]{1,0:T(8,128)(2,1)S(1)}, u32[]{:S(2)}, u32[]{:S(2)}) collective-permute-start(bf16[416,768]{1,0:T(8,128)(2,1)S(1)} %get-tuple-element.33), channel_id=1, source_target_pairs={{4,8},{8,4},{12,16},{16,12},{20,24},{24,20},{28,32},{32,28},{36,40... | collective-permute-start | bytes 1916936 | tf_op jit(solution)/shard_map/ppermute | solution.py:677
  30.4 3.9 %copy-start.6 = (bf16[352,128]{1,0:T(8,128)(2,1)S(1)}, bf16[352,128]{1,0:T(8,128)(2,1)}, u32[]{:S(2)}) copy-start(bf16[352,128]{1,0:T(8,128)(2,1)} %constant.2.clone.picks) | copy-start | bytes 270340
  30.7 19.0 %collective-permute-start.2 = (bf16[400,768]{1,0:T(8,128)(2,1)S(1)}, bf16[400,768]{1,0:T(8,128)(2,1)S(1)}, u32[]{:S(2)}, u32[]{:S(2)}) collective-permute-start(bf16[400,768]{1,0:T(8,128)(2,1)S(1)} %get-tuple-element.30), channel_id=1, source_target_pairs={{0,4},{4,0},{8,12},{12,8},{16,20},{20,16},{24,28},{28,24},{32,36},... | collective-permute-start | bytes 1843208 | tf_op jit(solution)/shard_map/ppermute | solution.py:677
  30.7 19.8 %collective-permute-start.3 = (bf16[400,768]{1,0:T(8,128)(2,1)S(1)}, bf16[400,768]{1,0:T(8,128)(2,1)S(1)}, u32[]{:S(2)}, u32[]{:S(2)}) collective-permute-start(bf16[400,768]{1,0:T(8,128)(2,1)S(1)} %get-tuple-element.31), channel_id=1, source_target_pairs={{4,8},{8,4},{12,16},{16,12},{20,24},{24,20},{28,32},{32,28},{36,40... | collective-permute-start | bytes 1843208 | tf_op jit(solution)/shard_map/ppermute | solution.py:677

commit v4 on v3

--- a/solution.py
+++ b/solution.py
@@ -13,6 +13,7 @@
 LANES = 128
 SIDE = 8
 CORNERS = 16
+KAPPA_ROW = 8
 F32 = jnp.float32
 BF16 = jnp.bfloat16
 
@@ -118,11 +119,11 @@
                 here = slice(j * size_x, (j + 1) * size_x)
                 y = first + j
                 hi, lo = _split(jnp.broadcast_to(k_all[:, y : y + 1], (size_x, LANES)))
-                msg[here, at : at + LANES] = jnp.broadcast_to(
-                    mask[:, y : y + 1], (size_x, LANES)
-                ).astype(BF16)
-                msg[here, at + LANES : at + 2 * LANES] = hi
-                msg[here, at + 2 * LANES : at + 3 * LANES] = lo
+                live = jnp.broadcast_to(mask[:, y : y + 1], (size_x, LANES))
+                lane = lax.broadcasted_iota(jnp.int32, live.shape, 1)
+                value = jnp.where(lane == 1, hi.astype(F32), live)
+                value = jnp.where(lane == 2, lo.astype(F32), value)
+                msg[here, at : at + LANES] = value.astype(BF16)
 
     _both_ways("face", lambda odd: write(msg_1, msg_2) if odd else write(msg_2, msg_1))
 
@@ -130,7 +131,7 @@
 def make_edges(counts, listed, kappa, state, pert, adj):
     size_x, size_y, channels = state.shape
     width = 16
-    strip = jax.ShapeDtypeStruct((REACH * size_x, 3 * channels + 3 * LANES), BF16)
+    strip = jax.ShapeDtypeStruct((REACH * size_x, 3 * channels + LANES), BF16)
     far = pl.BlockSpec(memory_space=pltpu.HBM)
     return pl.pallas_call(
         edge_kernel,
@@ -164,10 +165,9 @@
     for aux, first in ((aux_l, wide.shape[1] - REACH), (aux_r, size_y)):
         for j in range(REACH):
             here = slice(j * size_x, (j + 1) * size_x)
-            value = aux[here, LANES : 2 * LANES].astype(F32) + aux[
-                here, 2 * LANES : 3 * LANES
-            ].astype(F32)
-            wide = jnp.where(lane == first + j, jnp.concatenate([value, value], axis=1), wide)
+            both = aux[here, :].astype(F32)
+            value = jnp.broadcast_to(both[:, 1:2] + both[:, 2:3], wide.shape)
+            wide = jnp.where(lane == first + j, value, wide)
     return wide
 
 
@@ -190,17 +190,19 @@
     body = REACH * size_y
     aux = 3 * channels
     hi, lo = _split(_kappa_wide(kappa, from_l[:, aux:], from_r[:, aux:]))
-    extra = jnp.zeros((size_x, channels - 2 * hi.shape[1]), BF16)
+    extra = jnp.zeros((CORNERS, channels - 2 * hi.shape[1]), F32)
     for msg, adj, is_top in ((top, adj_t, True), (bot, adj_b, False)):
         first = 0 if is_top else adj.shape[0] - REACH
         msg[0:body, :] = adj[first : first + REACH].reshape(body, channels)
         pick_l, pick_r = _corner_picks(size_x, is_top)
+        row = 0 if is_top else size_x - REACH
+        place = _pick((CORNERS, size_x), [(KAPPA_ROW + k, row + k) for k in range(REACH)])
         here = slice(body, body + CORNERS)
         msg[here, :] = (
             _dot(pick_l, from_l[:, 2 * channels : aux])
             + _dot(pick_r, from_r[:, 2 * channels : aux])
+            + jnp.concatenate([_dot(place, hi), _dot(place, lo), extra], axis=1)
         ).astype(BF16)
-        msg[body + CORNERS :, :] = jnp.concatenate([hi, lo, extra], axis=1)
 
 
 def first_border(kappa, got, adj):
@@ -210,7 +212,7 @@
     whole = lambda a: pl.BlockSpec(a.shape, lambda i: (0,) * a.ndim)
     low = pl.BlockSpec((block, size_y, channels), lambda i: (0, 0, 0))
     high = pl.BlockSpec((block, size_y, channels), lambda i: (last, 0, 0))
-    shape = (REACH * size_y + CORNERS + size_x, channels)
+    shape = (REACH * size_y + CORNERS, channels)
     out = jax.ShapeDtypeStruct(shape, BF16)
     strips = jax.ShapeDtypeStruct((2,) + got[0].shape, BF16)
     return pl.pallas_call(
@@ -320,7 +322,8 @@
                 here = slice(n * cut, (n + 1) * cut)
                 side_x[here, :] = beside_all[n, :, :channels]
                 side_d[here, :] = beside_all[n, :, channels : 2 * channels]
-                side_m[here, :] = beside_all[n, :, 3 * channels : 3 * channels + LANES]
+                live = beside_all[n, :, 3 * channels :].astype(F32)[:, 0:1]
+                side_m[here, :] = jnp.broadcast_to(live, (cut, LANES)).astype(BF16)
 
         beside = pl.ds(pl.multiple_of(step * each, each), each)
     x_here = pl.ds(first + step * xs, xs)
@@ -467,8 +470,8 @@
     natural[REACH : REACH + size_x, :] = _kappa_wide(kappa, aux_l, aux_r)
     up = above[:, :wide].astype(F32) + above[:, wide : 2 * wide].astype(F32)
     down = below[:, :wide].astype(F32) + below[:, wide : 2 * wide].astype(F32)
-    natural[0:REACH, :] = up[size_x - REACH :]
-    natural[REACH + size_x : 2 * REACH + size_x, :] = down[:REACH]
+    natural[0:REACH, :] = up[KAPPA_ROW : KAPPA_ROW + REACH]
+    natural[REACH + size_x : 2 * REACH + size_x, :] = down[KAPPA_ROW : KAPPA_ROW + REACH]
     own = natural[:, :LANES].T
     rest = natural[:, LANES:].T
     for r in range(size_x + 2 * REACH):
@@ -503,7 +506,7 @@
             border[0], border[1] = (got_1[...], got_2[...]) if odd else (got_2[...], got_1[...])
 
         _both_ways("elem", order)
-        k_rows = slice(body + CORNERS, body + CORNERS + size_x)
+        k_rows = slice(body, body + CORNERS)
         _kappa_frame(
             kappa, from_l[:, aux:], from_r[:, aux:], above[k_rows, :], below[k_rows, :], natural, kap
         )

time: 58.7 us -> 58.8 us (level)
  transfers between devices with their start and end apart: 6 -> 6, of which waited for: 3 -> 2; matrix products, arithmetic and copies ran while one was open for 0% -> 0% of each run, Pallas kernels for 47% -> 47%
where the time goes in v4:
time: 58.8 us; the launch traced here: 58.6 us
  Pallas kernels  38.4 us (65%)
  starting transfers between devices  16.4 us (28%)
  waiting for transfers between devices  2.32 us (4%)
  between operations  1.49 us (3%)
    pallas_call x1, Pallas kernels, adjoint_all(): pl.pallas_call(adjoint_kernel, grid=(groups + blocks,), in_specs=[_held()...  15.5 us
    ppermute x3, starting transfers between devices, _swap(): lax.ppermute(second, axis, others)  13.8 us
    pallas_call x2, Pallas kernels, forward(): pl.pallas_call(functools.partial(forward_kernel, first, bool(sides), rows...  12 us
    pallas_call x1, Pallas kernels, tangent_all(): pl.pallas_call(tangent_kernel, grid=(channels // LANES,), in_specs=[_held...  7.93 us
    ppermute x3, starting transfers between devices, _swap(): lax.ppermute(first, axis, pairs)  2.56 us
    pallas_call x1, Pallas kernels, make_edges(): pl.pallas_call(edge_kernel, in_specs=[pl.BlockSpec(memory_space=pltpu.SME...  2.37 us
    ppermute x3, waiting for transfers between devices, _swap(): lax.ppermute(second, axis, others)  2.32 us
  transfers between devices with their start and end apart: 6, of which 2 were waited for; matrix products, arithmetic and copies ran while one was open for 0% of the time, Pallas kernels for 47%

profile of v4, /device:TPU:7, one launch (start us, length us, event | category | flops | bytes accessed | tf_op | source)
XLA Modules:
  0.0 58.6 jit_solution(6385511046646868920)
XLA Ops:
  1.3 0.0 copy-start
  1.3 0.0 copy-start.2
  1.3 0.0 copy-start.3
  1.3 0.0 copy-start.4
  1.3 0.0 copy-start.5
  1.3 0.0 copy-start.8
  1.3 2.4 %edges.1 = (bf16[48,2432]{1,0:T(8,128)(2,1)S(1)}, bf16[48,2432]{1,0:T(8,128)(2,1)S(1)}, bf16[2048,128]{1,0:T(8,128)(2,1)S(1)}) custom-call(s32[1,1]{1,0:T(1,128)S(6)} %copy.14.counts, s32[1,1024]{1,0:T(1,128)} %listed_hbm.1, f32[16,128]{1,0:T(8,128)} %kappa.3, bf16[16,128,768]{2,1,0:T(8,128)(2,1)} %refs_0_.3, bf16[16,128,768]{2,1,0:T(8,128)(2,1)} %pert.3, ...), custom_call_target="tpu_custom_call" | custom-call | tf_op jit(solution)/shard_map/edges/pallas_call | solution.py:136
  3.7 0.8 %collective-permute-start = (bf16[48,2432]{1,0:T(8,128)(2,1)S(1)}, bf16[48,2432]{1,0:T(8,128)(2,1)S(1)}, u32[]{:S(2)}, u32[]{:S(2)}) collective-permute-start(bf16[48,2432]{1,0:T(8,128)(2,1)S(1)} %get-tuple-element.22), channel_id=1, source_target_pairs={{0,1},{1,0},{2,3},{3,2},{4,5},{5,4},{6,7},{7,6},{8,9},{9,8},{10,11... | collective-permute-start | bytes 700424 | tf_op jit(solution)/shard_map/ppermute | solution.py:680
  4.5 3.4 %collective-permute-start.1 = (bf16[48,2432]{1,0:T(8,128)(2,1)S(1)}, bf16[48,2432]{1,0:T(8,128)(2,1)S(1)}, u32[]{:S(2)}, u32[]{:S(2)}) collective-permute-start(bf16[48,2432]{1,0:T(8,128)(2,1)S(1)} %get-tuple-element.23), channel_id=1, source_target_pairs={{1,2},{2,1},{5,6},{6,5},{9,10},{10,9},{13,14},{14,13},{17,18},{18,... | collective-permute-start | bytes 700424 | tf_op jit(solution)/shard_map/ppermute | solution.py:680
  7.8 0.0 copy-done
  7.9 0.0 copy-done.2
  7.9 0.0 copy-done.3
  7.9 0.0 copy-done.4
  7.9 0.0 copy-done.5
  7.9 0.0 copy-done.8
  7.9 0.0 copy-start.1
  7.9 0.0 copy-start.7
  7.9 2.9 %forward_part.1 = (bf16[512,2048]{1,0:T(8,128)(2,1)S(1)}, bf16[512,128]{1,0:T(8,128)(2,1)S(1)}) custom-call(bf16[16,128,768]{2,1,0:T(8,128)(2,1)S(1)} %copy-done.2, bf16[16,128,768]{2,1,0:T(8,128)(2,1)S(1)} %copy-done, bf16[2048,128]{1,0:T(8,128)(2,1)S(1)} %get-tuple-element.20.refs_2_.mask, bf16[768,512]{1,0:T(8,128)(2,1)S(1)} %copy-done.4, ...), custom_call_target="tpu_custom_call" | custom-call | tf_op jit(solution)/shard_map/forward_part/pallas_call | solution.py:380
  10.8 0.0 collective-permute-done.got_1
  10.8 1.2 %collective-permute-done.1.got_2 = bf16[48,2432]{1,0:T(8,128)(2,1)S(1)} collective-permute-done((bf16[48,2432]{1,0:T(8,128)(2,1)S(1)}, bf16[48,2432]{1,0:T(8,128)(2,1)S(1)}, u32[]{:S(2)}, u32[]{:S(2)}) %collective-permute-start.1) | collective-permute-done | bytes 233504 | tf_op jit(solution)/shard_map/ppermute | solution.py:680
  12.0 0.0 copy-done.1
  12.0 0.0 copy-done.7
  12.0 0.3 first_border.1
  12.3 1.7 %collective-permute-start.4 = (bf16[400,768]{1,0:T(8,128)(2,1)S(1)}, bf16[400,768]{1,0:T(8,128)(2,1)S(1)}, u32[]{:S(2)}, u32[]{:S(2)}) collective-permute-start(bf16[400,768]{1,0:T(8,128)(2,1)S(1)} %get-tuple-element.32), channel_id=1, source_target_pairs={{0,4},{4,0},{8,12},{12,8},{16,20},{20,16},{24,28},{28,24},{32,36},... | collective-permute-start | bytes 1843208 | tf_op jit(solution)/shard_map/ppermute | solution.py:680
  14.0 7.0 %collective-permute-start.5 = (bf16[400,768]{1,0:T(8,128)(2,1)S(1)}, bf16[400,768]{1,0:T(8,128)(2,1)S(1)}, u32[]{:S(2)}, u32[]{:S(2)}) collective-permute-start(bf16[400,768]{1,0:T(8,128)(2,1)S(1)} %get-tuple-element.33), channel_id=1, source_target_pairs={{4,8},{8,4},{12,16},{16,12},{20,24},{24,20},{28,32},{32,28},{36,40... | collective-permute-start | bytes 1843208 | tf_op jit(solution)/shard_map/ppermute | solution.py:680
  21.1 9.1 %forward_rest.1 = (bf16[1536,2048]{1,0:T(8,128)(2,1)S(1)}, bf16[1536,128]{1,0:T(8,128)(2,1)S(1)}, bf16[96,128]{1,0:T(8,128)(2,1)S(1)}) custom-call(bf16[16,128,768]{2,1,0:T(8,128)(2,1)S(1)} %copy-done.2, bf16[16,128,768]{2,1,0:T(8,128)(2,1)S(1)} %copy-done, bf16[2048,128]{1,0:T(8,128)(2,1)S(1)} %get-tuple-element.20.refs_2_.mask, ...), custom_call_target="tpu_custom_call" | custom-call | tf_op jit(solution)/shard_map/forward_rest/pallas_call | solution.py:380
  30.2 0.0 copy-start.6
  30.2 0.3 late_border.1
  30.5 0.1 collective-permute-start.2
  30.6 3.4 %collective-permute-start.3 = (bf16[400,768]{1,0:T(8,128)(2,1)S(1)}, bf16[400,768]{1,0:T(8,128)(2,1)S(1)}, u32[]{:S(2)}, u32[]{:S(2)}) collective-permute-start(bf16[400,768]{1,0:T(8,128)(2,1)S(1)} %get-tuple-element.31), channel_id=1, source_target_pairs={{4,8},{8,4},{12,16},{16,12},{20,24},{24,20},{28,32},{32,28},{36,40... | collective-permute-start | bytes 1843208 | tf_op jit(solution)/shard_map/ppermute | solution.py:680
  34.0 0.0 collective-permute-done.4.got_1
  34.0 0.0 collective-permute-done.5.got_2
  34.1 0.0 copy-done.6
  34.1 15.5 %adjoint.1 = (f32[3168,128]{1,0:T(8,128)S(1)}, f32[2048,768]{1,0:T(8,128)}) custom-call(bf16[16,128,768]{2,1,0:T(8,128)(2,1)S(1)} %copy-done.1, bf16[400,768]{1,0:T(8,128)(2,1)S(1)} %collective-permute-done.4.got_1, bf16[400,768]{1,0:T(8,128)(2,1)S(1)} %collective-permute-done.5.got_2, bf16[2,48,2432]{2,1,0:T(8,128)(2,1)S(1)} %get-tuple-element.27.refs_3_.strips, ...), custom_call_target="tpu_custom_call" | custom-call | tf_op jit(solution)/shard_map/adjoint/pallas_call | solution.py:575
  49.6 0.0 collective-permute-done.2.late_1
  49.6 1.1 %collective-permute-done.3.late_2 = bf16[400,768]{1,0:T(8,128)(2,1)S(1)} collective-permute-done((bf16[400,768]{1,0:T(8,128)(2,1)S(1)}, bf16[400,768]{1,0:T(8,128)(2,1)S(1)}, u32[]{:S(2)}, u32[]{:S(2)}) %collective-permute-start.3) | collective-permute-done | bytes 614432 | tf_op jit(solution)/shard_map/ppermute | solution.py:680
  50.7 7.9 %tangent.1 = f32[16,128,768]{2,1,0:T(8,128)} custom-call(bf16[16,128,768]{2,1,0:T(8,128)(2,1)S(1)} %copy-done, bf16[512,128]{1,0:T(8,128)(2,1)S(1)} %get-tuple-element.21.moved_t.moved_a, bf16[1536,128]{1,0:T(8,128)(2,1)S(1)} %get-tuple-element.28.moved_b, bf16[400,768]{1,0:T(8,128)(2,1)S(1)} %collective-permute-done.2.late_1, ...), custom_call_target="tpu_custom_call" | custom-call | tf_op jit(solution)/shard_map/tangent/pallas_call | solution.py:659
Async XLA Ops:
  1.3 6.6 %copy-start = (bf16[16,128,768]{2,1,0:T(8,128)(2,1)S(1)}, bf16[16,128,768]{2,1,0:T(8,128)(2,1)}, u32[]{:S(2)}) copy-start(bf16[16,128,768]{2,1,0:T(8,128)(2,1)} %pert.3) | copy-start | bytes 9437188
  1.3 6.6 %copy-start.2 = (bf16[16,128,768]{2,1,0:T(8,128)(2,1)S(1)}, bf16[16,128,768]{2,1,0:T(8,128)(2,1)}, u32[]{:S(2)}) copy-start(bf16[16,128,768]{2,1,0:T(8,128)(2,1)} %refs_0_.3) | copy-start | bytes 9437188
  1.3 6.6 %copy-start.3 = (bf16[3,512,512]{2,1,0:T(8,128)(2,1)S(1)}, bf16[3,512,512]{2,1,0:T(8,128)(2,1)}, u32[]{:S(2)}) copy-start(bf16[3,512,512]{2,1,0:T(8,128)(2,1)} %w_mid.1) | copy-start | bytes 4718596
  1.3 6.6 %copy-start.4 = (bf16[768,512]{1,0:T(8,128)(2,1)S(1)}, bf16[768,512]{1,0:T(8,128)(2,1)}, u32[]{:S(2)}) copy-start(bf16[768,512]{1,0:T(8,128)(2,1)} %w_in.1) | copy-start | bytes 2359300
  1.3 6.6 %copy-start.5 = (bf16[512,128]{1,0:T(8,128)(2,1)S(1)}, bf16[512,128]{1,0:T(8,128)(2,1)}, u32[]{:S(2)}) copy-start(bf16[512,128]{1,0:T(8,128)(2,1)} %w_out.1) | copy-start | bytes 393220
  1.3 6.6 %copy-start.8 = (f32[4,512]{1,0:T(4,128)S(1)}, f32[4,512]{1,0:T(4,128)}, u32[]{:S(2)}) copy-start(f32[4,512]{1,0:T(4,128)} %refs_7_.1) | copy-start | bytes 24580
  3.7 7.1 %collective-permute-start = (bf16[48,2432]{1,0:T(8,128)(2,1)S(1)}, bf16[48,2432]{1,0:T(8,128)(2,1)S(1)}, u32[]{:S(2)}, u32[]{:S(2)}) collective-permute-start(bf16[48,2432]{1,0:T(8,128)(2,1)S(1)} %get-tuple-element.22), channel_id=1, source_target_pairs={{0,1},{1,0},{2,3},{3,2},{4,5},{5,4},{6,7},{7,6},{8,9},{9,8},{10,11... | collective-permute-start | bytes 700424 | tf_op jit(solution)/shard_map/ppermute | solution.py:680
  4.5 7.5 %collective-permute-start.1 = (bf16[48,2432]{1,0:T(8,128)(2,1)S(1)}, bf16[48,2432]{1,0:T(8,128)(2,1)S(1)}, u32[]{:S(2)}, u32[]{:S(2)}) collective-permute-start(bf16[48,2432]{1,0:T(8,128)(2,1)S(1)} %get-tuple-element.23), channel_id=1, source_target_pairs={{1,2},{2,1},{5,6},{6,5},{9,10},{10,9},{13,14},{14,13},{17,18},{18,... | collective-permute-start | bytes 700424 | tf_op jit(solution)/shard_map/ppermute | solution.py:680
  7.9 4.1 %copy-start.1 = (bf16[16,128,768]{2,1,0:T(8,128)(2,1)S(1)}, bf16[16,128,768]{2,1,0:T(8,128)(2,1)}, u32[]{:S(2)}) copy-start(bf16[16,128,768]{2,1,0:T(8,128)(2,1)} %adj.3) | copy-start | bytes 9437188
  7.9 4.1 %copy-start.7 = (f32[16,128]{1,0:T(8,128)S(1)}, f32[16,128]{1,0:T(8,128)}, u32[]{:S(2)}) copy-start(f32[16,128]{1,0:T(8,128)} %kappa.3) | copy-start | bytes 24580
  12.3 21.7 %collective-permute-start.4 = (bf16[400,768]{1,0:T(8,128)(2,1)S(1)}, bf16[400,768]{1,0:T(8,128)(2,1)S(1)}, u32[]{:S(2)}, u32[]{:S(2)}) collective-permute-start(bf16[400,768]{1,0:T(8,128)(2,1)S(1)} %get-tuple-element.32), channel_id=1, source_target_pairs={{0,4},{4,0},{8,12},{12,8},{16,20},{20,16},{24,28},{28,24},{32,36},... | collective-permute-start | bytes 1843208 | tf_op jit(solution)/shard_map/ppermute | solution.py:680
  14.0 20.0 %collective-permute-start.5 = (bf16[400,768]{1,0:T(8,128)(2,1)S(1)}, bf16[400,768]{1,0:T(8,128)(2,1)S(1)}, u32[]{:S(2)}, u32[]{:S(2)}) collective-permute-start(bf16[400,768]{1,0:T(8,128)(2,1)S(1)} %get-tuple-element.33), channel_id=1, source_target_pairs={{4,8},{8,4},{12,16},{16,12},{20,24},{24,20},{28,32},{32,28},{36,40... | collective-permute-start | bytes 1843208 | tf_op jit(solution)/shard_map/ppermute | solution.py:680
  30.2 3.8 %copy-start.6 = (bf16[352,128]{1,0:T(8,128)(2,1)S(1)}, bf16[352,128]{1,0:T(8,128)(2,1)}, u32[]{:S(2)}) copy-start(bf16[352,128]{1,0:T(8,128)(2,1)} %constant.2.clone.picks) | copy-start | bytes 270340
  30.5 19.1 %collective-permute-start.2 = (bf16[400,768]{1,0:T(8,128)(2,1)S(1)}, bf16[400,768]{1,0:T(8,128)(2,1)S(1)}, u32[]{:S(2)}, u32[]{:S(2)}) collective-permute-start(bf16[400,768]{1,0:T(8,128)(2,1)S(1)} %get-tuple-element.30), channel_id=1, source_target_pairs={{0,4},{4,0},{8,12},{12,8},{16,20},{20,16},{24,28},{28,24},{32,36},... | collective-permute-start | bytes 1843208 | tf_op jit(solution)/shard_map/ppermute | solution.py:680
  30.6 20.1 %collective-permute-start.3 = (bf16[400,768]{1,0:T(8,128)(2,1)S(1)}, bf16[400,768]{1,0:T(8,128)(2,1)S(1)}, u32[]{:S(2)}, u32[]{:S(2)}) collective-permute-start(bf16[400,768]{1,0:T(8,128)(2,1)S(1)} %get-tuple-element.31), channel_id=1, source_target_pairs={{4,8},{8,4},{12,16},{16,12},{20,24},{24,20},{28,32},{32,28},{36,40... | collective-permute-start | bytes 1843208 | tf_op jit(solution)/shard_map/ppermute | solution.py:680

commit v5 on v4

--- a/solution.py
+++ b/solution.py
@@ -228,7 +228,7 @@
 
 def late_border_kernel(strips, moved_s, pert_t, pert_b, moved_t, moved_b, msg_1, msg_2):
     def write(odd):
-        top, bot = (msg_1, msg_2) if odd else (msg_2, msg_1)
+        top, bot = (msg_2, msg_1) if odd else (msg_1, msg_2)
         _write_late(
             strips.at[0], strips.at[1], moved_s, pert_t, pert_b, moved_t, moved_b, top, bot
         )
@@ -611,7 +611,7 @@
     @pl.when(step == 0)
     def _():
         def order(odd):
-            border[0], border[1] = (late_1[...], late_2[...]) if odd else (late_2[...], late_1[...])
+            border[0], border[1] = (late_2[...], late_1[...]) if odd else (late_1[...], late_2[...])
 
         _both_ways("elem", order)
         ends = [border[n, body : body + CORNERS, :] for n in range(2)]
@@ -673,10 +673,12 @@
     )(*args)
 
 
-def _swap(first, second, axis):
+def _swap(first, second, axis, flip=False):
     count = lax.axis_size(axis)
     pairs = [(i, i ^ 1) for i in range(count)]
     others = [(i, ((i + 1) ^ 1) - 1) for i in range(1, count - 1)]
+    if flip:
+        pairs, others = others, pairs
     return lax.ppermute(first, axis, pairs), lax.ppermute(second, axis, others)
 
 
@@ -696,7 +698,7 @@
     slopes_b, moved_b, moved_s = forward(
         part, size_x - part, state, perturbation, mask, (strips,), nets
     )
-    late = _swap(*late_border(strips, moved_s, perturbation, moved_a, moved_b), "elem")
+    late = _swap(*late_border(strips, moved_s, perturbation, moved_a, moved_b), "elem", True)
     kap, ad_out = adjoint_all(
         adjoint_end, first, strips, kappa, mask, slopes_a, slopes_b, weights
     )

time: 58.8 us -> 58.7 us (level)
    ppermute x3, starting transfers between devices: 13.8 us -> 10.7 us  [_swap(): lax.ppermute(second, axis, others)]
    ppermute x3, starting transfers between devices: 2.56 us -> 5.25 us  [_swap(): lax.ppermute(first, axis, pairs)]
    ppermute x3, waiting for transfers between devices: 0.01 us -> 1.36 us  [_swap(): lax.ppermute(first, axis, pairs)]
    ppermute x3, waiting for transfers between devices: 2.32 us -> 1.45 us  [_swap(): lax.ppermute(second, axis, others)]
  transfers between devices with their start and end apart: 6 -> 6, of which waited for: 2 -> 3; matrix products, arithmetic and copies ran while one was open for 0% -> 0% of each run, Pallas kernels for 47% -> 47%
where the time goes in v5:
time: 58.7 us; the launch traced here: 58.5 us
  Pallas kernels  38.3 us (65%)
  starting transfers between devices  15.9 us (27%)
  waiting for transfers between devices  2.8 us (5%)
  between operations  1.48 us (3%)
    pallas_call x1, Pallas kernels, adjoint_all(): pl.pallas_call(adjoint_kernel, grid=(groups + blocks,), in_specs=[_held()...  15.4 us
    pallas_call x2, Pallas kernels, forward(): pl.pallas_call(functools.partial(forward_kernel, first, bool(sides), rows...  12 us
    ppermute x3, starting transfers between devices, _swap(): lax.ppermute(second, axis, others)  10.7 us
    pallas_call x1, Pallas kernels, tangent_all(): pl.pallas_call(tangent_kernel, grid=(channels // LANES,), in_specs=[_held...  7.92 us
    ppermute x3, starting transfers between devices, _swap(): lax.ppermute(first, axis, pairs)  5.25 us
    pallas_call x1, Pallas kernels, make_edges(): pl.pallas_call(edge_kernel, in_specs=[pl.BlockSpec(memory_space=pltpu.SME...  2.37 us
    ppermute x3, waiting for transfers between devices, _swap(): lax.ppermute(second, axis, others)  1.45 us
    ppermute x3, waiting for transfers between devices, _swap(): lax.ppermute(first, axis, pairs)  1.36 us
  transfers between devices with their start and end apart: 6, of which 3 were waited for; matrix products, arithmetic and copies ran while one was open for 0% of the time, Pallas kernels for 47%

profile of v5, /device:TPU:7, one launch (start us, length us, event | category | flops | bytes accessed | tf_op | source)
XLA Modules:
  0.0 58.5 jit_solution(2054775324510777317)
XLA Ops:
  1.3 0.0 copy-start
  1.3 0.0 copy-start.2
  1.3 0.0 copy-start.3
  1.3 0.0 copy-start.4
  1.3 0.0 copy-start.5
  1.3 0.0 copy-start.8
  1.3 2.4 %edges.1 = (bf16[48,2432]{1,0:T(8,128)(2,1)S(1)}, bf16[48,2432]{1,0:T(8,128)(2,1)S(1)}, bf16[2048,128]{1,0:T(8,128)(2,1)S(1)}) custom-call(s32[1,1]{1,0:T(1,128)S(6)} %copy.14.counts, s32[1,1024]{1,0:T(1,128)} %listed_hbm.1, f32[16,128]{1,0:T(8,128)} %kappa.3, bf16[16,128,768]{2,1,0:T(8,128)(2,1)} %refs_0_.3, bf16[16,128,768]{2,1,0:T(8,128)(2,1)} %pert.3, ...), custom_call_target="tpu_custom_call" | custom-call | tf_op jit(solution)/shard_map/edges/pallas_call | solution.py:136
  3.7 0.8 %collective-permute-start = (bf16[48,2432]{1,0:T(8,128)(2,1)S(1)}, bf16[48,2432]{1,0:T(8,128)(2,1)S(1)}, u32[]{:S(2)}, u32[]{:S(2)}) collective-permute-start(bf16[48,2432]{1,0:T(8,128)(2,1)S(1)} %get-tuple-element.22), channel_id=1, source_target_pairs={{0,1},{1,0},{2,3},{3,2},{4,5},{5,4},{6,7},{7,6},{8,9},{9,8},{10,11... | collective-permute-start | bytes 700424 | tf_op jit(solution)/shard_map/ppermute | solution.py:682
  4.5 3.4 %collective-permute-start.1 = (bf16[48,2432]{1,0:T(8,128)(2,1)S(1)}, bf16[48,2432]{1,0:T(8,128)(2,1)S(1)}, u32[]{:S(2)}, u32[]{:S(2)}) collective-permute-start(bf16[48,2432]{1,0:T(8,128)(2,1)S(1)} %get-tuple-element.23), channel_id=1, source_target_pairs={{1,2},{2,1},{5,6},{6,5},{9,10},{10,9},{13,14},{14,13},{17,18},{18,... | collective-permute-start | bytes 700424 | tf_op jit(solution)/shard_map/ppermute | solution.py:682
  7.8 0.0 copy-done
  7.9 0.0 copy-done.2
  7.9 0.0 copy-done.3
  7.9 0.0 copy-done.4
  7.9 0.0 copy-done.5
  7.9 0.0 copy-done.8
  7.9 0.0 copy-start.1
  7.9 0.0 copy-start.7
  7.9 2.9 %forward_part.1 = (bf16[512,2048]{1,0:T(8,128)(2,1)S(1)}, bf16[512,128]{1,0:T(8,128)(2,1)S(1)}) custom-call(bf16[16,128,768]{2,1,0:T(8,128)(2,1)S(1)} %copy-done.2, bf16[16,128,768]{2,1,0:T(8,128)(2,1)S(1)} %copy-done, bf16[2048,128]{1,0:T(8,128)(2,1)S(1)} %get-tuple-element.20.refs_2_.mask, bf16[768,512]{1,0:T(8,128)(2,1)S(1)} %copy-done.4, ...), custom_call_target="tpu_custom_call" | custom-call | tf_op jit(solution)/shard_map/forward_part/pallas_call | solution.py:380
  10.8 0.0 collective-permute-done.got_1
  10.8 1.2 %collective-permute-done.1.got_2 = bf16[48,2432]{1,0:T(8,128)(2,1)S(1)} collective-permute-done((bf16[48,2432]{1,0:T(8,128)(2,1)S(1)}, bf16[48,2432]{1,0:T(8,128)(2,1)S(1)}, u32[]{:S(2)}, u32[]{:S(2)}) %collective-permute-start.1) | collective-permute-done | bytes 233504 | tf_op jit(solution)/shard_map/ppermute | solution.py:682
  12.0 0.0 copy-done.1
  12.0 0.0 copy-done.7
  12.0 0.3 first_border.1
  12.3 1.7 %collective-permute-start.4 = (bf16[400,768]{1,0:T(8,128)(2,1)S(1)}, bf16[400,768]{1,0:T(8,128)(2,1)S(1)}, u32[]{:S(2)}, u32[]{:S(2)}) collective-permute-start(bf16[400,768]{1,0:T(8,128)(2,1)S(1)} %get-tuple-element.32), channel_id=1, source_target_pairs={{0,4},{4,0},{8,12},{12,8},{16,20},{20,16},{24,28},{28,24},{32,36},... | collective-permute-start | bytes 1843208 | tf_op jit(solution)/shard_map/ppermute | solution.py:682
  14.0 7.0 %collective-permute-start.5 = (bf16[400,768]{1,0:T(8,128)(2,1)S(1)}, bf16[400,768]{1,0:T(8,128)(2,1)S(1)}, u32[]{:S(2)}, u32[]{:S(2)}) collective-permute-start(bf16[400,768]{1,0:T(8,128)(2,1)S(1)} %get-tuple-element.33), channel_id=1, source_target_pairs={{4,8},{8,4},{12,16},{16,12},{20,24},{24,20},{28,32},{32,28},{36,40... | collective-permute-start | bytes 1843208 | tf_op jit(solution)/shard_map/ppermute | solution.py:682
  21.1 9.1 %forward_rest.1 = (bf16[1536,2048]{1,0:T(8,128)(2,1)S(1)}, bf16[1536,128]{1,0:T(8,128)(2,1)S(1)}, bf16[96,128]{1,0:T(8,128)(2,1)S(1)}) custom-call(bf16[16,128,768]{2,1,0:T(8,128)(2,1)S(1)} %copy-done.2, bf16[16,128,768]{2,1,0:T(8,128)(2,1)S(1)} %copy-done, bf16[2048,128]{1,0:T(8,128)(2,1)S(1)} %get-tuple-element.20.refs_2_.mask, ...), custom_call_target="tpu_custom_call" | custom-call | tf_op jit(solution)/shard_map/forward_rest/pallas_call | solution.py:380
  30.2 0.0 copy-start.6
  30.2 0.3 late_border.1
  30.5 2.8 %collective-permute-start.2 = (bf16[400,768]{1,0:T(8,128)(2,1)S(1)}, bf16[400,768]{1,0:T(8,128)(2,1)S(1)}, u32[]{:S(2)}, u32[]{:S(2)}) collective-permute-start(bf16[400,768]{1,0:T(8,128)(2,1)S(1)} %get-tuple-element.30), channel_id=1, source_target_pairs={{4,8},{8,4},{12,16},{16,12},{20,24},{24,20},{28,32},{32,28},{36,40... | collective-permute-start | bytes 1843208 | tf_op jit(solution)/shard_map/ppermute | solution.py:682
  33.3 0.3 collective-permute-start.3
  33.6 0.0 collective-permute-done.4.got_1
  33.6 0.3 collective-permute-done.5.got_2
  33.8 0.0 copy-done.6
  33.8 15.4 %adjoint.1 = (f32[3168,128]{1,0:T(8,128)S(1)}, f32[2048,768]{1,0:T(8,128)}) custom-call(bf16[16,128,768]{2,1,0:T(8,128)(2,1)S(1)} %copy-done.1, bf16[400,768]{1,0:T(8,128)(2,1)S(1)} %collective-permute-done.4.got_1, bf16[400,768]{1,0:T(8,128)(2,1)S(1)} %collective-permute-done.5.got_2, bf16[2,48,2432]{2,1,0:T(8,128)(2,1)S(1)} %get-tuple-element.27.refs_3_.strips, ...), custom_call_target="tpu_custom_call" | custom-call | tf_op jit(solution)/shard_map/adjoint/pallas_call | solution.py:575
  49.3 1.4 %collective-permute-done.2.late_1 = bf16[400,768]{1,0:T(8,128)(2,1)S(1)} collective-permute-done((bf16[400,768]{1,0:T(8,128)(2,1)S(1)}, bf16[400,768]{1,0:T(8,128)(2,1)S(1)}, u32[]{:S(2)}, u32[]{:S(2)}) %collective-permute-start.2) | collective-permute-done | bytes 614432 | tf_op jit(solution)/shard_map/ppermute | solution.py:682
  50.6 0.0 collective-permute-done.3.late_2
  50.6 7.9 %tangent.1 = f32[16,128,768]{2,1,0:T(8,128)} custom-call(bf16[16,128,768]{2,1,0:T(8,128)(2,1)S(1)} %copy-done, bf16[512,128]{1,0:T(8,128)(2,1)S(1)} %get-tuple-element.21.moved_t.moved_a, bf16[1536,128]{1,0:T(8,128)(2,1)S(1)} %get-tuple-element.28.moved_b, bf16[400,768]{1,0:T(8,128)(2,1)S(1)} %collective-permute-done.2.late_1, ...), custom_call_target="tpu_custom_call" | custom-call | tf_op jit(solution)/shard_map/tangent/pallas_call | solution.py:659
Async XLA Ops:
  1.3 6.6 %copy-start = (bf16[16,128,768]{2,1,0:T(8,128)(2,1)S(1)}, bf16[16,128,768]{2,1,0:T(8,128)(2,1)}, u32[]{:S(2)}) copy-start(bf16[16,128,768]{2,1,0:T(8,128)(2,1)} %pert.3) | copy-start | bytes 9437188
  1.3 6.6 %copy-start.2 = (bf16[16,128,768]{2,1,0:T(8,128)(2,1)S(1)}, bf16[16,128,768]{2,1,0:T(8,128)(2,1)}, u32[]{:S(2)}) copy-start(bf16[16,128,768]{2,1,0:T(8,128)(2,1)} %refs_0_.3) | copy-start | bytes 9437188
  1.3 6.6 %copy-start.3 = (bf16[3,512,512]{2,1,0:T(8,128)(2,1)S(1)}, bf16[3,512,512]{2,1,0:T(8,128)(2,1)}, u32[]{:S(2)}) copy-start(bf16[3,512,512]{2,1,0:T(8,128)(2,1)} %w_mid.1) | copy-start | bytes 4718596
  1.3 6.6 %copy-start.4 = (bf16[768,512]{1,0:T(8,128)(2,1)S(1)}, bf16[768,512]{1,0:T(8,128)(2,1)}, u32[]{:S(2)}) copy-start(bf16[768,512]{1,0:T(8,128)(2,1)} %w_in.1) | copy-start | bytes 2359300
  1.3 6.6 %copy-start.5 = (bf16[512,128]{1,0:T(8,128)(2,1)S(1)}, bf16[512,128]{1,0:T(8,128)(2,1)}, u32[]{:S(2)}) copy-start(bf16[512,128]{1,0:T(8,128)(2,1)} %w_out.1) | copy-start | bytes 393220
  1.3 6.6 %copy-start.8 = (f32[4,512]{1,0:T(4,128)S(1)}, f32[4,512]{1,0:T(4,128)}, u32[]{:S(2)}) copy-start(f32[4,512]{1,0:T(4,128)} %refs_7_.1) | copy-start | bytes 24580
  3.7 7.1 %collective-permute-start = (bf16[48,2432]{1,0:T(8,128)(2,1)S(1)}, bf16[48,2432]{1,0:T(8,128)(2,1)S(1)}, u32[]{:S(2)}, u32[]{:S(2)}) collective-permute-start(bf16[48,2432]{1,0:T(8,128)(2,1)S(1)} %get-tuple-element.22), channel_id=1, source_target_pairs={{0,1},{1,0},{2,3},{3,2},{4,5},{5,4},{6,7},{7,6},{8,9},{9,8},{10,11... | collective-permute-start | bytes 700424 | tf_op jit(solution)/shard_map/ppermute | solution.py:682
  4.5 7.5 %collective-permute-start.1 = (bf16[48,2432]{1,0:T(8,128)(2,1)S(1)}, bf16[48,2432]{1,0:T(8,128)(2,1)S(1)}, u32[]{:S(2)}, u32[]{:S(2)}) collective-permute-start(bf16[48,2432]{1,0:T(8,128)(2,1)S(1)} %get-tuple-element.23), channel_id=1, source_target_pairs={{1,2},{2,1},{5,6},{6,5},{9,10},{10,9},{13,14},{14,13},{17,18},{18,... | collective-permute-start | bytes 700424 | tf_op jit(solution)/shard_map/ppermute | solution.py:682
  7.9 4.1 %copy-start.1 = (bf16[16,128,768]{2,1,0:T(8,128)(2,1)S(1)}, bf16[16,128,768]{2,1,0:T(8,128)(2,1)}, u32[]{:S(2)}) copy-start(bf16[16,128,768]{2,1,0:T(8,128)(2,1)} %adj.3) | copy-start | bytes 9437188
  7.9 4.1 %copy-start.7 = (f32[16,128]{1,0:T(8,128)S(1)}, f32[16,128]{1,0:T(8,128)}, u32[]{:S(2)}) copy-start(f32[16,128]{1,0:T(8,128)} %kappa.3) | copy-start | bytes 24580
  12.3 21.3 %collective-permute-start.4 = (bf16[400,768]{1,0:T(8,128)(2,1)S(1)}, bf16[400,768]{1,0:T(8,128)(2,1)S(1)}, u32[]{:S(2)}, u32[]{:S(2)}) collective-permute-start(bf16[400,768]{1,0:T(8,128)(2,1)S(1)} %get-tuple-element.32), channel_id=1, source_target_pairs={{0,4},{4,0},{8,12},{12,8},{16,20},{20,16},{24,28},{28,24},{32,36},... | collective-permute-start | bytes 1843208 | tf_op jit(solution)/shard_map/ppermute | solution.py:682
  14.0 19.8 %collective-permute-start.5 = (bf16[400,768]{1,0:T(8,128)(2,1)S(1)}, bf16[400,768]{1,0:T(8,128)(2,1)S(1)}, u32[]{:S(2)}, u32[]{:S(2)}) collective-permute-start(bf16[400,768]{1,0:T(8,128)(2,1)S(1)} %get-tuple-element.33), channel_id=1, source_target_pairs={{4,8},{8,4},{12,16},{16,12},{20,24},{24,20},{28,32},{32,28},{36,40... | collective-permute-start | bytes 1843208 | tf_op jit(solution)/shard_map/ppermute | solution.py:682
  30.2 3.6 %copy-start.6 = (bf16[352,128]{1,0:T(8,128)(2,1)S(1)}, bf16[352,128]{1,0:T(8,128)(2,1)}, u32[]{:S(2)}) copy-start(bf16[352,128]{1,0:T(8,128)(2,1)} %constant.2.clone.picks) | copy-start | bytes 270340
  30.5 20.1 %collective-permute-start.2 = (bf16[400,768]{1,0:T(8,128)(2,1)S(1)}, bf16[400,768]{1,0:T(8,128)(2,1)S(1)}, u32[]{:S(2)}, u32[]{:S(2)}) collective-permute-start(bf16[400,768]{1,0:T(8,128)(2,1)S(1)} %get-tuple-element.30), channel_id=1, source_target_pairs={{4,8},{8,4},{12,16},{16,12},{20,24},{24,20},{28,32},{32,28},{36,40... | collective-permute-start | bytes 1843208 | tf_op jit(solution)/shard_map/ppermute | solution.py:682
  33.3 17.3 %collective-permute-start.3 = (bf16[400,768]{1,0:T(8,128)(2,1)S(1)}, bf16[400,768]{1,0:T(8,128)(2,1)S(1)}, u32[]{:S(2)}, u32[]{:S(2)}) collective-permute-start(bf16[400,768]{1,0:T(8,128)(2,1)S(1)} %get-tuple-element.31), channel_id=1, source_target_pairs={{0,4},{4,0},{8,12},{12,8},{16,20},{20,16},{24,28},{28,24},{32,36},... | collective-permute-start | bytes 1843208 | tf_op jit(solution)/shard_map/ppermute | solution.py:682
